TPU v7x, 128 devices: a whole 4x4x4 slice. The times are simulated.
128 devices in a mesh: section: 2 (over core), peer: 64 (over z, y, x).
Axes of the slice: x: 4, y: 4, z: 4, core: 2. Of those that a mesh axis runs over, the one named last changes fastest.
Arguments:
- inputs: bfloat16 [64, 3, 128, 5120], P('peer'), may hold values from -6 to 6
- cotangent: bfloat16 [64, 3, 128, 5120], P('peer'), may hold values from -6 to 6
- down_proj: bfloat16 [2, 2, 5120, 128], P('section'), may hold values from -0.078125 to 0.078125
- up_proj: bfloat16 [2, 2, 5120, 128], P('section'), may hold values from -0.5 to 0.5
- norm_gain: float32 [2, 2, 5120], P('section'), may hold values from 0.5 to 1.5
- wiring: int32 [2, 144], replicated, may hold values from 0 to 63, as said below
- live_mask: int32 [2, 64], replicated, may hold values from 0 to 1, as said below
Outputs:
- down_step: bfloat16 [2, 2, 5120, 128], P('section')
- up_step: bfloat16 [2, 2, 5120, 128], P('section')
Inputs may be any that keep to these rules, and one draw needn't show every extreme that they name: `live_mask`: every segment has at least 48 live peers; exactly one segment has all 64 peers live, every other segment has at least one dead peer. wiring[s, m] is smaller than the number of live peers of segment s. No two micro-batches of one lane share a peer at one segment, and in every segment the live peer of highest index receives a micro-batch of every lane. Entries of inputs and cotangent that no micro-batch names are unused.
All inputs are finite; a program needn't handle non-finite values.
Results may differ from a plain program's by a relative error of at most 0.015.
Values may be sent and summed in bfloat16 or wider, within the bound.
No kernel may reach another device: no remote copies, remote signals or barrier semaphores. Data moves between devices by JAX's collectives and lax.ppermute only.
A program may use at most 192 MiB of HBM per device.

v0:
```python
import jax
import jax.numpy as jnp
from jax import lax
from jax.experimental import pallas as pl
from jax.experimental.pallas import tpu as pltpu
from jax.sharding import PartitionSpec as P

norm_eps = 1e-05
step_eps = 1e-06
bf16 = jnp.bfloat16
f32 = jnp.float32


def dot(a, b):
    return jnp.dot(a.astype(bf16), b.astype(bf16), preferred_element_type=f32)


def dot_nt(a, b):
    return lax.dot_general(
        a.astype(bf16), b.astype(bf16), (((1,), (1,)), ((), ())), preferred_element_type=f32
    )


def dot_tn(a, b):
    return lax.dot_general(
        a.astype(bf16), b.astype(bf16), (((0,), (0,)), ((), ())), preferred_element_type=f32
    )


def peer_table(wiring, live_mask):
    live_rank = jnp.cumsum(live_mask, axis=1) - 1
    matches = (live_mask[:, None, :] == 1) & (live_rank[:, None, :] == wiring[:, :, None])
    peer_ids = jnp.arange(live_mask.shape[1], dtype=jnp.int32)
    return jnp.sum(jnp.where(matches, peer_ids, 0), axis=2)


def row_sum(values):
    return jnp.sum(values, axis=1, keepdims=True)


def row_stage(proj, cot, square_sum, gram_low, gram_high, feature_count):
    k = cot[0].shape[1]

    def cut(g, i, j):
        return g[i * k : (i + 1) * k, j * k : (j + 1) * k].astype(bf16)

    ugd = {(0, 1): cut(gram_low, 0, 0), (2, 3): cut(gram_high, 0, 0)}
    uu = {
        (0, 0): cut(gram_low, 0, 1),
        (0, 1): cut(gram_low, 0, 2),
        (1, 1): cut(gram_low, 1, 2),
        (2, 2): cut(gram_high, 0, 1),
    }
    for i in (0, 1):
        ugd[(i, 2)] = cut(gram_low, i, 3)
        ugd[(i, 3)] = cut(gram_low, i, 4)
        uu[(i, 2)] = cut(gram_low, i, 5)

    hidden, active, inverse, full = [], [], [], []
    for l in range(4):
        r = lax.rsqrt(square_sum * (1.0 / feature_count) + norm_eps)
        pre = proj[l][0]
        for i in range(l):
            pre = pre + dot(active[i], ugd[(i, l)])
        h = r * pre
        a = (h * jax.nn.sigmoid(h)).astype(bf16)
        hidden.append(h)
        active.append(a)
        inverse.append(r)
        if l < 3:
            along = proj[l][1]
            for i in range(l):
                along = along + dot(active[i], uu[(i, l)])
            own = dot(a, uu[(l, l)])
            square_sum = square_sum + row_sum((2.0 * along + own) * a.astype(f32))
            full.append(along + own)

    back = [None] * 4
    weight = [None] * 4
    weight[3] = jnp.zeros_like(square_sum)
    for l in (3, 2, 1, 0):
        grad = cot[l]
        for j in range(l + 1, 4):
            grad = grad + dot_nt(back[j], ugd[(l, j)])
        if l < 3:
            grad = grad - weight[l] * full[l]
        for i in range(l + 1, 3):
            grad = grad - weight[i] * dot_nt(active[i], uu[(l, i)])
        sig = jax.nn.sigmoid(hidden[l])
        hid_grad = (grad * sig * (1.0 + hidden[l] * (1.0 - sig))).astype(bf16).astype(f32)
        back[l] = (inverse[l] * hid_grad).astype(bf16)
        if l > 0:
            centred = row_sum(hidden[l] * hid_grad) * (1.0 / feature_count)
            weight[l - 1] = weight[l] + inverse[l] * inverse[l] * centred
    less = [(-weight[l] * active[l].astype(f32)).astype(bf16) for l in range(4)]

    def scaled(w, l):
        return (-w * active[l].astype(f32)).astype(bf16)

    def against(left, parts):
        turned = left.astype(f32).T.astype(bf16)
        product = dot(turned, jnp.concatenate(parts, axis=1))
        return [product[:, i * k : (i + 1) * k] for i in range(len(parts))]

    a, b, w = active, back, weight
    a0 = against(a[0], [b[1], less[0], less[1], b[2], b[3], less[2]])
    a1 = against(a[1], [scaled(w[1], 0), less[1], b[2], b[3], less[2]])
    a2 = against(a[2], [scaled(w[2], 0), scaled(w[2], 1), b[3], less[2]])
    b1 = against(b[1], [a[0]])
    b2 = against(b[2], [a[0], a[1]])
    b3 = against(b[3], [a[0], a[1], a[2]])
    none = jnp.zeros((k, k), f32)
    mix_first = [
        [none, none, b1[0], none],
        [none, a0[0], a0[1], a0[2]],
        [none, none, a1[0], a1[1]],
        [none, none, b2[0], b2[1]],
        [none, none, b3[0], b3[1]],
        [none, none, a2[0], a2[1]],
    ]
    mix_second = [
        [none, none, none, none],
        [a0[3], a0[4], a0[5], none],
        [a1[2], a1[3], a1[4], none],
        [none, none, none, none],
        [none, none, b3[2], none],
        [none, a2[2], a2[3], none],
    ]
    return active, back, less, mix_first, mix_second


def joined(parts):
    return jnp.concatenate(list(parts), axis=1)


def front(x, c, down, up, gain):
    lanes, rows, features = x.shape
    k = down.shape[2]
    block = 1024
    steps = features // block
    total = lanes * rows

    def kernel(x_ref, c_ref, d_ref, u_ref, g_ref, sent_ref, acc, squares, packed):
        step = pl.program_id(0)
        columns = jnp.concatenate([g_ref[...]] * 4, axis=0).T
        gained = [
            (d_ref[l].astype(f32) * columns[:, l : l + 1]).astype(bf16) for l in range(2)
        ]
        ups = [u_ref[0], u_ref[1]]
        flat = x_ref[...].reshape(total, block)
        of_x = dot(flat, joined(gained + ups))
        of_c = dot(c_ref[...].reshape(total, block), joined(ups))
        part = jnp.zeros((total, k), f32)
        for j in range(block // k):
            wide = flat[:, j * k : (j + 1) * k].astype(f32)
            part = part + wide * wide

        @pl.when(step == 0)
        def _():
            acc[:, : 4 * k] = of_x
            acc[:, 4 * k :] = of_c
            squares[...] = part

        @pl.when(step > 0)
        def _():
            acc[:, : 4 * k] += of_x
            acc[:, 4 * k :] += of_c
            squares[...] += part

        @pl.when(step == steps - 1)
        def _():
            for j in range(lanes):
                at = slice(j * rows, (j + 1) * rows)
                for half in range(2):
                    for t in range(3):
                        packed[t, pl.ds(2 * j + half, rows, stride=8), :] = acc[
                            at, (half * 3 + t) * k : (half * 3 + t + 1) * k
                        ]
                square = jnp.broadcast_to(row_sum(squares[at, :]), (rows, k))
                coarse = square.astype(bf16).astype(f32)
                packed[j, pl.ds(6, rows, stride=8), :] = coarse
                packed[j, pl.ds(7, rows, stride=8), :] = square - coarse
            for t in range(3):
                sent_ref[:, t * k : (t + 1) * k] = packed[t].astype(bf16)

    return pl.pallas_call(
        kernel,
        grid=(steps,),
        in_specs=[
            pl.BlockSpec((lanes, rows, block), lambda i: (0, 0, i)),
            pl.BlockSpec((lanes, rows, block), lambda i: (0, 0, i)),
            pl.BlockSpec((2, block, k), lambda i: (0, i, 0)),
            pl.BlockSpec((2, block, k), lambda i: (0, i, 0)),
            pl.BlockSpec((2, block), lambda i: (0, i)),
        ],
        out_specs=pl.BlockSpec((8 * rows, 3 * k), lambda i: (0, 0)),
        out_shape=jax.ShapeDtypeStruct((8 * rows, 3 * k), bf16),
        scratch_shapes=[
            pltpu.VMEM((total, 6 * k), f32),
            pltpu.VMEM((total, k), f32),
            pltpu.VMEM((3, 8 * rows, k), f32),
        ],
        compiler_params=pltpu.CompilerParams(vmem_limit_bytes=48 << 20),
        name="front",
    )(x, c, down, up, gain)


def prepare(section, down, up, gain, down_other, up_other, gain_other):
    _, features, k = down.shape
    block = 1024
    steps = features // block

    def kernel(s_ref, d, u, g, d2, u2, g2, w_ref, low_ref, high_ref):
        step = pl.program_id(0)
        gains = jnp.concatenate([g[...], g2[...]] * 2, axis=0).T
        first = s_ref[0] == 0

        def choose(one, two):
            return jnp.where(first, one.astype(f32), two.astype(f32))

        gain_one = choose(gains[:, :2], gains[:, 2:4])
        gain_two = choose(gains[:, 2:4], gains[:, :2])
        parts = [
            choose(d[1], d2[1]) * gain_one[:, 1:2],
            choose(u[0], u2[0]),
            choose(u[1], u2[1]),
            choose(d2[0], d[0]) * gain_two[:, :1],
            choose(d2[1], d[1]) * gain_two[:, 1:2],
            choose(u2[0], u[0]),
        ]
        parts = [part.astype(bf16) for part in parts]
        weights = joined(parts)
        w_ref[...] = weights
        low = dot_tn(joined(parts[1:3]), weights)
        high = dot_tn(parts[5], joined(parts[4:]))

        @pl.when(step == 0)
        def _():
            low_ref[...] = low
            high_ref[...] = high

        @pl.when(step > 0)
        def _():
            low_ref[...] += low
            high_ref[...] += high

    two = pl.BlockSpec((2, block, k), lambda i, s: (0, i, 0))
    row = pl.BlockSpec((2, block), lambda i, s: (0, i))
    return pl.pallas_call(
        kernel,
        grid_spec=pltpu.PrefetchScalarGridSpec(
            num_scalar_prefetch=1,
            grid=(steps,),
            in_specs=[two, two, row, two, two, row],
            out_specs=[
                pl.BlockSpec((block, 6 * k), lambda i, s: (i, 0)),
                pl.BlockSpec((2 * k, 6 * k), lambda i, s: (0, 0)),
                pl.BlockSpec((k, 2 * k), lambda i, s: (0, 0)),
            ],
        ),
        out_shape=[
            jax.ShapeDtypeStruct((features, 6 * k), bf16),
            jax.ShapeDtypeStruct((2 * k, 6 * k), f32),
            jax.ShapeDtypeStruct((k, 2 * k), f32),
        ],
        compiler_params=pltpu.CompilerParams(vmem_limit_bytes=48 << 20),
        name="prepare",
    )(section[None], down, up, gain, down_other, up_other, gain_other)


def turn(x, c):
    lanes, rows, features = x.shape
    block = 1024

    def kernel(x_ref, c_ref, out):
        for j in range(lanes):
            out[:, j * rows : (j + 1) * rows] = x_ref[j].T
            out[:, (lanes + j) * rows : (lanes + j + 1) * rows] = c_ref[j].T

    spec = pl.BlockSpec((lanes, rows, block), lambda i: (0, 0, i))
    return pl.pallas_call(
        kernel,
        grid=(features // block,),
        in_specs=[spec, spec],
        out_specs=pl.BlockSpec((block, 2 * lanes * rows), lambda i: (i, 0)),
        out_shape=jax.ShapeDtypeStruct((features, 2 * lanes * rows), bf16),
        compiler_params=pltpu.CompilerParams(vmem_limit_bytes=48 << 20),
        name="turn",
    )(x, c)


def meet(received, first, second, gram_low, gram_high, lanes, features):
    total = first.shape[0]
    group = total // lanes
    slots = received.shape[1]
    k = received.shape[2] // 3

    def kernel(rec, i0, i1, t0, t1, low_gram, high_gram, out, mix):
        grid = lax.broadcasted_iota(jnp.int32, (total, slots), 1)
        turned = lax.broadcasted_iota(jnp.int32, (slots, total), 0)

        def pick(base):
            return (grid == base).astype(f32).astype(bf16)

        def place(base):
            return (turned == base).astype(f32).astype(bf16)

        at_start = pick(i0[...])
        at_start_next = pick(i0[...] + 1)
        at_end = pick(i1[...] + 1)
        lane = lax.broadcasted_iota(jnp.int32, (total, 1), 0) // group
        norm_row = i0[...] - 2 * lane + 6
        sums = dot(pick(norm_row), rec[0]) + dot(pick(norm_row + 1), rec[0])
        square_sum = jnp.concatenate(
            [sums[j * group : (j + 1) * group, j * k : (j + 1) * k] for j in range(lanes)], axis=0
        )[:, :1]
        proj, cot = [], []
        for s in range(2):
            low = dot(at_start, rec[s])
            high = dot(at_start_next, rec[s, :, :k])
            tail = dot(at_end, rec[s, :, k:])
            proj += [(low[:, :k], low[:, 2 * k :]), (low[:, k : 2 * k], high)]
            cot += [tail[:, :k], tail[:, k:]]
        active, back, less, mix_first, mix_second = row_stage(
            proj, cot, square_sum, low_gram[...], high_gram[...], features
        )
        to_start = place(t0[...])
        to_start_next = place(t0[...] + 1)
        to_end = place(t1[...] + 1)
        for s in range(2):
            l0, l1 = 2 * s, 2 * s + 1
            out[s] = dot(to_start, joined([back[l0], back[l1], less[l0]])).astype(bf16)
            high = dot(to_start_next, less[l1])
            tail = dot(to_end, joined([active[l0], active[l1]]))
            out[s] += joined([high, tail]).astype(bf16)
        for s, table in enumerate((mix_first, mix_second)):
            for i, row in enumerate(table):
                mix[s, i * k : (i + 1) * k, :] = joined(row).astype(bf16)

    return pl.pallas_call(
        kernel,
        out_shape=[
            jax.ShapeDtypeStruct(received.shape, bf16),
            jax.ShapeDtypeStruct((2, 6 * k, 4 * k), bf16),
        ],
        compiler_params=pltpu.CompilerParams(vmem_limit_bytes=48 << 20),
        name="meet",
    )(
        received,
        first[:, None],
        second[:, None],
        first[None, :],
        second[None, :],
        gram_low,
        gram_high,
    )


def unpack(returned, mix_own, mix_other, lanes):
    rows, k = returned.shape[0] // 8, returned.shape[1] // 3

    def kernel(ret, own, oth, xs, cs, mix, wide):
        for t in range(3):
            wide[t] = ret[:, t * k : (t + 1) * k].astype(f32)
        for j in range(lanes):
            at = slice(j * rows, (j + 1) * rows)
            low = [wide[t, pl.ds(2 * j, rows, stride=8), :].astype(bf16) for t in range(3)]
            high = [wide[t, pl.ds(2 * j + 1, rows, stride=8), :].astype(bf16) for t in range(3)]
            xs[at, :] = joined(low + high[:1])
            cs[at, :] = joined(high[1:])
        mix[...] = (own[...].astype(f32) + oth[...].astype(f32)).astype(bf16)

    return pl.pallas_call(
        kernel,
        out_shape=[
            jax.ShapeDtypeStruct((lanes * rows, 4 * k), bf16),
            jax.ShapeDtypeStruct((lanes * rows, 2 * k), bf16),
            jax.ShapeDtypeStruct(mix_own.shape, bf16),
        ],
        scratch_shapes=[pltpu.VMEM((3, 8 * rows, k), f32)],
        compiler_params=pltpu.CompilerParams(vmem_limit_bytes=48 << 20),
        name="unpack",
    )(returned, mix_own, mix_other)


def piece(at, turned, weights, gain, xs, cs, mix, minor):
    features, both = turned.shape
    k = cs.shape[1] // 2
    quarter = features // 4
    block = 640
    steps = quarter // block
    total = both // 2
    fresh = minor is None

    def kernel(at_ref, t_ref, w_ref, g_ref, xs_ref, cs_ref, mix_ref, *refs):
        out, last_out = refs[-2:]
        value = dot(t_ref[:, :total], xs_ref[...]) + dot(w_ref[...], mix_ref[...])
        last = dot(t_ref[:, total:], cs_ref[...])
        gains = jnp.concatenate([g_ref[...]] * 4, axis=0).T
        out[:, :k] = (value[:, :k] * gains[:, :1]).astype(bf16)
        out[:, k : 2 * k] = (value[:, k : 2 * k] * gains[:, 1:2]).astype(bf16)
        out[:, 2 * k :] = (value[:, 2 * k : 3 * k] + last[:, :k]).astype(bf16)
        last_out[0] = (value[:, 3 * k :] + last[:, k:]).astype(bf16)

    in_specs = [
        pl.BlockSpec((block, both), lambda i, at: (at[0] * steps + i, 0)),
        pl.BlockSpec((block, 6 * k), lambda i, at: (at[0] * steps + i, 0)),
        pl.BlockSpec((2, block), lambda i, at: (0, at[0] * steps + i)),
        pl.BlockSpec((total, 4 * k), lambda i, at: (0, 0)),
        pl.BlockSpec((total, 2 * k), lambda i, at: (0, 0)),
        pl.BlockSpec((6 * k, 4 * k), lambda i, at: (0, 0)),
    ]
    operands = [at[None], turned, weights, gain, xs, cs, mix]
    if not fresh:
        in_specs.append(pl.BlockSpec(memory_space=pl.ANY))
        operands.append(minor)
    return pl.pallas_call(
        kernel,
        grid_spec=pltpu.PrefetchScalarGridSpec(
            num_scalar_prefetch=1,
            grid=(steps,),
            in_specs=in_specs,
            out_specs=[
                pl.BlockSpec((block, 3 * k), lambda i, at: (i, 0)),
                pl.BlockSpec((1, block, k), lambda i, at: (at[0], i, 0)),
            ],
        ),
        out_shape=[
            jax.ShapeDtypeStruct((quarter, 3 * k), bf16),
            jax.ShapeDtypeStruct((4, quarter, k), bf16),
        ],
        input_output_aliases={} if fresh else {7: 1},
        compiler_params=pltpu.CompilerParams(vmem_limit_bytes=48 << 20),
        name="piece",
    )(*operands)


def finish(starts, major, minor, features, k):
    quarter = features // 4
    part = quarter // 4

    def kernel(at, *refs):
        ins, (down, up) = refs[:8], refs[8:]
        group = pl.program_id(0)

        def run(blocks, out, which):
            total = jnp.zeros((8, k), f32)
            for ref in blocks:
                v = ref[...].astype(f32)
                total = total + jnp.sum((v * v).reshape(quarter // 8, 8, k), axis=0)
            mean = jnp.sum(total) * (1.0 / (features * k))
            scale = lax.rsqrt(jnp.full((1, k), mean, f32) + step_eps)
            for i, ref in enumerate(blocks):
                for j in range(4):
                    row = pl.multiple_of(at[which, i, j], 16)
                    v = ref[j * part : (j + 1) * part, :].astype(f32)
                    out[0, pl.ds(row, part), :] = (v * scale).astype(bf16)

        @pl.when(group < 2)
        def _():
            run(ins[:4], down, 0)

        @pl.when(group == 2)
        def _():
            run(ins[:4], up, 0)

        @pl.when(group == 3)
        def _():
            run(ins[4:], up, 1)

    return pl.pallas_call(
        kernel,
        grid_spec=pltpu.PrefetchScalarGridSpec(
            num_scalar_prefetch=1,
            grid=(4,),
            in_specs=[pl.BlockSpec((quarter, k), lambda g, at: (0, jnp.minimum(g, 2)))] * 4
            + [pl.BlockSpec((quarter, k), lambda g, at: (0, 0))] * 4,
            out_specs=[
                pl.BlockSpec((1, features, k), lambda g, at: (jnp.minimum(g, 1), 0, 0)),
                pl.BlockSpec((1, features, k), lambda g, at: (jnp.maximum(g - 2, 0), 0, 0)),
            ],
        ),
        out_shape=[jax.ShapeDtypeStruct((2, features, k), bf16)] * 2,
        compiler_params=pltpu.CompilerParams(vmem_limit_bytes=48 << 20),
        name="finish",
    )(starts, *major, *minor)


def coords(peer):
    return peer // 16, (peer // 4) % 4, peer % 4


MAJOR = ((0, 1, 2), (1, 0, 2))
MINOR = ((2, 1, 0), (2, 0, 1))


def hop(values, order, stage, by):
    pairs = []
    for s in range(2):
        axis = order[s][stage]
        for p in range(64):
            c = list(coords(p))
            c[axis] = (c[axis] + by) % 4
            pairs.append((s * 64 + p, s * 64 + c[0] * 16 + c[1] * 4 + c[2]))
    return lax.ppermute(values, ("section", "peer"), pairs)


def summed(parts, order, at):
    step = parts[0].shape[0] // 4

    def cut(by):
        start = ((at + by) % 4) * step
        return sum(lax.dynamic_slice_in_dim(p, start, step, axis=0).astype(f32) for p in parts)

    arrived = [hop(cut(by).astype(bf16), order, 1, by) for by in (2, 1, 3)]
    own = cut(0) + sum(part.astype(f32) for part in arrived)
    own = lax.optimization_barrier(own.astype(bf16))
    two, one, three = [hop(own, order, 2, by).astype(f32) for by in (2, 1, 3)]
    return ((own.astype(f32) + two) + (one + three)).astype(bf16)


def gathered(block, order):
    wide = jnp.concatenate([block] + [hop(block, order, 1, by) for by in (1, 2, 3)], axis=0)
    return [wide] + [hop(wide, order, 0, by) for by in (1, 2, 3)]


def local(inputs, cotangent, down_proj, up_proj, norm_gain, wiring, live_mask):
    section = lax.axis_index("section")
    peer = lax.axis_index("peer")
    _, lanes, rows, features = inputs.shape
    k = down_proj.shape[3]
    x, c = inputs[0], cotangent[0]
    gain, up = norm_gain[0], up_proj[0]
    is_first = section == 0
    swap = [(0, 1), (1, 0)]
    down = down_proj[0]
    down_other = lax.ppermute(down, "section", swap)
    up_other = lax.ppermute(up, "section", swap)
    gain_other = lax.ppermute(gain, "section", swap)
    sent = front(x, c, down, up, gain)
    received = lax.all_to_all(
        sent.reshape(rows, 8, 3 * k), ("section", "peer"), 0, 0, tiled=True
    ).reshape(2, -1, 3 * k)
    weights, gram_low, gram_high = prepare(
        section, down, up, gain, down_other, up_other, gain_other
    )
    holders = peer_table(wiring, live_mask)
    total = holders.shape[1]
    lane_of = jnp.arange(total, dtype=jnp.int32) // (total // lanes)
    base = holders * 8 + 2 * lane_of
    out, mix = meet(
        received, base[0], base[1], gram_low, gram_high, lanes, features
    )
    mix_own = lax.dynamic_index_in_dim(mix, section, 0, keepdims=False)
    mix_other = lax.ppermute(
        lax.dynamic_index_in_dim(mix, 1 - section, 0, keepdims=False), "section", swap
    )
    returned = lax.all_to_all(
        out.reshape(rows, 8, 3 * k), ("section", "peer"), 0, 0, tiled=True
    ).reshape(8 * rows, 3 * k)
    turned = turn(*lax.optimization_barrier((x, c, mix))[:2])
    xs, cs, mix = unpack(returned, mix_own, mix_other, lanes)

    where = jnp.stack(coords(peer))
    at_major = [jnp.where(is_first, where[MAJOR[0][i]], where[MAJOR[1][i]]) for i in range(3)]
    at_minor = [jnp.where(is_first, where[MINOR[0][i]], where[MINOR[1][i]]) for i in range(3)]

    major, minor = [], None
    for by in (2, 1, 3, 0):
        index = ((at_major[0] + by) % 4).astype(jnp.int32)
        part, minor = piece(index, turned, weights, gain, xs, cs, mix, minor)
        major.append(hop(part, MAJOR, 0, by) if by else part)

    def pick_minor(by):
        return lax.dynamic_index_in_dim(minor, (at_minor[0] + by) % 4, 0, keepdims=False)

    minor = [hop(pick_minor(by), MINOR, 0, by) for by in (2, 1, 3)] + [pick_minor(0)]
    minor = gathered(summed(minor, MINOR, at_minor[1]), MINOR)
    major = gathered(summed(major, MAJOR, at_major[1]), MAJOR)

    back = jnp.arange(4, dtype=jnp.int32)
    starts = jnp.stack(
        [
            ((at[0] - back) % 4)[:, None] * (features // 4)
            + ((at[1] - back) % 4)[None, :] * (features // 16)
            for at in (at_major, at_minor)
        ]
    ).astype(jnp.int32)
    down_step, up_step = finish(starts, major, minor, features, k)
    return down_step[None], up_step[None]


def solution(mesh):
    placed = (
        P("peer", None, None, None),
        P("peer", None, None, None),
        P("section", None, None, None),
        P("section", None, None, None),
        P("section", None, None),
        P(),
        P(),
    )
    return jax.shard_map(
        local,
        mesh=mesh,
        in_specs=placed,
        out_specs=(P("section", None, None, None), P("section", None, None, None)),
        check_vma=False,
    )
```

profile of v0, /device:TPU:0, one launch (start us, length us, event | category | flops | bytes accessed | tf_op | source)
XLA Modules:
  0.0 191.1 jit_solution(15370341498073933074)
XLA Ops:
  1.3 1.7 copy-done.1
  3.1 1.7 copy-done.3
  5.6 10.2 %front.1 = bf16[1024,384]{1,0:T(8,128)(2,1)} custom-call(bf16[3,128,5120]{2,1,0:T(8,128)(2,1)} %bitcast.42, bf16[3,128,5120]{2,1,0:T(8,128)(2,1)} %bitcast.59, bf16[2,5120,128]{2,1,0:T(8,128)(2,1)S(1)} %bitcast.45, bf16[2,5120,128]{2,1,0:T(8,128)(2,1)S(1)} %bitcast.49, f32[2,5120]{1,0:T(2,128)S(1)} %bitcast.53), custom_call_target="tpu_custom_call" | custom-call | tf_op jit(solution)/shard_map/front/pallas_call | solution.py:186
  15.7 11.2 %all-to-all-start = ((bf16[128,8,384]{2,1,0:T(8,128)(2,1)}), bf16[128,8,384]{2,1,0:T(8,128)(2,1)S(1)}, u32[]{:S(2)}, u32[]{:S(2)}) async-start(bf16[128,8,384]{2,1,0:T(8,128)(2,1)} %bitcast.6), calls=%async_computation | async-start | bytes 1572864 | tf_op jit(solution)/shard_map/all_to_all | solution.py:541
  28.9 11.4 %prepare.1 = (bf16[5120,768]{1,0:T(8,128)(2,1)}, f32[256,768]{1,0:T(8,128)S(1)}, f32[128,256]{1,0:T(8,128)S(1)}) custom-call(s32[1]{0:T(128)} %bitcast.10.s_ref, bf16[2,5120,128]{2,1,0:T(8,128)(2,1)S(1)} %bitcast.46, bf16[2,5120,128]{2,1,0:T(8,128)(2,1)} %bitcast.48, f32[2,5120]{1,0:T(2,128)S(1)} %bitcast.54, bf16[2,5120,128]{2,1,0:T(8,128)(2,1)} %collective-permute-done.d2, ...), custom_call_target="tpu_custom_call" | custom-call | tf_op jit(solution)/shard_map/prepare/pallas_call | solution.py:249
  46.6 3.7 %meet.1 = (bf16[2,512,384]{2,1,0:T(8,128)(2,1)}, bf16[2,768,512]{2,1,0:T(8,128)(2,1)S(1)}) custom-call(bf16[2,512,384]{2,1,0:T(8,128)(2,1)S(1)} %bitcast.50, s32[144,1]{1,0:T(8,128)S(1)} %copy-done.12, s32[144,1]{1,0:T(8,128)S(1)} %copy-done.13, s32[1,144]{1,0:T(1,128)S(1)} %get-tuple-element.56.t0, s32[1,144]{1,0:T(1,128)S(1)} %get-tuple-element.53.t1, ...), custom_call_target="tpu_custom_call" | custom-call | tf_op jit(solution)/shard_map/meet/pallas_call | solution.py:340
  50.5 9.1 %all-to-all-start.1 = ((bf16[128,8,384]{2,1,0:T(8,128)(2,1)}), bf16[128,8,384]{2,1,0:T(8,128)(2,1)S(1)}, u32[]{:S(2)}, u32[]{:S(2)}) async-start(bf16[128,8,384]{2,1,0:T(8,128)(2,1)} %bitcast.11), calls=%async_computation.1 | async-start | bytes 1572864 | tf_op jit(solution)/shard_map/all_to_all | solution.py:558
  59.7 2.1 %copy-done = bf16[1,3,128,5120]{3,2,1,0:T(8,128)(2,1)S(1)} copy-done((bf16[1,3,128,5120]{3,2,1,0:T(8,128)(2,1)S(1)}, bf16[1,3,128,5120]{3,2,1,0:T(8,128)(2,1)}, u32[]{:S(2)}) %copy-start) | copy-done | bytes 3932184
  61.8 7.4 %turn.1.t_ref = bf16[5120,768]{1,0:T(8,128)(2,1)} custom-call(bf16[3,128,5120]{2,1,0:T(8,128)(2,1)S(1)} %bitcast.43, bf16[3,128,5120]{2,1,0:T(8,128)(2,1)} %bitcast.60), custom_call_target="tpu_custom_call" | custom-call | tf_op jit(solution)/shard_map/turn/pallas_call | solution.py:281
  69.2 6.1 %all-to-all-done.1 = bf16[128,8,384]{2,1,0:T(8,128)(2,1)S(1)} async-done(((bf16[128,8,384]{2,1,0:T(8,128)(2,1)}), bf16[128,8,384]{2,1,0:T(8,128)(2,1)S(1)}, u32[]{:S(2)}, u32[]{:S(2)}) %all-to-all-start.1) | async-done | bytes 786464 | tf_op jit(solution)/shard_map/all_to_all | solution.py:558
  78.0 4.9 %piece.4 = (bf16[1280,384]{1,0:T(8,128)(2,1)}, bf16[4,1280,128]{2,1,0:T(8,128)(2,1)S(1)}) custom-call(s32[1]{0:T(128)} %bitcast.at_ref, bf16[5120,768]{1,0:T(8,128)(2,1)} %turn.1.t_ref, bf16[5120,768]{1,0:T(8,128)(2,1)} %get-tuple-element.27.w_ref, f32[2,5120]{1,0:T(2,128)S(1)} %bitcast.55, bf16[384,512]{1,0:T(8,128)(2,1)S(1)} %get-tuple-element.29.xs_ref, ...), custom_call_target="tpu_custom_call" | custom-call | tf_op jit(solution)/shard_map/piece/pallas_call | solution.py:417
  82.9 4.9 %piece.5 = (bf16[1280,384]{1,0:T(8,128)(2,1)}, bf16[4,1280,128]{2,1,0:T(8,128)(2,1)S(1)}) custom-call(s32[1]{0:T(128)} %bitcast.15.at_ref, bf16[5120,768]{1,0:T(8,128)(2,1)} %turn.1.t_ref, bf16[5120,768]{1,0:T(8,128)(2,1)} %get-tuple-element.27.w_ref, f32[2,5120]{1,0:T(2,128)S(1)} %bitcast.56, ...), custom_call_target="tpu_custom_call", output_to_operand_aliasing={{1}: (7, {})} | custom-call | tf_op jit(solution)/shard_map/piece/pallas_call | solution.py:417
  87.8 4.9 %piece.6 = (bf16[1280,384]{1,0:T(8,128)(2,1)}, bf16[4,1280,128]{2,1,0:T(8,128)(2,1)S(1)}) custom-call(s32[1]{0:T(128)} %bitcast.16.at_ref, bf16[5120,768]{1,0:T(8,128)(2,1)} %turn.1.t_ref, bf16[5120,768]{1,0:T(8,128)(2,1)} %get-tuple-element.27.w_ref, f32[2,5120]{1,0:T(2,128)S(1)} %bitcast.57, ...), custom_call_target="tpu_custom_call", output_to_operand_aliasing={{1}: (7, {})} | custom-call | tf_op jit(solution)/shard_map/piece/pallas_call | solution.py:417
  95.9 4.1 %piece.7 = (bf16[1280,384]{1,0:T(8,128)(2,1)S(1)}, bf16[4,1280,128]{2,1,0:T(8,128)(2,1)S(1)}) custom-call(s32[1]{0:T(128)} %bitcast.17.at_ref, bf16[5120,768]{1,0:T(8,128)(2,1)} %turn.1.t_ref, bf16[5120,768]{1,0:T(8,128)(2,1)} %get-tuple-element.27.w_ref, f32[2,5120]{1,0:T(2,128)S(1)} %bitcast.58, ...), custom_call_target="tpu_custom_call", output_to_operand_aliasing={{1}: (7, {})} | custom-call | tf_op jit(solution)/shard_map/piece/pallas_call | solution.py:417
  104.5 2.6 %collective-permute-done.6 = bf16[1280,384]{1,0:T(8,128)(2,1)} collective-permute-done((bf16[1280,384]{1,0:T(8,128)(2,1)}, bf16[1280,384]{1,0:T(8,128)(2,1)}, u32[]{:S(2)}, u32[]{:S(2)}) %collective-permute-start.6) | collective-permute-done | bytes 983072 | tf_op jit(solution)/shard_map/ppermute | solution.py:505
  107.6 12.4 %collective-permute-done.5 = bf16[1280,384]{1,0:T(8,128)(2,1)} collective-permute-done((bf16[1280,384]{1,0:T(8,128)(2,1)}, bf16[1280,384]{1,0:T(8,128)(2,1)}, u32[]{:S(2)}, u32[]{:S(2)}) %collective-permute-start.5) | collective-permute-done | bytes 983072 | tf_op jit(solution)/shard_map/ppermute | solution.py:505
  120.0 2.8 %add_convert_fusion.4 = (bf16[320,384]{1,0:T(8,128)(2,1)}, bf16[320,384]{1,0:T(8,128)(2,1)S(1)}, bf16[320,384]{1,0:T(8,128)(2,1)}) fusion(bf16[1280,384]{1,0:T(8,128)(2,1)S(1)} %copy-done.7, s32[]{:T(128)S(6)} %select_n.213, bf16[1280,384]{1,0:T(8,128)(2,1)} %collective-permute-done.6, bf16[1280,384]{1,0:T(8,128)(2,1)} %collective-permute-done.5, ...), kind=kLoop, calls=%fused_computation.7 | loop fusion | flops 2949120 | bytes 3686412 | tf_op jit(solution)/shard_map/convert_element_type | solution.py:515
  124.5 2.1 %collective-permute-start.9 = (bf16[320,384]{1,0:T(8,128)(2,1)S(1)}, bf16[320,384]{1,0:T(8,128)(2,1)}, u32[]{:S(2)}, u32[]{:S(2)}) collective-permute-start(bf16[320,384]{1,0:T(8,128)(2,1)S(1)} %get-tuple-element.43), channel_id=1, source_target_pairs={{0,12},{1,13},{2,14},{3,15},{4,0},{5,1},{6,2},{7,3},{8,4},{9,5},{1... | collective-permute-start | bytes 737288 | tf_op jit(solution)/shard_map/ppermute | solution.py:505
  127.4 1.8 collective-permute-start.22
  133.5 1.7 add_convert_fusion.1
  137.1 2.2 %collective-permute-start.12 = (bf16[320,384]{1,0:T(8,128)(2,1)S(1)}, bf16[320,384]{1,0:T(8,128)(2,1)S(1)}, u32[]{:S(2)}, u32[]{:S(2)}) collective-permute-start(bf16[320,384]{1,0:T(8,128)(2,1)S(1)} %add_convert_fusion.1), channel_id=1, source_target_pairs={{0,3},{1,0},{2,1},{3,2},{4,7},{5,4},{6,5},{7,6},{8,11},{9,8},{10,9... | collective-permute-start | bytes 737288 | tf_op jit(solution)/shard_map/ppermute | solution.py:505
  140.4 1.9 %collective-permute-start.25 = (bf16[320,128]{1,0:T(8,128)(2,1)S(1)}, bf16[320,128]{1,0:T(8,128)(2,1)S(1)}, u32[]{:S(2)}, u32[]{:S(2)}) collective-permute-start(bf16[320,128]{1,0:T(8,128)(2,1)S(1)} %fusion.4), channel_id=1, source_target_pairs={{0,32},{1,33},{2,34},{3,35},{4,36},{5,37},{6,38},{7,39},{8,40},{9,... | collective-permute-start | bytes 245768 | tf_op jit(solution)/shard_map/ppermute | solution.py:505
  142.3 2.6 %collective-permute-done.10 = bf16[320,384]{1,0:T(8,128)(2,1)S(1)} collective-permute-done((bf16[320,384]{1,0:T(8,128)(2,1)S(1)}, bf16[320,384]{1,0:T(8,128)(2,1)S(1)}, u32[]{:S(2)}, u32[]{:S(2)}) %collective-permute-start.10) | collective-permute-done | bytes 245792 | tf_op jit(solution)/shard_map/ppermute | solution.py:505
  147.6 3.3 %collective-permute-start.14 = (bf16[320,384]{1,0:T(8,128)(2,1)S(1)}, bf16[320,384]{1,0:T(8,128)(2,1)S(1)}, u32[]{:S(2)}, u32[]{:S(2)}) collective-permute-start(bf16[320,384]{1,0:T(8,128)(2,1)S(1)} %add_convert_fusion), channel_id=1, source_target_pairs={{0,8},{1,9},{2,10},{3,11},{4,12},{5,13},{6,14},{7,15},{8,0},{9,1},... | collective-permute-start | bytes 737288 | tf_op jit(solution)/shard_map/ppermute | solution.py:505
  151.2 1.8 collective-permute-start.28
  159.7 2.7 %collective-permute-start.17 = (bf16[1280,384]{1,0:T(8,128)(2,1)S(1)}, bf16[1280,384]{1,0:T(8,128)(2,1)S(1)}, u32[]{:S(2)}, u32[]{:S(2)}) collective-permute-start(bf16[1280,384]{1,0:T(8,128)(2,1)S(1)} %pad_maximum_fusion.refs_0_), channel_id=1, source_target_pairs={{0,32},{1,33},{2,34},{3,35},{4,36},{5,37},{6,38},{7,39},{8,40},{9,... | collective-permute-start | bytes 2949128 | tf_op jit(solution)/shard_map/ppermute | solution.py:505
  163.8 2.5 %collective-permute-start.32 = (bf16[1280,128]{1,0:T(8,128)(2,1)S(1)}, bf16[1280,128]{1,0:T(8,128)(2,1)S(1)}, u32[]{:S(2)}, u32[]{:S(2)}) collective-permute-start(bf16[1280,128]{1,0:T(8,128)(2,1)S(1)} %pad_maximum_fusion.1.refs_4_), channel_id=1, source_target_pairs={{0,2},{1,3},{2,0},{3,1},{4,6},{5,7},{6,4},{7,5},{8,10},{9,11},{10,... | collective-permute-start | bytes 983048 | tf_op jit(solution)/shard_map/ppermute | solution.py:505
  166.3 8.6 %collective-permute-done.31.refs_5_ = bf16[1280,128]{1,0:T(8,128)(2,1)S(1)} collective-permute-done((bf16[1280,128]{1,0:T(8,128)(2,1)S(1)}, bf16[1280,128]{1,0:T(8,128)(2,1)S(1)}, u32[]{:S(2)}, u32[]{:S(2)}) %collective-permute-start.31) | collective-permute-done | bytes 327712 | tf_op jit(solution)/shard_map/ppermute | solution.py:505
  175.5 3.0 %collective-permute-done.32.refs_6_ = bf16[1280,128]{1,0:T(8,128)(2,1)S(1)} collective-permute-done((bf16[1280,128]{1,0:T(8,128)(2,1)S(1)}, bf16[1280,128]{1,0:T(8,128)(2,1)S(1)}, u32[]{:S(2)}, u32[]{:S(2)}) %collective-permute-start.32) | collective-permute-done | bytes 327712 | tf_op jit(solution)/shard_map/ppermute | solution.py:505
  178.5 3.4 %collective-permute-done.33.refs_7_ = bf16[1280,128]{1,0:T(8,128)(2,1)S(1)} collective-permute-done((bf16[1280,128]{1,0:T(8,128)(2,1)S(1)}, bf16[1280,128]{1,0:T(8,128)(2,1)S(1)}, u32[]{:S(2)}, u32[]{:S(2)}) %collective-permute-start.33) | collective-permute-done | bytes 327712 | tf_op jit(solution)/shard_map/ppermute | solution.py:505
  182.0 3.0 %collective-permute-done.17.refs_2_ = bf16[1280,384]{1,0:T(8,128)(2,1)S(1)} collective-permute-done((bf16[1280,384]{1,0:T(8,128)(2,1)S(1)}, bf16[1280,384]{1,0:T(8,128)(2,1)S(1)}, u32[]{:S(2)}, u32[]{:S(2)}) %collective-permute-start.17) | collective-permute-done | bytes 983072 | tf_op jit(solution)/shard_map/ppermute | solution.py:505
  185.5 5.6 %finish.1 = (bf16[2,5120,128]{2,1,0:T(8,128)(2,1)}, bf16[2,5120,128]{2,1,0:T(8,128)(2,1)}) custom-call(s32[2,4,4]{2,1,0:T(4,128)S(1)} %pad_add_fusion.at, bf16[1280,384]{1,0:T(8,128)(2,1)S(1)} %pad_maximum_fusion.refs_0_, bf16[1280,384]{1,0:T(8,128)(2,1)S(1)} %collective-permute-done.16.refs_1_, bf16[1280,384]{1,0:T(8,128)(2,1)S(1)} %collective-permute-done.17.refs_2_, ...), custom_call_target="tpu_custom_call" | custom-call | tf_op jit(solution)/shard_map/finish/pallas_call | solution.py:471
  (109 shorter events, 42.7 us)
Async XLA Ops:
  0.6 28.2 %collective-permute-start = (bf16[2,5120,128]{2,1,0:T(8,128)(2,1)}, bf16[2,5120,128]{2,1,0:T(8,128)(2,1)}, u32[]{:S(2)}, u32[]{:S(2)}) collective-permute-start(bf16[2,5120,128]{2,1,0:T(8,128)(2,1)} %bitcast.44), channel_id=1, source_target_pairs={{0,64},{64,0},{1,65},{65,1},{2,66},{66,2},{3,67},{67,3},{4,68},{68... | collective-permute-start | bytes 7864328 | tf_op jit(solution)/shard_map/ppermute | solution.py:537
  0.7 28.1 %collective-permute-start.1 = (bf16[2,5120,128]{2,1,0:T(8,128)(2,1)}, bf16[2,5120,128]{2,1,0:T(8,128)(2,1)}, u32[]{:S(2)}, u32[]{:S(2)}) collective-permute-start(bf16[2,5120,128]{2,1,0:T(8,128)(2,1)} %bitcast.47), channel_id=1, source_target_pairs={{0,64},{64,0},{1,65},{65,1},{2,66},{66,2},{3,67},{67,3},{4,68},{68... | collective-permute-start | bytes 7864328 | tf_op jit(solution)/shard_map/ppermute | solution.py:538
  1.2 27.6 %collective-permute-start.2 = (f32[2,5120]{1,0:T(2,128)}, f32[2,5120]{1,0:T(2,128)S(1)}, u32[]{:S(2)}, u32[]{:S(2)}) collective-permute-start(f32[2,5120]{1,0:T(2,128)} %bitcast.52), channel_id=1, source_target_pairs={{0,64},{64,0},{1,65},{65,1},{2,66},{66,2},{3,67},{67,3},{4,68},{68... | collective-permute-start | bytes 122888 | tf_op jit(solution)/shard_map/ppermute | solution.py:539
  15.7 27.1 %all-to-all-start = ((bf16[128,8,384]{2,1,0:T(8,128)(2,1)}), bf16[128,8,384]{2,1,0:T(8,128)(2,1)S(1)}, u32[]{:S(2)}, u32[]{:S(2)}) async-start(bf16[128,8,384]{2,1,0:T(8,128)(2,1)} %bitcast.6), calls=%async_computation | async-start | bytes 1572864 | tf_op jit(solution)/shard_map/all_to_all | solution.py:541
  50.4 24.9 %collective-permute-start.3 = (bf16[768,512]{1,0:T(8,128)(2,1)S(1)}, bf16[768,512]{1,0:T(8,128)(2,1)S(1)}, u32[]{:S(2)}, u32[]{:S(2)}) collective-permute-start(bf16[768,512]{1,0:T(8,128)(2,1)S(1)} %get-tuple-element.48), channel_id=1, source_target_pairs={{0,64},{64,0},{1,65},{65,1},{2,66},{66,2},{3,67},{67,3},{4,68},{68... | collective-permute-start | bytes 2359304 | tf_op jit(solution)/shard_map/ppermute | solution.py:555
  50.5 24.8 %all-to-all-start.1 = ((bf16[128,8,384]{2,1,0:T(8,128)(2,1)}), bf16[128,8,384]{2,1,0:T(8,128)(2,1)S(1)}, u32[]{:S(2)}, u32[]{:S(2)}) async-start(bf16[128,8,384]{2,1,0:T(8,128)(2,1)} %bitcast.11), calls=%async_computation.1 | async-start | bytes 1572864 | tf_op jit(solution)/shard_map/all_to_all | solution.py:558
  92.7 14.4 %collective-permute-start.6 = (bf16[1280,384]{1,0:T(8,128)(2,1)}, bf16[1280,384]{1,0:T(8,128)(2,1)}, u32[]{:S(2)}, u32[]{:S(2)}) collective-permute-start(bf16[1280,384]{1,0:T(8,128)(2,1)} %get-tuple-element.36), channel_id=1, source_target_pairs={{0,48},{1,49},{2,50},{3,51},{4,52},{5,53},{6,54},{7,55},{8,56},{9,... | collective-permute-start | bytes 2949128 | tf_op jit(solution)/shard_map/ppermute | solution.py:505
  93.9 26.2 %collective-permute-start.5 = (bf16[1280,384]{1,0:T(8,128)(2,1)}, bf16[1280,384]{1,0:T(8,128)(2,1)}, u32[]{:S(2)}, u32[]{:S(2)}) collective-permute-start(bf16[1280,384]{1,0:T(8,128)(2,1)} %get-tuple-element.34), channel_id=1, source_target_pairs={{0,16},{1,17},{2,18},{3,19},{4,20},{5,21},{6,22},{7,23},{8,24},{9,... | collective-permute-start | bytes 2949128 | tf_op jit(solution)/shard_map/ppermute | solution.py:505
  94.7 25.3 %collective-permute-start.4 = (bf16[1280,384]{1,0:T(8,128)(2,1)}, bf16[1280,384]{1,0:T(8,128)(2,1)}, u32[]{:S(2)}, u32[]{:S(2)}) collective-permute-start(bf16[1280,384]{1,0:T(8,128)(2,1)} %get-tuple-element.32), channel_id=1, source_target_pairs={{0,32},{1,33},{2,34},{3,35},{4,36},{5,37},{6,38},{7,39},{8,40},{9,... | collective-permute-start | bytes 2949128 | tf_op jit(solution)/shard_map/ppermute | solution.py:505
  102.1 22.4 %collective-permute-start.19 = (bf16[1280,128]{1,0:T(8,128)(2,1)}, bf16[1280,128]{1,0:T(8,128)(2,1)S(1)}, u32[]{:S(2)}, u32[]{:S(2)}) collective-permute-start(bf16[1280,128]{1,0:T(8,128)(2,1)} %get-tuple-element.50), channel_id=1, source_target_pairs={{0,2},{1,3},{2,0},{3,1},{4,6},{5,7},{6,4},{7,5},{8,10},{9,11},{10,... | collective-permute-start | bytes 983048 | tf_op jit(solution)/shard_map/ppermute | solution.py:505
  103.4 23.2 %collective-permute-start.20 = (bf16[1280,128]{1,0:T(8,128)(2,1)}, bf16[1280,128]{1,0:T(8,128)(2,1)S(1)}, u32[]{:S(2)}, u32[]{:S(2)}) collective-permute-start(bf16[1280,128]{1,0:T(8,128)(2,1)} %get-tuple-element.52), channel_id=1, source_target_pairs={{0,1},{1,2},{2,3},{3,0},{4,5},{5,6},{6,7},{7,4},{8,9},{9,10},{10,1... | collective-permute-start | bytes 983048 | tf_op jit(solution)/shard_map/ppermute | solution.py:505
  107.1 19.5 %collective-permute-start.21 = (bf16[1280,128]{1,0:T(8,128)(2,1)}, bf16[1280,128]{1,0:T(8,128)(2,1)S(1)}, u32[]{:S(2)}, u32[]{:S(2)}) collective-permute-start(bf16[1280,128]{1,0:T(8,128)(2,1)} %get-tuple-element.51), channel_id=1, source_target_pairs={{0,3},{1,0},{2,1},{3,2},{4,7},{5,4},{6,5},{7,6},{8,11},{9,8},{10,9... | collective-permute-start | bytes 983048 | tf_op jit(solution)/shard_map/ppermute | solution.py:505
  122.9 8.1 %collective-permute-start.7 = (bf16[320,384]{1,0:T(8,128)(2,1)}, bf16[320,384]{1,0:T(8,128)(2,1)}, u32[]{:S(2)}, u32[]{:S(2)}) collective-permute-start(bf16[320,384]{1,0:T(8,128)(2,1)} %get-tuple-element.42), channel_id=1, source_target_pairs={{0,8},{1,9},{2,10},{3,11},{4,12},{5,13},{6,14},{7,15},{8,0},{9,1},... | collective-permute-start | bytes 737288 | tf_op jit(solution)/shard_map/ppermute | solution.py:505
  123.4 10.1 %collective-permute-start.8 = (bf16[320,384]{1,0:T(8,128)(2,1)}, bf16[320,384]{1,0:T(8,128)(2,1)}, u32[]{:S(2)}, u32[]{:S(2)}) collective-permute-start(bf16[320,384]{1,0:T(8,128)(2,1)} %get-tuple-element.44), channel_id=1, source_target_pairs={{0,4},{1,5},{2,6},{3,7},{4,8},{5,9},{6,10},{7,11},{8,12},{9,13},{1... | collective-permute-start | bytes 737288 | tf_op jit(solution)/shard_map/ppermute | solution.py:505
  124.5 9.0 %collective-permute-start.9 = (bf16[320,384]{1,0:T(8,128)(2,1)S(1)}, bf16[320,384]{1,0:T(8,128)(2,1)}, u32[]{:S(2)}, u32[]{:S(2)}) collective-permute-start(bf16[320,384]{1,0:T(8,128)(2,1)S(1)} %get-tuple-element.43), channel_id=1, source_target_pairs={{0,12},{1,13},{2,14},{3,15},{4,0},{5,1},{6,2},{7,3},{8,4},{9,5},{1... | collective-permute-start | bytes 737288 | tf_op jit(solution)/shard_map/ppermute | solution.py:505
  127.4 9.6 %collective-permute-start.22 = (bf16[320,128]{1,0:T(8,128)(2,1)S(1)}, bf16[320,128]{1,0:T(8,128)(2,1)}, u32[]{:S(2)}, u32[]{:S(2)}) collective-permute-start(bf16[320,128]{1,0:T(8,128)(2,1)S(1)} %get-tuple-element.45), channel_id=1, source_target_pairs={{0,8},{1,9},{2,10},{3,11},{4,12},{5,13},{6,14},{7,15},{8,0},{9,1},... | collective-permute-start | bytes 245768 | tf_op jit(solution)/shard_map/ppermute | solution.py:505
  129.2 10.0 %collective-permute-start.23 = (bf16[320,128]{1,0:T(8,128)(2,1)}, bf16[320,128]{1,0:T(8,128)(2,1)}, u32[]{:S(2)}, u32[]{:S(2)}) collective-permute-start(bf16[320,128]{1,0:T(8,128)(2,1)} %get-tuple-element.47), channel_id=1, source_target_pairs={{0,4},{1,5},{2,6},{3,7},{4,8},{5,9},{6,10},{7,11},{8,12},{9,13},{1... | collective-permute-start | bytes 245768 | tf_op jit(solution)/shard_map/ppermute | solution.py:505
  131.0 8.3 %collective-permute-start.24 = (bf16[320,128]{1,0:T(8,128)(2,1)}, bf16[320,128]{1,0:T(8,128)(2,1)}, u32[]{:S(2)}, u32[]{:S(2)}) collective-permute-start(bf16[320,128]{1,0:T(8,128)(2,1)} %get-tuple-element.46), channel_id=1, source_target_pairs={{0,12},{1,13},{2,14},{3,15},{4,0},{5,1},{6,2},{7,3},{8,4},{9,5},{1... | collective-permute-start | bytes 245768 | tf_op jit(solution)/shard_map/ppermute | solution.py:505
  135.2 9.7 %collective-permute-start.10 = (bf16[320,384]{1,0:T(8,128)(2,1)S(1)}, bf16[320,384]{1,0:T(8,128)(2,1)S(1)}, u32[]{:S(2)}, u32[]{:S(2)}) collective-permute-start(bf16[320,384]{1,0:T(8,128)(2,1)S(1)} %add_convert_fusion.1), channel_id=1, source_target_pairs={{0,2},{1,3},{2,0},{3,1},{4,6},{5,7},{6,4},{7,5},{8,10},{9,11},{10,... | collective-permute-start | bytes 737288 | tf_op jit(solution)/shard_map/ppermute | solution.py:505
  136.1 11.4 %collective-permute-start.11 = (bf16[320,384]{1,0:T(8,128)(2,1)S(1)}, bf16[320,384]{1,0:T(8,128)(2,1)S(1)}, u32[]{:S(2)}, u32[]{:S(2)}) collective-permute-start(bf16[320,384]{1,0:T(8,128)(2,1)S(1)} %add_convert_fusion.1), channel_id=1, source_target_pairs={{0,1},{1,2},{2,3},{3,0},{4,5},{5,6},{6,7},{7,4},{8,9},{9,10},{10,1... | collective-permute-start | bytes 737288 | tf_op jit(solution)/shard_map/ppermute | solution.py:505
  137.1 10.4 %collective-permute-start.12 = (bf16[320,384]{1,0:T(8,128)(2,1)S(1)}, bf16[320,384]{1,0:T(8,128)(2,1)S(1)}, u32[]{:S(2)}, u32[]{:S(2)}) collective-permute-start(bf16[320,384]{1,0:T(8,128)(2,1)S(1)} %add_convert_fusion.1), channel_id=1, source_target_pairs={{0,3},{1,0},{2,1},{3,2},{4,7},{5,4},{6,5},{7,6},{8,11},{9,8},{10,9... | collective-permute-start | bytes 737288 | tf_op jit(solution)/shard_map/ppermute | solution.py:505
  140.4 10.5 %collective-permute-start.25 = (bf16[320,128]{1,0:T(8,128)(2,1)S(1)}, bf16[320,128]{1,0:T(8,128)(2,1)S(1)}, u32[]{:S(2)}, u32[]{:S(2)}) collective-permute-start(bf16[320,128]{1,0:T(8,128)(2,1)S(1)} %fusion.4), channel_id=1, source_target_pairs={{0,32},{1,33},{2,34},{3,35},{4,36},{5,37},{6,38},{7,39},{8,40},{9,... | collective-permute-start | bytes 245768 | tf_op jit(solution)/shard_map/ppermute | solution.py:505
  142.3 8.9 %collective-permute-start.26 = (bf16[320,128]{1,0:T(8,128)(2,1)S(1)}, bf16[320,128]{1,0:T(8,128)(2,1)S(1)}, u32[]{:S(2)}, u32[]{:S(2)}) collective-permute-start(bf16[320,128]{1,0:T(8,128)(2,1)S(1)} %fusion.4), channel_id=1, source_target_pairs={{0,16},{1,17},{2,18},{3,19},{4,20},{5,21},{6,22},{7,23},{8,24},{9,... | collective-permute-start | bytes 245768 | tf_op jit(solution)/shard_map/ppermute | solution.py:505
  147.6 10.2 %collective-permute-start.14 = (bf16[320,384]{1,0:T(8,128)(2,1)S(1)}, bf16[320,384]{1,0:T(8,128)(2,1)S(1)}, u32[]{:S(2)}, u32[]{:S(2)}) collective-permute-start(bf16[320,384]{1,0:T(8,128)(2,1)S(1)} %add_convert_fusion), channel_id=1, source_target_pairs={{0,8},{1,9},{2,10},{3,11},{4,12},{5,13},{6,14},{7,15},{8,0},{9,1},... | collective-permute-start | bytes 737288 | tf_op jit(solution)/shard_map/ppermute | solution.py:505
  151.2 11.2 %collective-permute-start.28 = (bf16[320,128]{1,0:T(8,128)(2,1)S(1)}, bf16[320,128]{1,0:T(8,128)(2,1)S(1)}, u32[]{:S(2)}, u32[]{:S(2)}) collective-permute-start(bf16[320,128]{1,0:T(8,128)(2,1)S(1)} %add_convert_fusion.5), channel_id=1, source_target_pairs={{0,4},{1,5},{2,6},{3,7},{4,8},{5,9},{6,10},{7,11},{8,12},{9,13},{1... | collective-permute-start | bytes 245768 | tf_op jit(solution)/shard_map/ppermute | solution.py:505
  153.1 10.1 %collective-permute-start.29 = (bf16[320,128]{1,0:T(8,128)(2,1)S(1)}, bf16[320,128]{1,0:T(8,128)(2,1)S(1)}, u32[]{:S(2)}, u32[]{:S(2)}) collective-permute-start(bf16[320,128]{1,0:T(8,128)(2,1)S(1)} %add_convert_fusion.5), channel_id=1, source_target_pairs={{0,8},{1,9},{2,10},{3,11},{4,12},{5,13},{6,14},{7,15},{8,0},{9,1},... | collective-permute-start | bytes 245768 | tf_op jit(solution)/shard_map/ppermute | solution.py:505
  155.0 8.1 %collective-permute-start.30 = (bf16[320,128]{1,0:T(8,128)(2,1)S(1)}, bf16[320,128]{1,0:T(8,128)(2,1)S(1)}, u32[]{:S(2)}, u32[]{:S(2)}) collective-permute-start(bf16[320,128]{1,0:T(8,128)(2,1)S(1)} %add_convert_fusion.5), channel_id=1, source_target_pairs={{0,12},{1,13},{2,14},{3,15},{4,0},{5,1},{6,2},{7,3},{8,4},{9,5},{1... | collective-permute-start | bytes 245768 | tf_op jit(solution)/shard_map/ppermute | solution.py:505
  158.7 23.3 %collective-permute-start.16 = (bf16[1280,384]{1,0:T(8,128)(2,1)S(1)}, bf16[1280,384]{1,0:T(8,128)(2,1)S(1)}, u32[]{:S(2)}, u32[]{:S(2)}) collective-permute-start(bf16[1280,384]{1,0:T(8,128)(2,1)S(1)} %pad_maximum_fusion.refs_0_), channel_id=1, source_target_pairs={{0,16},{1,17},{2,18},{3,19},{4,20},{5,21},{6,22},{7,23},{8,24},{9,... | collective-permute-start | bytes 2949128 | tf_op jit(solution)/shard_map/ppermute | solution.py:505
  159.7 25.3 %collective-permute-start.17 = (bf16[1280,384]{1,0:T(8,128)(2,1)S(1)}, bf16[1280,384]{1,0:T(8,128)(2,1)S(1)}, u32[]{:S(2)}, u32[]{:S(2)}) collective-permute-start(bf16[1280,384]{1,0:T(8,128)(2,1)S(1)} %pad_maximum_fusion.refs_0_), channel_id=1, source_target_pairs={{0,32},{1,33},{2,34},{3,35},{4,36},{5,37},{6,38},{7,39},{8,40},{9,... | collective-permute-start | bytes 2949128 | tf_op jit(solution)/shard_map/ppermute | solution.py:505
  162.4 23.1 %collective-permute-start.18 = (bf16[1280,384]{1,0:T(8,128)(2,1)S(1)}, bf16[1280,384]{1,0:T(8,128)(2,1)S(1)}, u32[]{:S(2)}, u32[]{:S(2)}) collective-permute-start(bf16[1280,384]{1,0:T(8,128)(2,1)S(1)} %pad_maximum_fusion.refs_0_), channel_id=1, source_target_pairs={{0,48},{1,49},{2,50},{3,51},{4,52},{5,53},{6,54},{7,55},{8,56},{9,... | collective-permute-start | bytes 2949128 | tf_op jit(solution)/shard_map/ppermute | solution.py:505
  163.2 11.7 %collective-permute-start.31 = (bf16[1280,128]{1,0:T(8,128)(2,1)S(1)}, bf16[1280,128]{1,0:T(8,128)(2,1)S(1)}, u32[]{:S(2)}, u32[]{:S(2)}) collective-permute-start(bf16[1280,128]{1,0:T(8,128)(2,1)S(1)} %pad_maximum_fusion.1.refs_4_), channel_id=1, source_target_pairs={{0,1},{1,2},{2,3},{3,0},{4,5},{5,6},{6,7},{7,4},{8,9},{9,10},{10,1... | collective-permute-start | bytes 983048 | tf_op jit(solution)/shard_map/ppermute | solution.py:505
  163.8 14.7 %collective-permute-start.32 = (bf16[1280,128]{1,0:T(8,128)(2,1)S(1)}, bf16[1280,128]{1,0:T(8,128)(2,1)S(1)}, u32[]{:S(2)}, u32[]{:S(2)}) collective-permute-start(bf16[1280,128]{1,0:T(8,128)(2,1)S(1)} %pad_maximum_fusion.1.refs_4_), channel_id=1, source_target_pairs={{0,2},{1,3},{2,0},{3,1},{4,6},{5,7},{6,4},{7,5},{8,10},{9,11},{10,... | collective-permute-start | bytes 983048 | tf_op jit(solution)/shard_map/ppermute | solution.py:505
  (22 other events, 151.8 us)
where the time goes:
time: 192 us; the launch traced here: 191 us
  starting transfers between devices  58.4 us (30%)
  Pallas kernels  57.7 us (30%)
  waiting for transfers between devices  49.5 us (26%)
  local copies, waits for them, and re-layouts  17.3 us (9%)
  other arithmetic  7.17 us (4%)
    ppermute x30, waiting for transfers between devices, hop(): return lax.ppermute(values, ('section', 'peer'), pairs)  42.4 us
    ppermute x30, starting transfers between devices, hop(): return lax.ppermute(values, ('section', 'peer'), pairs)  37.4 us
    pallas_call x4, Pallas kernels, piece(): pl.pallas_call(kernel, grid_spec=pltpu.PrefetchScalarGridSpec(num_scalar_...  18.8 us
    unnamed x36, local copies, waits for them, and re-layouts  14.7 us
    pallas_call x1, Pallas kernels, prepare(): pl.pallas_call(kernel, grid_spec=pltpu.PrefetchScalarGridSpec(num_scalar_...  11.4 us
    all_to_all x1, starting transfers between devices, local(): lax.all_to_all(sent.reshape(rows, 8, 3 * k), ('section', 'peer'), 0, 0, t...  11.2 us
    pallas_call x1, Pallas kernels, front(): pl.pallas_call(kernel, grid=(steps,), in_specs=[pl.BlockSpec((lanes, rows...  10.2 us
    all_to_all x1, starting transfers between devices, local(): lax.all_to_all(out.reshape(rows, 8, 3 * k), ('section', 'peer'), 0, 0, ti...  9.06 us
  transfers between devices with their start and end apart: 36, of which 16 were waited for; matrix products, arithmetic and copies ran while one was open for 5% of the time, Pallas kernels for 17%

commit v1 on v0

--- a/solution.py
+++ b/solution.py
@@ -129,6 +129,10 @@
     return active, back, less, mix_first, mix_second
 
 
+def in_hbm(*arrays):
+    return [pltpu.with_memory_space_constraint(array, pltpu.HBM) for array in arrays]
+
+
 def joined(parts):
     return jnp.concatenate(list(parts), axis=1)
 
@@ -200,9 +204,9 @@
             pltpu.VMEM((total, k), f32),
             pltpu.VMEM((3, 8 * rows, k), f32),
         ],
-        compiler_params=pltpu.CompilerParams(vmem_limit_bytes=48 << 20),
+        compiler_params=pltpu.CompilerParams(vmem_limit_bytes=20 << 20),
         name="front",
-    )(x, c, down, up, gain)
+    )(*in_hbm(x, c, down, up, gain))
 
 
 def prepare(section, down, up, gain, down_other, up_other, gain_other):
@@ -210,7 +214,7 @@
     block = 1024
     steps = features // block
 
-    def kernel(s_ref, d, u, g, d2, u2, g2, w_ref, low_ref, high_ref):
+    def kernel(s_ref, d, u, g, d2, u2, g2, w_ref, low_out, high_out, low_ref, high_ref):
         step = pl.program_id(0)
         gains = jnp.concatenate([g[...], g2[...]] * 2, axis=0).T
         first = s_ref[0] == 0
@@ -244,6 +248,11 @@
             low_ref[...] += low
             high_ref[...] += high
 
+        @pl.when(step == steps - 1)
+        def _():
+            low_out[...] = low_ref[...].astype(bf16)
+            high_out[...] = high_ref[...].astype(bf16)
+
     two = pl.BlockSpec((2, block, k), lambda i, s: (0, i, 0))
     row = pl.BlockSpec((2, block), lambda i, s: (0, i))
     return pl.pallas_call(
@@ -257,15 +266,16 @@
                 pl.BlockSpec((2 * k, 6 * k), lambda i, s: (0, 0)),
                 pl.BlockSpec((k, 2 * k), lambda i, s: (0, 0)),
             ],
+            scratch_shapes=[pltpu.VMEM((2 * k, 6 * k), f32), pltpu.VMEM((k, 2 * k), f32)],
         ),
         out_shape=[
-            jax.ShapeDtypeStruct((features, 6 * k), bf16),
-            jax.ShapeDtypeStruct((2 * k, 6 * k), f32),
-            jax.ShapeDtypeStruct((k, 2 * k), f32),
+            pltpu.HBM((features, 6 * k), bf16),
+            pltpu.HBM((2 * k, 6 * k), bf16),
+            pltpu.HBM((k, 2 * k), bf16),
         ],
-        compiler_params=pltpu.CompilerParams(vmem_limit_bytes=48 << 20),
+        compiler_params=pltpu.CompilerParams(vmem_limit_bytes=24 << 20),
         name="prepare",
-    )(section[None], down, up, gain, down_other, up_other, gain_other)
+    )(section[None], *in_hbm(down, up, gain), down_other, up_other, gain_other)
 
 
 def turn(x, c):
@@ -283,19 +293,27 @@
         grid=(features // block,),
         in_specs=[spec, spec],
         out_specs=pl.BlockSpec((block, 2 * lanes * rows), lambda i: (i, 0)),
-        out_shape=jax.ShapeDtypeStruct((features, 2 * lanes * rows), bf16),
-        compiler_params=pltpu.CompilerParams(vmem_limit_bytes=48 << 20),
+        out_shape=pltpu.HBM((features, 2 * lanes * rows), bf16),
+        compiler_params=pltpu.CompilerParams(vmem_limit_bytes=12 << 20),
         name="turn",
-    )(x, c)
-
-
-def meet(received, first, second, gram_low, gram_high, lanes, features):
+    )(*in_hbm(x, c))
+
+
+def meet(section, received, first, second, gram_low, gram_high, lanes, features):
     total = first.shape[0]
     group = total // lanes
     slots = received.shape[1]
     k = received.shape[2] // 3
 
-    def kernel(rec, i0, i1, t0, t1, low_gram, high_gram, out, mix):
+    def kernel(mine, rec, columns, rows, far_low, far_high, out, own, oth, low, high, sems):
+        copies = [
+            pltpu.make_async_copy(far_low, low, sems.at[0]),
+            pltpu.make_async_copy(far_high, high, sems.at[1]),
+        ]
+        for copy in copies:
+            copy.start()
+        i0, i1 = columns[:, :1], columns[:, 1:]
+        t0, t1 = rows[:1, :], rows[1:, :]
         grid = lax.broadcasted_iota(jnp.int32, (total, slots), 1)
         turned = lax.broadcasted_iota(jnp.int32, (slots, total), 0)
 
@@ -305,61 +323,68 @@
         def place(base):
             return (turned == base).astype(f32).astype(bf16)
 
-        at_start = pick(i0[...])
-        at_start_next = pick(i0[...] + 1)
-        at_end = pick(i1[...] + 1)
+        at_start = pick(i0)
+        at_start_next = pick(i0 + 1)
+        at_end = pick(i1 + 1)
         lane = lax.broadcasted_iota(jnp.int32, (total, 1), 0) // group
-        norm_row = i0[...] - 2 * lane + 6
+        norm_row = i0 - 2 * lane + 6
         sums = dot(pick(norm_row), rec[0]) + dot(pick(norm_row + 1), rec[0])
         square_sum = jnp.concatenate(
             [sums[j * group : (j + 1) * group, j * k : (j + 1) * k] for j in range(lanes)], axis=0
         )[:, :1]
         proj, cot = [], []
         for s in range(2):
-            low = dot(at_start, rec[s])
-            high = dot(at_start_next, rec[s, :, :k])
+            near = dot(at_start, rec[s])
+            next_up = dot(at_start_next, rec[s, :, :k])
             tail = dot(at_end, rec[s, :, k:])
-            proj += [(low[:, :k], low[:, 2 * k :]), (low[:, k : 2 * k], high)]
+            proj += [(near[:, :k], near[:, 2 * k :]), (near[:, k : 2 * k], next_up)]
             cot += [tail[:, :k], tail[:, k:]]
+        for copy in copies:
+            copy.wait()
         active, back, less, mix_first, mix_second = row_stage(
-            proj, cot, square_sum, low_gram[...], high_gram[...], features
+            proj, cot, square_sum, low[...], high[...], features
         )
-        to_start = place(t0[...])
-        to_start_next = place(t0[...] + 1)
-        to_end = place(t1[...] + 1)
+        to_start = place(t0)
+        to_start_next = place(t0 + 1)
+        to_end = place(t1 + 1)
         for s in range(2):
             l0, l1 = 2 * s, 2 * s + 1
             out[s] = dot(to_start, joined([back[l0], back[l1], less[l0]])).astype(bf16)
-            high = dot(to_start_next, less[l1])
+            weighted = dot(to_start_next, less[l1])
             tail = dot(to_end, joined([active[l0], active[l1]]))
-            out[s] += joined([high, tail]).astype(bf16)
-        for s, table in enumerate((mix_first, mix_second)):
-            for i, row in enumerate(table):
-                mix[s, i * k : (i + 1) * k, :] = joined(row).astype(bf16)
-
-    return pl.pallas_call(
-        kernel,
-        out_shape=[
-            jax.ShapeDtypeStruct(received.shape, bf16),
-            jax.ShapeDtypeStruct((2, 6 * k, 4 * k), bf16),
+            out[s] += joined([weighted, tail]).astype(bf16)
+        first_section = mine[0] == 0
+        for i, (one, two) in enumerate(zip(mix_first, mix_second)):
+            at = slice(i * k, (i + 1) * k)
+            one, two = joined(one), joined(two)
+            own[at, :] = jnp.where(first_section, one, two).astype(bf16)
+            oth[at, :] = jnp.where(first_section, two, one).astype(bf16)
+
+    columns = jnp.stack([first, second], axis=1)
+    rows = jnp.stack([first, second])
+    local_ref = pl.BlockSpec(memory_space=pltpu.VMEM)
+    far_ref = pl.BlockSpec(memory_space=pl.ANY)
+    mix = jax.ShapeDtypeStruct((6 * k, 4 * k), bf16)
+    return pl.pallas_call(
+        kernel,
+        in_specs=[pl.BlockSpec(memory_space=pltpu.SMEM)] + [local_ref] * 3 + [far_ref] * 2,
+        out_shape=[jax.ShapeDtypeStruct(received.shape, bf16), mix, mix],
+        scratch_shapes=[
+            pltpu.VMEM(gram_low.shape, bf16),
+            pltpu.VMEM(gram_high.shape, bf16),
+            pltpu.SemaphoreType.DMA((2,)),
         ],
-        compiler_params=pltpu.CompilerParams(vmem_limit_bytes=48 << 20),
+        compiler_params=pltpu.CompilerParams(vmem_limit_bytes=16 << 20),
         name="meet",
-    )(
-        received,
-        first[:, None],
-        second[:, None],
-        first[None, :],
-        second[None, :],
-        gram_low,
-        gram_high,
-    )
+    )(section[None], received, columns, rows, *in_hbm(gram_low, gram_high))
 
 
 def unpack(returned, mix_own, mix_other, lanes):
     rows, k = returned.shape[0] // 8, returned.shape[1] // 3
 
-    def kernel(ret, own, oth, xs, cs, mix, wide):
+    def kernel(ret, own, far, xs, cs, mix, wide, oth, sem):
+        copy = pltpu.make_async_copy(far, oth, sem)
+        copy.start()
         for t in range(3):
             wide[t] = ret[:, t * k : (t + 1) * k].astype(f32)
         for j in range(lanes):
@@ -368,129 +393,169 @@
             high = [wide[t, pl.ds(2 * j + 1, rows, stride=8), :].astype(bf16) for t in range(3)]
             xs[at, :] = joined(low + high[:1])
             cs[at, :] = joined(high[1:])
+        copy.wait()
         mix[...] = (own[...].astype(f32) + oth[...].astype(f32)).astype(bf16)
 
-    return pl.pallas_call(
-        kernel,
+    local_ref = pl.BlockSpec(memory_space=pltpu.VMEM)
+    shapes = [(lanes * rows, 4 * k), (lanes * rows, 2 * k), mix_own.shape]
+    return pl.pallas_call(
+        kernel,
+        in_specs=[local_ref, local_ref, pl.BlockSpec(memory_space=pl.ANY)],
+        out_shape=[jax.ShapeDtypeStruct(shape, bf16) for shape in shapes],
+        scratch_shapes=[
+            pltpu.VMEM((3, 8 * rows, k), f32),
+            pltpu.VMEM(mix_own.shape, bf16),
+            pltpu.SemaphoreType.DMA,
+        ],
+        compiler_params=pltpu.CompilerParams(vmem_limit_bytes=8 << 20),
+        name="unpack",
+    )(returned, mix_own, *in_hbm(mix_other))
+
+
+def piece(at, size, turned, weights, xs, cs, mix):
+    both = turned.shape[1]
+    k = cs.shape[1] // 2
+    total = both // 2
+    parts = 4
+    chunk = size // parts
+
+    def kernel(at_ref, t_ref, w_ref, xs_ref, cs_ref, mix_ref, major, minor, t_buf, w_buf, sems):
+        copies = []
+        for i in range(parts):
+            rows = pl.ds(pl.multiple_of(at_ref[0] + i * chunk, 16), chunk)
+            copies.append(
+                [
+                    pltpu.make_async_copy(t_ref.at[rows, :], t_buf.at[i], sems.at[i, 0]),
+                    pltpu.make_async_copy(w_ref.at[rows, :], w_buf.at[i], sems.at[i, 1]),
+                ]
+            )
+        for copy in copies[0] + copies[1]:
+            copy.start()
+        for i in range(parts):
+            rows = slice(i * chunk, (i + 1) * chunk)
+            for copy in copies[i]:
+                copy.wait()
+            if i + 2 < parts:
+                for copy in copies[i + 2]:
+                    copy.start()
+            value = dot(t_buf[i, :, :total], xs_ref[...]) + dot(w_buf[i], mix_ref[...])
+            last = dot(t_buf[i, :, total:], cs_ref[...])
+            major[rows, : 2 * k] = value[:, : 2 * k].astype(bf16)
+            major[rows, 2 * k :] = (value[:, 2 * k : 3 * k] + last[:, :k]).astype(bf16)
+            minor[rows, :] = (value[:, 3 * k :] + last[:, k:]).astype(bf16)
+
+    local_ref = pl.BlockSpec(memory_space=pltpu.VMEM)
+    far_ref = pl.BlockSpec(memory_space=pl.ANY)
+    return pl.pallas_call(
+        kernel,
+        in_specs=[pl.BlockSpec(memory_space=pltpu.SMEM)] + [far_ref] * 2 + [local_ref] * 3,
+        out_specs=[local_ref] * 2,
         out_shape=[
-            jax.ShapeDtypeStruct((lanes * rows, 4 * k), bf16),
-            jax.ShapeDtypeStruct((lanes * rows, 2 * k), bf16),
-            jax.ShapeDtypeStruct(mix_own.shape, bf16),
+            jax.ShapeDtypeStruct((size, 3 * k), bf16),
+            jax.ShapeDtypeStruct((size, k), bf16),
         ],
-        scratch_shapes=[pltpu.VMEM((3, 8 * rows, k), f32)],
-        compiler_params=pltpu.CompilerParams(vmem_limit_bytes=48 << 20),
-        name="unpack",
-    )(returned, mix_own, mix_other)
-
-
-def piece(at, turned, weights, gain, xs, cs, mix, minor):
-    features, both = turned.shape
-    k = cs.shape[1] // 2
-    quarter = features // 4
-    block = 640
-    steps = quarter // block
-    total = both // 2
-    fresh = minor is None
-
-    def kernel(at_ref, t_ref, w_ref, g_ref, xs_ref, cs_ref, mix_ref, *refs):
-        out, last_out = refs[-2:]
-        value = dot(t_ref[:, :total], xs_ref[...]) + dot(w_ref[...], mix_ref[...])
-        last = dot(t_ref[:, total:], cs_ref[...])
-        gains = jnp.concatenate([g_ref[...]] * 4, axis=0).T
-        out[:, :k] = (value[:, :k] * gains[:, :1]).astype(bf16)
-        out[:, k : 2 * k] = (value[:, k : 2 * k] * gains[:, 1:2]).astype(bf16)
-        out[:, 2 * k :] = (value[:, 2 * k : 3 * k] + last[:, :k]).astype(bf16)
-        last_out[0] = (value[:, 3 * k :] + last[:, k:]).astype(bf16)
-
-    in_specs = [
-        pl.BlockSpec((block, both), lambda i, at: (at[0] * steps + i, 0)),
-        pl.BlockSpec((block, 6 * k), lambda i, at: (at[0] * steps + i, 0)),
-        pl.BlockSpec((2, block), lambda i, at: (0, at[0] * steps + i)),
-        pl.BlockSpec((total, 4 * k), lambda i, at: (0, 0)),
-        pl.BlockSpec((total, 2 * k), lambda i, at: (0, 0)),
-        pl.BlockSpec((6 * k, 4 * k), lambda i, at: (0, 0)),
-    ]
-    operands = [at[None], turned, weights, gain, xs, cs, mix]
-    if not fresh:
-        in_specs.append(pl.BlockSpec(memory_space=pl.ANY))
-        operands.append(minor)
-    return pl.pallas_call(
-        kernel,
-        grid_spec=pltpu.PrefetchScalarGridSpec(
-            num_scalar_prefetch=1,
-            grid=(steps,),
-            in_specs=in_specs,
-            out_specs=[
-                pl.BlockSpec((block, 3 * k), lambda i, at: (i, 0)),
-                pl.BlockSpec((1, block, k), lambda i, at: (at[0], i, 0)),
-            ],
-        ),
-        out_shape=[
-            jax.ShapeDtypeStruct((quarter, 3 * k), bf16),
-            jax.ShapeDtypeStruct((4, quarter, k), bf16),
+        scratch_shapes=[
+            pltpu.VMEM((parts, chunk, both), bf16),
+            pltpu.VMEM((parts, chunk, 6 * k), bf16),
+            pltpu.SemaphoreType.DMA((parts, 2)),
         ],
-        input_output_aliases={} if fresh else {7: 1},
-        compiler_params=pltpu.CompilerParams(vmem_limit_bytes=48 << 20),
+        compiler_params=pltpu.CompilerParams(vmem_limit_bytes=16 << 20),
         name="piece",
-    )(*operands)
+    )(at[None], *in_hbm(turned, weights), xs, cs, mix)
+
+
+def squares(block):
+    rows, width = block.shape
+
+    def kernel(ref, out):
+        v = ref[...].astype(f32)
+        out[...] = jnp.sum((v * v).reshape(4, rows // 32, 8, width), axis=1)
+
+    return pl.pallas_call(
+        kernel,
+        out_shape=jax.ShapeDtypeStruct((4, 8, width), f32),
+        compiler_params=pltpu.CompilerParams(vmem_limit_bytes=8 << 20),
+        name="squares",
+    )(block)
 
 
 def finish(starts, major, minor, features, k):
     quarter = features // 4
     part = quarter // 4
+    late = 2
+    early = [i for i in range(4) if i != late]
+    blocks = [*major, *minor]
+    known = [squares(major[i]) for i in early] + [squares(minor[i]) for i in early]
 
     def kernel(at, *refs):
-        ins, (down, up) = refs[:8], refs[8:]
+        ins, known, (down, up) = refs[:8], refs[8:14], refs[14:]
         group = pl.program_id(0)
 
-        def run(blocks, out, which):
-            total = jnp.zeros((8, k), f32)
-            for ref in blocks:
-                v = ref[...].astype(f32)
-                total = total + jnp.sum((v * v).reshape(quarter // 8, 8, k), axis=0)
+        def run(which, out):
+            sums = [None] * 4
+            for i in range(4):
+                if i == late:
+                    v = ins[which * 4 + i][...].astype(f32)
+                    v = jnp.sum((v * v).reshape(4, part // 8, 8, k), axis=1)
+                else:
+                    v = known[which * 3 + early.index(i)][...]
+                sums[i] = ring_sum(v[0], v[2], v[1], v[3])
+            total = ring_sum(sums[0], sums[2], sums[1], sums[3])
             mean = jnp.sum(total) * (1.0 / (features * k))
             scale = lax.rsqrt(jnp.full((1, k), mean, f32) + step_eps)
-            for i, ref in enumerate(blocks):
+            for i in range(4):
                 for j in range(4):
                     row = pl.multiple_of(at[which, i, j], 16)
-                    v = ref[j * part : (j + 1) * part, :].astype(f32)
+                    v = ins[which * 4 + i][j * part : (j + 1) * part, :].astype(f32)
                     out[0, pl.ds(row, part), :] = (v * scale).astype(bf16)
 
         @pl.when(group < 2)
         def _():
-            run(ins[:4], down, 0)
+            run(0, down)
 
         @pl.when(group == 2)
         def _():
-            run(ins[:4], up, 0)
+            run(0, up)
 
         @pl.when(group == 3)
         def _():
-            run(ins[4:], up, 1)
+            run(1, up)
+
+    def specs(shape, columns):
+        zeros = (0,) * (len(shape) - 1)
+        return pl.BlockSpec(shape, lambda g, at: (*zeros, columns(g)))
+
+    def clipped(g):
+        return jnp.minimum(g, 2)
+
+    def fixed(g):
+        return 0
 
     return pl.pallas_call(
         kernel,
         grid_spec=pltpu.PrefetchScalarGridSpec(
             num_scalar_prefetch=1,
             grid=(4,),
-            in_specs=[pl.BlockSpec((quarter, k), lambda g, at: (0, jnp.minimum(g, 2)))] * 4
-            + [pl.BlockSpec((quarter, k), lambda g, at: (0, 0))] * 4,
+            in_specs=[specs((quarter, k), clipped)] * 4
+            + [specs((quarter, k), fixed)] * 4
+            + [specs((4, 8, k), clipped)] * 3
+            + [specs((4, 8, k), fixed)] * 3,
             out_specs=[
                 pl.BlockSpec((1, features, k), lambda g, at: (jnp.minimum(g, 1), 0, 0)),
                 pl.BlockSpec((1, features, k), lambda g, at: (jnp.maximum(g - 2, 0), 0, 0)),
             ],
         ),
         out_shape=[jax.ShapeDtypeStruct((2, features, k), bf16)] * 2,
-        compiler_params=pltpu.CompilerParams(vmem_limit_bytes=48 << 20),
+        compiler_params=pltpu.CompilerParams(vmem_limit_bytes=16 << 20),
         name="finish",
-    )(starts, *major, *minor)
+    )(starts, *blocks, *known)
 
 
 def coords(peer):
     return peer // 16, (peer // 4) % 4, peer % 4
 
 
-MAJOR = ((0, 1, 2), (1, 0, 2))
+MAJOR = ((0, 1, 2), (1, 2, 0))
 MINOR = ((2, 1, 0), (2, 0, 1))
 
 
@@ -505,18 +570,23 @@
     return lax.ppermute(values, ("section", "peer"), pairs)
 
 
-def summed(parts, order, at):
+def ring_sum(own, two, one, three):
+    return (own + two) + (one + three)
+
+
+def summed(parts, order, at, gains=None):
     step = parts[0].shape[0] // 4
 
     def cut(by):
-        start = ((at + by) % 4) * step
+        start = ((at[1] + by) % 4) * step
         return sum(lax.dynamic_slice_in_dim(p, start, step, axis=0).astype(f32) for p in parts)
 
     arrived = [hop(cut(by).astype(bf16), order, 1, by) for by in (2, 1, 3)]
     own = cut(0) + sum(part.astype(f32) for part in arrived)
     own = lax.optimization_barrier(own.astype(bf16))
     two, one, three = [hop(own, order, 2, by).astype(f32) for by in (2, 1, 3)]
-    return ((own.astype(f32) + two) + (one + three)).astype(bf16)
+    total = ring_sum(own.astype(f32), two, one, three)
+    return (total if gains is None else total * gains).astype(bf16)
 
 
 def gathered(block, order):
@@ -548,41 +618,48 @@
     total = holders.shape[1]
     lane_of = jnp.arange(total, dtype=jnp.int32) // (total // lanes)
     base = holders * 8 + 2 * lane_of
-    out, mix = meet(
-        received, base[0], base[1], gram_low, gram_high, lanes, features
+    out, mix_own, mix_leaving = meet(
+        section, received, base[0], base[1], gram_low, gram_high, lanes, features
     )
-    mix_own = lax.dynamic_index_in_dim(mix, section, 0, keepdims=False)
-    mix_other = lax.ppermute(
-        lax.dynamic_index_in_dim(mix, 1 - section, 0, keepdims=False), "section", swap
-    )
+    mix_other = lax.ppermute(mix_leaving, "section", swap)
     returned = lax.all_to_all(
         out.reshape(rows, 8, 3 * k), ("section", "peer"), 0, 0, tiled=True
     ).reshape(8 * rows, 3 * k)
-    turned = turn(*lax.optimization_barrier((x, c, mix))[:2])
+    turned = turn(*lax.optimization_barrier((x, c, mix_own))[:2])
     xs, cs, mix = unpack(returned, mix_own, mix_other, lanes)
 
     where = jnp.stack(coords(peer))
-    at_major = [jnp.where(is_first, where[MAJOR[0][i]], where[MAJOR[1][i]]) for i in range(3)]
-    at_minor = [jnp.where(is_first, where[MINOR[0][i]], where[MINOR[1][i]]) for i in range(3)]
-
-    major, minor = [], None
+    at_major, at_minor = (
+        [jnp.where(is_first, where[order[0][i]], where[order[1][i]]) for i in range(3)]
+        for order in (MAJOR, MINOR)
+    )
+    quarter = features // 4
+    major, minor = [], []
     for by in (2, 1, 3, 0):
-        index = ((at_major[0] + by) % 4).astype(jnp.int32)
-        part, minor = piece(index, turned, weights, gain, xs, cs, mix, minor)
+        index = ((at_major[0] + by) % 4) * quarter
+        part, rest = piece(index.astype(jnp.int32), quarter, turned, weights, xs, cs, mix)
         major.append(hop(part, MAJOR, 0, by) if by else part)
+        minor.append(rest)
 
     def pick_minor(by):
-        return lax.dynamic_index_in_dim(minor, (at_minor[0] + by) % 4, 0, keepdims=False)
-
+        ahead = (at_minor[0] + by - at_major[0]) % 4
+        return lax.select_n(
+            jnp.broadcast_to(ahead, minor[0].shape), minor[3], minor[1], minor[0], minor[2]
+        )
+
+    step = features // 16
+    row = at_major[0] * quarter + at_major[1] * step
+    gains = lax.dynamic_slice_in_dim(gain, row, step, axis=1).T
+    gains = joined([jnp.broadcast_to(gains[:, l : l + 1], (step, k)) for l in range(2)])
+    gains = joined([gains, jnp.ones((step, k), f32)])
     minor = [hop(pick_minor(by), MINOR, 0, by) for by in (2, 1, 3)] + [pick_minor(0)]
-    minor = gathered(summed(minor, MINOR, at_minor[1]), MINOR)
-    major = gathered(summed(major, MAJOR, at_major[1]), MAJOR)
+    minor = gathered(summed(minor, MINOR, at_minor), MINOR)
+    major = gathered(summed(major, MAJOR, at_major, gains), MAJOR)
 
     back = jnp.arange(4, dtype=jnp.int32)
     starts = jnp.stack(
         [
-            ((at[0] - back) % 4)[:, None] * (features // 4)
-            + ((at[1] - back) % 4)[None, :] * (features // 16)
+            ((at[0] - back) % 4)[:, None] * quarter + ((at[1] - back) % 4)[None, :] * step
             for at in (at_major, at_minor)
         ]
     ).astype(jnp.int32)

time: 192 us -> 177 us (0.922)
  local copies, waits for them, and re-layouts: 17.3 us -> 1.98 us
  waiting for transfers between devices: 49.5 us -> 40.7 us
  Pallas kernels: 57.7 us -> 66.3 us
    unnamed x36 -> x6, local copies, waits for them, and re-layouts: 14.7 us -> 0.89 us
    ppermute x30, waiting for transfers between devices: 42.4 us -> 30 us  [hop(): return lax.ppermute(values, ('section', 'peer'), pairs)]
    pallas_call x6 -> x12, Pallas kernels: 23.2 us -> 30.2 us  [the longest x4 23.3 us: piece(): pl.pallas_call(kernel, in_specs=[pl.BlockSpec(memory_space=pltpu.SMEM)] +...]
    ppermute x30, starting transfers between devices: 37.4 us -> 41.2 us  [hop(): return lax.ppermute(values, ('section', 'peer'), pairs)]
    all_to_all x1, starting transfers between devices: 9.06 us -> 6.07 us  [local(): lax.all_to_all(out.reshape(rows, 8, 3 * k), ('section', 'peer'), 0, 0, ti...]
    all_to_all x1, waiting for transfers between devices: 1.04 us -> 3.85 us  [local(): lax.all_to_all(sent.reshape(rows, 8, 3 * k), ('section', 'peer'), 0, 0, t...]
  transfers between devices with their start and end apart: 36 -> 36, of which waited for: 16 -> 12; matrix products, arithmetic and copies ran while one was open for 5% -> 5% of each run, Pallas kernels for 17% -> 28%
where the time goes in v1:
time: 177 us; the launch traced here: 176 us
  Pallas kernels  66.3 us (37%)
  starting transfers between devices  59.2 us (33%)
  waiting for transfers between devices  40.7 us (23%)
  other arithmetic  7.23 us (4%)
  local copies, waits for them, and re-layouts  1.98 us (1%)
    ppermute x30, starting transfers between devices, hop(): return lax.ppermute(values, ('section', 'peer'), pairs)  41.2 us
    ppermute x30, waiting for transfers between devices, hop(): return lax.ppermute(values, ('section', 'peer'), pairs)  30 us
    pallas_call x4, Pallas kernels, piece(): pl.pallas_call(kernel, in_specs=[pl.BlockSpec(memory_space=pltpu.SMEM)] +...  23.3 us
    pallas_call x1, Pallas kernels, prepare(): pl.pallas_call(kernel, grid_spec=pltpu.PrefetchScalarGridSpec(num_scalar_...  11.4 us
    all_to_all x1, starting transfers between devices, local(): lax.all_to_all(sent.reshape(rows, 8, 3 * k), ('section', 'peer'), 0, 0, t...  11.2 us
    pallas_call x1, Pallas kernels, front(): pl.pallas_call(kernel, grid=(steps,), in_specs=[pl.BlockSpec((lanes, rows...  10.5 us
    pallas_call x1, Pallas kernels, turn(): pl.pallas_call(kernel, grid=(features // block,), in_specs=[spec, spec],...  8.99 us
    all_to_all x1, waiting for transfers between devices, local(): lax.all_to_all(out.reshape(rows, 8, 3 * k), ('section', 'peer'), 0, 0, ti...  6.83 us
  transfers between devices with their start and end apart: 36, of which 12 were waited for; matrix products, arithmetic and copies ran while one was open for 5% of the time, Pallas kernels for 28%

profile of v1, /device:TPU:0, one launch (start us, length us, event | category | flops | bytes accessed | tf_op | source)
XLA Modules:
  0.0 176.4 jit_solution(11511049413083582204)
XLA Ops:
  1.3 10.5 %front.1 = bf16[1024,384]{1,0:T(8,128)(2,1)} custom-call(bf16[3,128,5120]{2,1,0:T(8,128)(2,1)} %bitcast.26, bf16[3,128,5120]{2,1,0:T(8,128)(2,1)} %bitcast.28, bf16[2,5120,128]{2,1,0:T(8,128)(2,1)} %bitcast.31, bf16[2,5120,128]{2,1,0:T(8,128)(2,1)} %bitcast.34, f32[2,5120]{1,0:T(2,128)} %bitcast.37), custom_call_target="tpu_custom_call" | custom-call | tf_op jit(solution)/shard_map/front/pallas_call | solution.py:190
  11.9 11.2 %all-to-all-start = ((bf16[128,8,384]{2,1,0:T(8,128)(2,1)}), bf16[128,8,384]{2,1,0:T(8,128)(2,1)S(1)}, u32[]{:S(2)}, u32[]{:S(2)}) async-start(bf16[128,8,384]{2,1,0:T(8,128)(2,1)} %bitcast.7), calls=%async_computation | async-start | bytes 1572864 | tf_op jit(solution)/shard_map/all_to_all | solution.py:611
  23.6 11.4 %prepare.1 = (bf16[5120,768]{1,0:T(8,128)(2,1)}, bf16[256,768]{1,0:T(8,128)(2,1)}, bf16[128,256]{1,0:T(8,128)(2,1)}) custom-call(s32[1]{0:T(128)} %bitcast.3.s_ref.mine, bf16[2,5120,128]{2,1,0:T(8,128)(2,1)} %bitcast.32, bf16[2,5120,128]{2,1,0:T(8,128)(2,1)} %bitcast.35, f32[2,5120]{1,0:T(2,128)} %bitcast.38, ...), custom_call_target="tpu_custom_call" | custom-call | tf_op jit(solution)/shard_map/prepare/pallas_call | solution.py:258
  35.1 3.8 %all-to-all-done = bf16[128,8,384]{2,1,0:T(8,128)(2,1)S(1)} async-done(((bf16[128,8,384]{2,1,0:T(8,128)(2,1)}), bf16[128,8,384]{2,1,0:T(8,128)(2,1)S(1)}, u32[]{:S(2)}, u32[]{:S(2)}) %all-to-all-start) | async-done | bytes 786464 | tf_op jit(solution)/shard_map/all_to_all | solution.py:611
  38.9 5.0 %meet.1 = (bf16[2,512,384]{2,1,0:T(8,128)(2,1)}, bf16[768,512]{1,0:T(8,128)(2,1)S(1)}, bf16[768,512]{1,0:T(8,128)(2,1)}) custom-call(s32[1]{0:T(128)} %bitcast.3.s_ref.mine, bf16[2,512,384]{2,1,0:T(8,128)(2,1)S(1)} %bitcast.24, s32[144,2]{1,0:T(8,128)S(1)} %copy.12.columns, s32[2,144]{1,0:T(2,128)S(1)} %multiply_add_fusion.rows, ...), custom_call_target="tpu_custom_call" | custom-call | tf_op jit(solution)/shard_map/meet/pallas_call | solution.py:368
  44.1 6.1 %all-to-all-start.1 = ((bf16[128,8,384]{2,1,0:T(8,128)(2,1)}), bf16[128,8,384]{2,1,0:T(8,128)(2,1)S(1)}, u32[]{:S(2)}, u32[]{:S(2)}) async-start(bf16[128,8,384]{2,1,0:T(8,128)(2,1)} %bitcast.11), calls=%async_computation.1 | async-start | bytes 1572864 | tf_op jit(solution)/shard_map/all_to_all | solution.py:625
  50.2 9.0 %turn.1.t_ref = bf16[5120,768]{1,0:T(8,128)(2,1)} custom-call(bf16[3,128,5120]{2,1,0:T(8,128)(2,1)} %bitcast.27, bf16[3,128,5120]{2,1,0:T(8,128)(2,1)} %bitcast.29), custom_call_target="tpu_custom_call" | custom-call | tf_op jit(solution)/shard_map/turn/pallas_call | solution.py:291
  59.2 6.8 %all-to-all-done.1 = bf16[128,8,384]{2,1,0:T(8,128)(2,1)S(1)} async-done(((bf16[128,8,384]{2,1,0:T(8,128)(2,1)}), bf16[128,8,384]{2,1,0:T(8,128)(2,1)S(1)}, u32[]{:S(2)}, u32[]{:S(2)}) %all-to-all-start.1) | async-done | bytes 786464 | tf_op jit(solution)/shard_map/all_to_all | solution.py:625
  68.2 6.1 %piece.4 = (bf16[1280,384]{1,0:T(8,128)(2,1)}, bf16[1280,128]{1,0:T(8,128)(2,1)S(1)}) custom-call(s32[1]{0:T(128)} %bitcast.at_ref, bf16[5120,768]{1,0:T(8,128)(2,1)} %turn.1.t_ref, bf16[5120,768]{1,0:T(8,128)(2,1)} %get-tuple-element.28.w_ref, bf16[384,512]{1,0:T(8,128)(2,1)S(1)} %get-tuple-element.31.xs_ref, ...), custom_call_target="tpu_custom_call" | custom-call | tf_op jit(solution)/shard_map/piece/pallas_call | solution.py:449
  75.8 6.0 %piece.5 = (bf16[1280,384]{1,0:T(8,128)(2,1)}, bf16[1280,128]{1,0:T(8,128)(2,1)S(1)}) custom-call(s32[1]{0:T(128)} %bitcast.13.at_ref, bf16[5120,768]{1,0:T(8,128)(2,1)} %turn.1.t_ref, bf16[5120,768]{1,0:T(8,128)(2,1)} %get-tuple-element.28.w_ref, bf16[384,512]{1,0:T(8,128)(2,1)S(1)} %get-tuple-element.31.xs_ref, ...), custom_call_target="tpu_custom_call" | custom-call | tf_op jit(solution)/shard_map/piece/pallas_call | solution.py:449
  81.8 6.0 %piece.6 = (bf16[1280,384]{1,0:T(8,128)(2,1)}, bf16[1280,128]{1,0:T(8,128)(2,1)S(1)}) custom-call(s32[1]{0:T(128)} %bitcast.14.at_ref, bf16[5120,768]{1,0:T(8,128)(2,1)} %turn.1.t_ref, bf16[5120,768]{1,0:T(8,128)(2,1)} %get-tuple-element.28.w_ref, bf16[384,512]{1,0:T(8,128)(2,1)S(1)} %get-tuple-element.31.xs_ref, ...), custom_call_target="tpu_custom_call" | custom-call | tf_op jit(solution)/shard_map/piece/pallas_call | solution.py:449
  88.8 2.4 %collective-permute-start.6 = (bf16[1280,384]{1,0:T(8,128)(2,1)}, bf16[1280,384]{1,0:T(8,128)(2,1)}, u32[]{:S(2)}, u32[]{:S(2)}) collective-permute-start(bf16[1280,384]{1,0:T(8,128)(2,1)} %get-tuple-element.36), channel_id=1, source_target_pairs={{0,48},{1,49},{2,50},{3,51},{4,52},{5,53},{6,54},{7,55},{8,56},{9,... | collective-permute-start | bytes 2949128 | tf_op jit(solution)/shard_map/ppermute | solution.py:570
  91.2 5.1 %piece.7 = (bf16[1280,384]{1,0:T(8,128)(2,1)S(1)}, bf16[1280,128]{1,0:T(8,128)(2,1)S(1)}) custom-call(s32[1]{0:T(128)} %bitcast.15.at_ref, bf16[5120,768]{1,0:T(8,128)(2,1)} %turn.1.t_ref, bf16[5120,768]{1,0:T(8,128)(2,1)} %get-tuple-element.28.w_ref, bf16[384,512]{1,0:T(8,128)(2,1)S(1)} %get-tuple-element.31.xs_ref, ...), custom_call_target="tpu_custom_call" | custom-call | tf_op jit(solution)/shard_map/piece/pallas_call | solution.py:449
  99.0 2.1 %collective-permute-start.21 = (bf16[1280,128]{1,0:T(8,128)(2,1)S(1)}, bf16[1280,128]{1,0:T(8,128)(2,1)S(1)}, u32[]{:S(2)}, u32[]{:S(2)}) collective-permute-start(bf16[1280,128]{1,0:T(8,128)(2,1)S(1)} %get-tuple-element.54), channel_id=1, source_target_pairs={{0,3},{1,0},{2,1},{3,2},{4,7},{5,4},{6,5},{7,6},{8,11},{9,8},{10,9... | collective-permute-start | bytes 983048 | tf_op jit(solution)/shard_map/ppermute | solution.py:570
  101.2 2.4 %collective-permute-done.5 = bf16[1280,384]{1,0:T(8,128)(2,1)} collective-permute-done((bf16[1280,384]{1,0:T(8,128)(2,1)}, bf16[1280,384]{1,0:T(8,128)(2,1)}, u32[]{:S(2)}, u32[]{:S(2)}) %collective-permute-start.5) | collective-permute-done | bytes 983072 | tf_op jit(solution)/shard_map/ppermute | solution.py:570
  103.6 2.8 %add_convert_fusion.3 = (bf16[320,384]{1,0:T(8,128)(2,1)}, bf16[320,384]{1,0:T(8,128)(2,1)}, bf16[320,384]{1,0:T(8,128)(2,1)}) fusion(bf16[1280,384]{1,0:T(8,128)(2,1)S(1)} %get-tuple-element.37, s32[]{:T(128)S(6)} %select_n.294, bf16[1280,384]{1,0:T(8,128)(2,1)} %collective-permute-done.6, bf16[1280,384]{1,0:T(8,128)(2,1)} %collective-permute-done.5, ...), kind=kLoop, calls=%fused_computation.6 | loop fusion | flops 2949120 | bytes 3686412 | tf_op jit(solution)/shard_map/convert_element_type | solution.py:584
  106.4 1.7 collective-permute-start.7
  109.3 2.1 %collective-permute-start.9 = (bf16[320,384]{1,0:T(8,128)(2,1)}, bf16[320,384]{1,0:T(8,128)(2,1)S(1)}, u32[]{:S(2)}, u32[]{:S(2)}) collective-permute-start(bf16[320,384]{1,0:T(8,128)(2,1)} %get-tuple-element.47), channel_id=1, source_target_pairs={{0,12},{1,13},{2,14},{3,15},{4,0},{5,1},{6,2},{7,3},{8,4},{9,5},{1... | collective-permute-start | bytes 737288 | tf_op jit(solution)/shard_map/ppermute | solution.py:570
  112.1 3.7 %collective-permute-done.20 = bf16[1280,128]{1,0:T(8,128)(2,1)S(1)} collective-permute-done((bf16[1280,128]{1,0:T(8,128)(2,1)S(1)}, bf16[1280,128]{1,0:T(8,128)(2,1)S(1)}, u32[]{:S(2)}, u32[]{:S(2)}) %collective-permute-start.20) | collective-permute-done | bytes 327712 | tf_op jit(solution)/shard_map/ppermute | solution.py:570
  118.2 3.1 %collective-permute-start.24 = (bf16[320,128]{1,0:T(8,128)(2,1)S(1)}, bf16[320,128]{1,0:T(8,128)(2,1)}, u32[]{:S(2)}, u32[]{:S(2)}) collective-permute-start(bf16[320,128]{1,0:T(8,128)(2,1)S(1)} %get-tuple-element.50), channel_id=1, source_target_pairs={{0,12},{1,13},{2,14},{3,15},{4,0},{5,1},{6,2},{7,3},{8,4},{9,5},{1... | collective-permute-start | bytes 245768 | tf_op jit(solution)/shard_map/ppermute | solution.py:570
  121.3 1.6 add_convert_fusion
  125.2 2.3 %collective-permute-start.12 = (bf16[320,384]{1,0:T(8,128)(2,1)S(1)}, bf16[320,384]{1,0:T(8,128)(2,1)S(1)}, u32[]{:S(2)}, u32[]{:S(2)}) collective-permute-start(bf16[320,384]{1,0:T(8,128)(2,1)S(1)} %add_convert_fusion), channel_id=1, source_target_pairs={{0,3},{1,0},{2,1},{3,2},{4,7},{5,4},{6,5},{7,6},{8,11},{9,8},{10,9... | collective-permute-start | bytes 737288 | tf_op jit(solution)/shard_map/ppermute | solution.py:570
  130.8 2.0 %collective-permute-start.27 = (bf16[320,128]{1,0:T(8,128)(2,1)S(1)}, bf16[320,128]{1,0:T(8,128)(2,1)S(1)}, u32[]{:S(2)}, u32[]{:S(2)}) collective-permute-start(bf16[320,128]{1,0:T(8,128)(2,1)S(1)} %add_convert_fusion.5), channel_id=1, source_target_pairs={{0,48},{1,49},{2,50},{3,51},{4,52},{5,53},{6,54},{7,55},{8,56},{9,... | collective-permute-start | bytes 245768 | tf_op jit(solution)/shard_map/ppermute | solution.py:570
  135.4 1.9 %collective-permute-start.15 = (bf16[320,384]{1,0:T(8,128)(2,1)S(1)}, bf16[320,384]{1,0:T(8,128)(2,1)S(1)}, u32[]{:S(2)}, u32[]{:S(2)}) collective-permute-start(bf16[320,384]{1,0:T(8,128)(2,1)S(1)} %fusion), channel_id=1, source_target_pairs={{0,12},{1,13},{2,14},{3,15},{4,0},{5,1},{6,2},{7,3},{8,4},{9,5},{1... | collective-permute-start | bytes 737288 | tf_op jit(solution)/shard_map/ppermute | solution.py:570
  138.0 2.1 %collective-permute-start.29 = (bf16[320,128]{1,0:T(8,128)(2,1)S(1)}, bf16[320,128]{1,0:T(8,128)(2,1)S(1)}, u32[]{:S(2)}, u32[]{:S(2)}) collective-permute-start(bf16[320,128]{1,0:T(8,128)(2,1)S(1)} %add_convert_fusion.4), channel_id=1, source_target_pairs={{0,8},{1,9},{2,10},{3,11},{4,12},{5,13},{6,14},{7,15},{8,0},{9,1},... | collective-permute-start | bytes 245768 | tf_op jit(solution)/shard_map/ppermute | solution.py:570
  140.2 4.5 %collective-permute-done.13 = bf16[320,384]{1,0:T(8,128)(2,1)S(1)} collective-permute-done((bf16[320,384]{1,0:T(8,128)(2,1)S(1)}, bf16[320,384]{1,0:T(8,128)(2,1)S(1)}, u32[]{:S(2)}, u32[]{:S(2)}) %collective-permute-start.13) | collective-permute-done | bytes 245792 | tf_op jit(solution)/shard_map/ppermute | solution.py:570
  145.2 3.2 %collective-permute-start.18 = (bf16[1280,384]{1,0:T(8,128)(2,1)S(1)}, bf16[1280,384]{1,0:T(8,128)(2,1)S(1)}, u32[]{:S(2)}, u32[]{:S(2)}) collective-permute-start(bf16[1280,384]{1,0:T(8,128)(2,1)S(1)} %pad_maximum_fusion.ref.refs_0_), channel_id=1, source_target_pairs={{0,48},{1,49},{2,50},{3,51},{4,52},{5,53},{6,54},{7,55},{8,56},{9,... | collective-permute-start | bytes 2949128 | tf_op jit(solution)/shard_map/ppermute | solution.py:570
  148.5 1.6 collective-permute-done.30
  152.3 7.1 %collective-permute-done.33.ref.refs_7_ = bf16[1280,128]{1,0:T(8,128)(2,1)S(1)} collective-permute-done((bf16[1280,128]{1,0:T(8,128)(2,1)S(1)}, bf16[1280,128]{1,0:T(8,128)(2,1)S(1)}, u32[]{:S(2)}, u32[]{:S(2)}) %collective-permute-start.33) | collective-permute-done | bytes 327712 | tf_op jit(solution)/shard_map/ppermute | solution.py:570
  159.3 1.9 %collective-permute-start.32 = (bf16[1280,128]{1,0:T(8,128)(2,1)S(1)}, bf16[1280,128]{1,0:T(8,128)(2,1)S(1)}, u32[]{:S(2)}, u32[]{:S(2)}) collective-permute-start(bf16[1280,128]{1,0:T(8,128)(2,1)S(1)} %pad_maximum_fusion.1.ref.refs_4_), channel_id=1, source_target_pairs={{0,2},{1,3},{2,0},{3,1},{4,6},{5,7},{6,4},{7,5},{8,10},{9,11},{10,... | collective-permute-start | bytes 983048 | tf_op jit(solution)/shard_map/ppermute | solution.py:570
  162.4 8.6 %collective-permute-done.16.ref.refs_1_ = bf16[1280,384]{1,0:T(8,128)(2,1)S(1)} collective-permute-done((bf16[1280,384]{1,0:T(8,128)(2,1)S(1)}, bf16[1280,384]{1,0:T(8,128)(2,1)S(1)}, u32[]{:S(2)}, u32[]{:S(2)}) %collective-permute-start.16) | collective-permute-done | bytes 983072 | tf_op jit(solution)/shard_map/ppermute | solution.py:570
  171.3 5.1 %finish.1 = (bf16[2,5120,128]{2,1,0:T(8,128)(2,1)}, bf16[2,5120,128]{2,1,0:T(8,128)(2,1)}) custom-call(s32[2,4,4]{2,1,0:T(4,128)S(1)} %pad_add_fusion.at, bf16[1280,384]{1,0:T(8,128)(2,1)S(1)} %pad_maximum_fusion.ref.refs_0_, bf16[1280,384]{1,0:T(8,128)(2,1)S(1)} %collective-permute-done.16.ref.refs_1_, ...), custom_call_target="tpu_custom_call" | custom-call | tf_op jit(solution)/shard_map/finish/pallas_call | solution.py:534
  (91 shorter events, 25.7 us)
Async XLA Ops:
  0.6 23.0 %collective-permute-start = (bf16[2,5120,128]{2,1,0:T(8,128)(2,1)}, bf16[2,5120,128]{2,1,0:T(8,128)(2,1)S(1)}, u32[]{:S(2)}, u32[]{:S(2)}) collective-permute-start(bf16[2,5120,128]{2,1,0:T(8,128)(2,1)} %bitcast.30), channel_id=1, source_target_pairs={{0,64},{64,0},{1,65},{65,1},{2,66},{66,2},{3,67},{67,3},{4,68},{68... | collective-permute-start | bytes 7864328 | tf_op jit(solution)/shard_map/ppermute | solution.py:607
  0.7 22.9 %collective-permute-start.1 = (bf16[2,5120,128]{2,1,0:T(8,128)(2,1)}, bf16[2,5120,128]{2,1,0:T(8,128)(2,1)}, u32[]{:S(2)}, u32[]{:S(2)}) collective-permute-start(bf16[2,5120,128]{2,1,0:T(8,128)(2,1)} %bitcast.33), channel_id=1, source_target_pairs={{0,64},{64,0},{1,65},{65,1},{2,66},{66,2},{3,67},{67,3},{4,68},{68... | collective-permute-start | bytes 7864328 | tf_op jit(solution)/shard_map/ppermute | solution.py:608
  1.2 22.4 %collective-permute-start.2 = (f32[2,5120]{1,0:T(2,128)}, f32[2,5120]{1,0:T(2,128)S(1)}, u32[]{:S(2)}, u32[]{:S(2)}) collective-permute-start(f32[2,5120]{1,0:T(2,128)} %bitcast.36), channel_id=1, source_target_pairs={{0,64},{64,0},{1,65},{65,1},{2,66},{66,2},{3,67},{67,3},{4,68},{68... | collective-permute-start | bytes 122888 | tf_op jit(solution)/shard_map/ppermute | solution.py:609
  11.9 27.1 %all-to-all-start = ((bf16[128,8,384]{2,1,0:T(8,128)(2,1)}), bf16[128,8,384]{2,1,0:T(8,128)(2,1)S(1)}, u32[]{:S(2)}, u32[]{:S(2)}) async-start(bf16[128,8,384]{2,1,0:T(8,128)(2,1)} %bitcast.7), calls=%async_computation | async-start | bytes 1572864 | tf_op jit(solution)/shard_map/all_to_all | solution.py:611
  44.0 22.1 %collective-permute-start.3 = (bf16[768,512]{1,0:T(8,128)(2,1)}, bf16[768,512]{1,0:T(8,128)(2,1)S(1)}, u32[]{:S(2)}, u32[]{:S(2)}) collective-permute-start(bf16[768,512]{1,0:T(8,128)(2,1)} %get-tuple-element.30), channel_id=1, source_target_pairs={{0,64},{64,0},{1,65},{65,1},{2,66},{66,2},{3,67},{67,3},{4,68},{68... | collective-permute-start | bytes 2359304 | tf_op jit(solution)/shard_map/ppermute | solution.py:624
  44.1 22.0 %all-to-all-start.1 = ((bf16[128,8,384]{2,1,0:T(8,128)(2,1)}), bf16[128,8,384]{2,1,0:T(8,128)(2,1)S(1)}, u32[]{:S(2)}, u32[]{:S(2)}) async-start(bf16[128,8,384]{2,1,0:T(8,128)(2,1)} %bitcast.11), calls=%async_computation.1 | async-start | bytes 1572864 | tf_op jit(solution)/shard_map/all_to_all | solution.py:625
  74.3 24.7 %collective-permute-start.4 = (bf16[1280,384]{1,0:T(8,128)(2,1)}, bf16[1280,384]{1,0:T(8,128)(2,1)}, u32[]{:S(2)}, u32[]{:S(2)}) collective-permute-start(bf16[1280,384]{1,0:T(8,128)(2,1)} %get-tuple-element.34), channel_id=1, source_target_pairs={{0,32},{1,33},{2,34},{3,35},{4,36},{5,37},{6,38},{7,39},{8,40},{9,... | collective-permute-start | bytes 2949128 | tf_op jit(solution)/shard_map/ppermute | solution.py:570
  87.9 15.7 %collective-permute-start.5 = (bf16[1280,384]{1,0:T(8,128)(2,1)}, bf16[1280,384]{1,0:T(8,128)(2,1)}, u32[]{:S(2)}, u32[]{:S(2)}) collective-permute-start(bf16[1280,384]{1,0:T(8,128)(2,1)} %get-tuple-element.35), channel_id=1, source_target_pairs={{0,16},{1,17},{2,18},{3,19},{4,20},{5,21},{6,22},{7,23},{8,24},{9,... | collective-permute-start | bytes 2949128 | tf_op jit(solution)/shard_map/ppermute | solution.py:570
  88.8 14.8 %collective-permute-start.6 = (bf16[1280,384]{1,0:T(8,128)(2,1)}, bf16[1280,384]{1,0:T(8,128)(2,1)}, u32[]{:S(2)}, u32[]{:S(2)}) collective-permute-start(bf16[1280,384]{1,0:T(8,128)(2,1)} %get-tuple-element.36), channel_id=1, source_target_pairs={{0,48},{1,49},{2,50},{3,51},{4,52},{5,53},{6,54},{7,55},{8,56},{9,... | collective-permute-start | bytes 2949128 | tf_op jit(solution)/shard_map/ppermute | solution.py:570
  96.5 12.8 %collective-permute-start.19 = (bf16[1280,128]{1,0:T(8,128)(2,1)S(1)}, bf16[1280,128]{1,0:T(8,128)(2,1)S(1)}, u32[]{:S(2)}, u32[]{:S(2)}) collective-permute-start(bf16[1280,128]{1,0:T(8,128)(2,1)S(1)} %get-tuple-element.52), channel_id=1, source_target_pairs={{0,2},{1,3},{2,0},{3,1},{4,6},{5,7},{6,4},{7,5},{8,10},{9,11},{10,... | collective-permute-start | bytes 983048 | tf_op jit(solution)/shard_map/ppermute | solution.py:570
  97.9 17.9 %collective-permute-start.20 = (bf16[1280,128]{1,0:T(8,128)(2,1)S(1)}, bf16[1280,128]{1,0:T(8,128)(2,1)S(1)}, u32[]{:S(2)}, u32[]{:S(2)}) collective-permute-start(bf16[1280,128]{1,0:T(8,128)(2,1)S(1)} %get-tuple-element.55), channel_id=1, source_target_pairs={{0,1},{1,2},{2,3},{3,0},{4,5},{5,6},{6,7},{7,4},{8,9},{9,10},{10,1... | collective-permute-start | bytes 983048 | tf_op jit(solution)/shard_map/ppermute | solution.py:570
  99.0 16.8 %collective-permute-start.21 = (bf16[1280,128]{1,0:T(8,128)(2,1)S(1)}, bf16[1280,128]{1,0:T(8,128)(2,1)S(1)}, u32[]{:S(2)}, u32[]{:S(2)}) collective-permute-start(bf16[1280,128]{1,0:T(8,128)(2,1)S(1)} %get-tuple-element.54), channel_id=1, source_target_pairs={{0,3},{1,0},{2,1},{3,2},{4,7},{5,4},{6,5},{7,6},{8,11},{9,8},{10,9... | collective-permute-start | bytes 983048 | tf_op jit(solution)/shard_map/ppermute | solution.py:570
  106.4 11.8 %collective-permute-start.7 = (bf16[320,384]{1,0:T(8,128)(2,1)}, bf16[320,384]{1,0:T(8,128)(2,1)}, u32[]{:S(2)}, u32[]{:S(2)}) collective-permute-start(bf16[320,384]{1,0:T(8,128)(2,1)} %get-tuple-element.46), channel_id=1, source_target_pairs={{0,8},{1,9},{2,10},{3,11},{4,12},{5,13},{6,14},{7,15},{8,0},{9,1},... | collective-permute-start | bytes 737288 | tf_op jit(solution)/shard_map/ppermute | solution.py:570
  108.1 13.2 %collective-permute-start.8 = (bf16[320,384]{1,0:T(8,128)(2,1)}, bf16[320,384]{1,0:T(8,128)(2,1)}, u32[]{:S(2)}, u32[]{:S(2)}) collective-permute-start(bf16[320,384]{1,0:T(8,128)(2,1)} %get-tuple-element.48), channel_id=1, source_target_pairs={{0,4},{1,5},{2,6},{3,7},{4,8},{5,9},{6,10},{7,11},{8,12},{9,13},{1... | collective-permute-start | bytes 737288 | tf_op jit(solution)/shard_map/ppermute | solution.py:570
  109.3 12.0 %collective-permute-start.9 = (bf16[320,384]{1,0:T(8,128)(2,1)}, bf16[320,384]{1,0:T(8,128)(2,1)S(1)}, u32[]{:S(2)}, u32[]{:S(2)}) collective-permute-start(bf16[320,384]{1,0:T(8,128)(2,1)} %get-tuple-element.47), channel_id=1, source_target_pairs={{0,12},{1,13},{2,14},{3,15},{4,0},{5,1},{6,2},{7,3},{8,4},{9,5},{1... | collective-permute-start | bytes 737288 | tf_op jit(solution)/shard_map/ppermute | solution.py:570
  116.6 8.6 %collective-permute-start.22 = (bf16[320,128]{1,0:T(8,128)(2,1)S(1)}, bf16[320,128]{1,0:T(8,128)(2,1)S(1)}, u32[]{:S(2)}, u32[]{:S(2)}) collective-permute-start(bf16[320,128]{1,0:T(8,128)(2,1)S(1)} %get-tuple-element.49), channel_id=1, source_target_pairs={{0,8},{1,9},{2,10},{3,11},{4,12},{5,13},{6,14},{7,15},{8,0},{9,1},... | collective-permute-start | bytes 245768 | tf_op jit(solution)/shard_map/ppermute | solution.py:570
  118.0 9.6 %collective-permute-start.23 = (bf16[320,128]{1,0:T(8,128)(2,1)}, bf16[320,128]{1,0:T(8,128)(2,1)S(1)}, u32[]{:S(2)}, u32[]{:S(2)}) collective-permute-start(bf16[320,128]{1,0:T(8,128)(2,1)} %get-tuple-element.51), channel_id=1, source_target_pairs={{0,4},{1,5},{2,6},{3,7},{4,8},{5,9},{6,10},{7,11},{8,12},{9,13},{1... | collective-permute-start | bytes 245768 | tf_op jit(solution)/shard_map/ppermute | solution.py:570
  118.2 9.4 %collective-permute-start.24 = (bf16[320,128]{1,0:T(8,128)(2,1)S(1)}, bf16[320,128]{1,0:T(8,128)(2,1)}, u32[]{:S(2)}, u32[]{:S(2)}) collective-permute-start(bf16[320,128]{1,0:T(8,128)(2,1)S(1)} %get-tuple-element.50), channel_id=1, source_target_pairs={{0,12},{1,13},{2,14},{3,15},{4,0},{5,1},{6,2},{7,3},{8,4},{9,5},{1... | collective-permute-start | bytes 245768 | tf_op jit(solution)/shard_map/ppermute | solution.py:570
  122.9 7.9 %collective-permute-start.10 = (bf16[320,384]{1,0:T(8,128)(2,1)S(1)}, bf16[320,384]{1,0:T(8,128)(2,1)S(1)}, u32[]{:S(2)}, u32[]{:S(2)}) collective-permute-start(bf16[320,384]{1,0:T(8,128)(2,1)S(1)} %add_convert_fusion), channel_id=1, source_target_pairs={{0,2},{1,3},{2,0},{3,1},{4,6},{5,7},{6,4},{7,5},{8,10},{9,11},{10,... | collective-permute-start | bytes 737288 | tf_op jit(solution)/shard_map/ppermute | solution.py:570
  124.3 9.0 %collective-permute-start.11 = (bf16[320,384]{1,0:T(8,128)(2,1)S(1)}, bf16[320,384]{1,0:T(8,128)(2,1)S(1)}, u32[]{:S(2)}, u32[]{:S(2)}) collective-permute-start(bf16[320,384]{1,0:T(8,128)(2,1)S(1)} %add_convert_fusion), channel_id=1, source_target_pairs={{0,1},{1,2},{2,3},{3,0},{4,5},{5,6},{6,7},{7,4},{8,9},{9,10},{10,1... | collective-permute-start | bytes 737288 | tf_op jit(solution)/shard_map/ppermute | solution.py:570
  125.2 8.1 %collective-permute-start.12 = (bf16[320,384]{1,0:T(8,128)(2,1)S(1)}, bf16[320,384]{1,0:T(8,128)(2,1)S(1)}, u32[]{:S(2)}, u32[]{:S(2)}) collective-permute-start(bf16[320,384]{1,0:T(8,128)(2,1)S(1)} %add_convert_fusion), channel_id=1, source_target_pairs={{0,3},{1,0},{2,1},{3,2},{4,7},{5,4},{6,5},{7,6},{8,11},{9,8},{10,9... | collective-permute-start | bytes 737288 | tf_op jit(solution)/shard_map/ppermute | solution.py:570
  133.7 11.0 %collective-permute-start.13 = (bf16[320,384]{1,0:T(8,128)(2,1)S(1)}, bf16[320,384]{1,0:T(8,128)(2,1)S(1)}, u32[]{:S(2)}, u32[]{:S(2)}) collective-permute-start(bf16[320,384]{1,0:T(8,128)(2,1)S(1)} %fusion), channel_id=1, source_target_pairs={{0,4},{1,5},{2,6},{3,7},{4,8},{5,9},{6,10},{7,11},{8,12},{9,13},{1... | collective-permute-start | bytes 737288 | tf_op jit(solution)/shard_map/ppermute | solution.py:570
  133.8 10.9 %collective-permute-start.14 = (bf16[320,384]{1,0:T(8,128)(2,1)S(1)}, bf16[320,384]{1,0:T(8,128)(2,1)S(1)}, u32[]{:S(2)}, u32[]{:S(2)}) collective-permute-start(bf16[320,384]{1,0:T(8,128)(2,1)S(1)} %fusion), channel_id=1, source_target_pairs={{0,8},{1,9},{2,10},{3,11},{4,12},{5,13},{6,14},{7,15},{8,0},{9,1},... | collective-permute-start | bytes 737288 | tf_op jit(solution)/shard_map/ppermute | solution.py:570
  135.4 9.6 %collective-permute-start.15 = (bf16[320,384]{1,0:T(8,128)(2,1)S(1)}, bf16[320,384]{1,0:T(8,128)(2,1)S(1)}, u32[]{:S(2)}, u32[]{:S(2)}) collective-permute-start(bf16[320,384]{1,0:T(8,128)(2,1)S(1)} %fusion), channel_id=1, source_target_pairs={{0,12},{1,13},{2,14},{3,15},{4,0},{5,1},{6,2},{7,3},{8,4},{9,5},{1... | collective-permute-start | bytes 737288 | tf_op jit(solution)/shard_map/ppermute | solution.py:570
  137.3 11.1 %collective-permute-start.28 = (bf16[320,128]{1,0:T(8,128)(2,1)S(1)}, bf16[320,128]{1,0:T(8,128)(2,1)S(1)}, u32[]{:S(2)}, u32[]{:S(2)}) collective-permute-start(bf16[320,128]{1,0:T(8,128)(2,1)S(1)} %add_convert_fusion.4), channel_id=1, source_target_pairs={{0,4},{1,5},{2,6},{3,7},{4,8},{5,9},{6,10},{7,11},{8,12},{9,13},{1... | collective-permute-start | bytes 245768 | tf_op jit(solution)/shard_map/ppermute | solution.py:570
  138.0 10.4 %collective-permute-start.29 = (bf16[320,128]{1,0:T(8,128)(2,1)S(1)}, bf16[320,128]{1,0:T(8,128)(2,1)S(1)}, u32[]{:S(2)}, u32[]{:S(2)}) collective-permute-start(bf16[320,128]{1,0:T(8,128)(2,1)S(1)} %add_convert_fusion.4), channel_id=1, source_target_pairs={{0,8},{1,9},{2,10},{3,11},{4,12},{5,13},{6,14},{7,15},{8,0},{9,1},... | collective-permute-start | bytes 245768 | tf_op jit(solution)/shard_map/ppermute | solution.py:570
  145.1 25.9 %collective-permute-start.16 = (bf16[1280,384]{1,0:T(8,128)(2,1)S(1)}, bf16[1280,384]{1,0:T(8,128)(2,1)S(1)}, u32[]{:S(2)}, u32[]{:S(2)}) collective-permute-start(bf16[1280,384]{1,0:T(8,128)(2,1)S(1)} %pad_maximum_fusion.ref.refs_0_), channel_id=1, source_target_pairs={{0,16},{1,17},{2,18},{3,19},{4,20},{5,21},{6,22},{7,23},{8,24},{9,... | collective-permute-start | bytes 2949128 | tf_op jit(solution)/shard_map/ppermute | solution.py:570
  145.2 25.9 %collective-permute-start.18 = (bf16[1280,384]{1,0:T(8,128)(2,1)S(1)}, bf16[1280,384]{1,0:T(8,128)(2,1)S(1)}, u32[]{:S(2)}, u32[]{:S(2)}) collective-permute-start(bf16[1280,384]{1,0:T(8,128)(2,1)S(1)} %pad_maximum_fusion.ref.refs_0_), channel_id=1, source_target_pairs={{0,48},{1,49},{2,50},{3,51},{4,52},{5,53},{6,54},{7,55},{8,56},{9,... | collective-permute-start | bytes 2949128 | tf_op jit(solution)/shard_map/ppermute | solution.py:570
  148.4 22.9 %collective-permute-start.17 = (bf16[1280,384]{1,0:T(8,128)(2,1)S(1)}, bf16[1280,384]{1,0:T(8,128)(2,1)S(1)}, u32[]{:S(2)}, u32[]{:S(2)}) collective-permute-start(bf16[1280,384]{1,0:T(8,128)(2,1)S(1)} %pad_maximum_fusion.ref.refs_0_), channel_id=1, source_target_pairs={{0,32},{1,33},{2,34},{3,35},{4,36},{5,37},{6,38},{7,39},{8,40},{9,... | collective-permute-start | bytes 2949128 | tf_op jit(solution)/shard_map/ppermute | solution.py:570
  150.1 9.2 %collective-permute-start.33 = (bf16[1280,128]{1,0:T(8,128)(2,1)S(1)}, bf16[1280,128]{1,0:T(8,128)(2,1)S(1)}, u32[]{:S(2)}, u32[]{:S(2)}) collective-permute-start(bf16[1280,128]{1,0:T(8,128)(2,1)S(1)} %pad_maximum_fusion.1.ref.refs_4_), channel_id=1, source_target_pairs={{0,3},{1,0},{2,1},{3,2},{4,7},{5,4},{6,5},{7,6},{8,11},{9,8},{10,9... | collective-permute-start | bytes 983048 | tf_op jit(solution)/shard_map/ppermute | solution.py:570
  151.0 11.2 %collective-permute-start.31 = (bf16[1280,128]{1,0:T(8,128)(2,1)S(1)}, bf16[1280,128]{1,0:T(8,128)(2,1)S(1)}, u32[]{:S(2)}, u32[]{:S(2)}) collective-permute-start(bf16[1280,128]{1,0:T(8,128)(2,1)S(1)} %pad_maximum_fusion.1.ref.refs_4_), channel_id=1, source_target_pairs={{0,1},{1,2},{2,3},{3,0},{4,5},{5,6},{6,7},{7,4},{8,9},{9,10},{10,1... | collective-permute-start | bytes 983048 | tf_op jit(solution)/shard_map/ppermute | solution.py:570
  159.3 11.9 %collective-permute-start.32 = (bf16[1280,128]{1,0:T(8,128)(2,1)S(1)}, bf16[1280,128]{1,0:T(8,128)(2,1)S(1)}, u32[]{:S(2)}, u32[]{:S(2)}) collective-permute-start(bf16[1280,128]{1,0:T(8,128)(2,1)S(1)} %pad_maximum_fusion.1.ref.refs_4_), channel_id=1, source_target_pairs={{0,2},{1,3},{2,0},{3,1},{4,6},{5,7},{6,4},{7,5},{8,10},{9,11},{10,... | collective-permute-start | bytes 983048 | tf_op jit(solution)/shard_map/ppermute | solution.py:570
  (7 other events, 71.0 us)

commit v2 on v1

--- a/solution.py
+++ b/solution.py
@@ -339,14 +339,14 @@
             tail = dot(at_end, rec[s, :, k:])
             proj += [(near[:, :k], near[:, 2 * k :]), (near[:, k : 2 * k], next_up)]
             cot += [tail[:, :k], tail[:, k:]]
+        to_start = place(t0)
+        to_start_next = place(t0 + 1)
+        to_end = place(t1 + 1)
         for copy in copies:
             copy.wait()
         active, back, less, mix_first, mix_second = row_stage(
             proj, cot, square_sum, low[...], high[...], features
         )
-        to_start = place(t0)
-        to_start_next = place(t0 + 1)
-        to_end = place(t1 + 1)
         for s in range(2):
             l0, l1 = 2 * s, 2 * s + 1
             out[s] = dot(to_start, joined([back[l0], back[l1], less[l0]])).astype(bf16)
@@ -416,7 +416,7 @@
     both = turned.shape[1]
     k = cs.shape[1] // 2
     total = both // 2
-    parts = 4
+    parts = 2
     chunk = size // parts
 
     def kernel(at_ref, t_ref, w_ref, xs_ref, cs_ref, mix_ref, major, minor, t_buf, w_buf, sems):

time: 177 us -> 174 us (0.983)
  Pallas kernels: 66.3 us -> 63 us
    pallas_call x4, Pallas kernels: 23.3 us -> 19.8 us  [piece(): pl.pallas_call(kernel, in_specs=[pl.BlockSpec(memory_space=pltpu.SMEM)] +...]
  transfers between devices with their start and end apart: 36 -> 36, of which waited for: 12 -> 12; matrix products, arithmetic and copies ran while one was open for 5% -> 5% of each run, Pallas kernels for 28% -> 27%
where the time goes in v2:
time: 174 us; the launch traced here: 173 us
  Pallas kernels  63 us (36%)
  starting transfers between devices  59.2 us (34%)
  waiting for transfers between devices  40.7 us (23%)
  other arithmetic  7.23 us (4%)
  local copies, waits for them, and re-layouts  1.98 us (1%)
    ppermute x30, starting transfers between devices, hop(): return lax.ppermute(values, ('section', 'peer'), pairs)  41.2 us
    ppermute x30, waiting for transfers between devices, hop(): return lax.ppermute(values, ('section', 'peer'), pairs)  30 us
    pallas_call x4, Pallas kernels, piece(): pl.pallas_call(kernel, in_specs=[pl.BlockSpec(memory_space=pltpu.SMEM)] +...  19.8 us
    pallas_call x1, Pallas kernels, prepare(): pl.pallas_call(kernel, grid_spec=pltpu.PrefetchScalarGridSpec(num_scalar_...  11.4 us
    all_to_all x1, starting transfers between devices, local(): lax.all_to_all(sent.reshape(rows, 8, 3 * k), ('section', 'peer'), 0, 0, t...  11.2 us
    pallas_call x1, Pallas kernels, front(): pl.pallas_call(kernel, grid=(steps,), in_specs=[pl.BlockSpec((lanes, rows...  10.5 us
    pallas_call x1, Pallas kernels, turn(): pl.pallas_call(kernel, grid=(features // block,), in_specs=[spec, spec],...  8.99 us
    all_to_all x1, waiting for transfers between devices, local(): lax.all_to_all(out.reshape(rows, 8, 3 * k), ('section', 'peer'), 0, 0, ti...  6.83 us
  transfers between devices with their start and end apart: 36, of which 12 were waited for; matrix products, arithmetic and copies ran while one was open for 5% of the time, Pallas kernels for 27%

profile of v2, /device:TPU:0, one launch (start us, length us, event | category | flops | bytes accessed | tf_op | source)
XLA Modules:
  0.0 173.1 jit_solution(8332834880824649916)
XLA Ops:
  1.3 10.5 %front.1 = bf16[1024,384]{1,0:T(8,128)(2,1)} custom-call(bf16[3,128,5120]{2,1,0:T(8,128)(2,1)} %bitcast.26, bf16[3,128,5120]{2,1,0:T(8,128)(2,1)} %bitcast.28, bf16[2,5120,128]{2,1,0:T(8,128)(2,1)} %bitcast.31, bf16[2,5120,128]{2,1,0:T(8,128)(2,1)} %bitcast.34, f32[2,5120]{1,0:T(2,128)} %bitcast.37), custom_call_target="tpu_custom_call" | custom-call | tf_op jit(solution)/shard_map/front/pallas_call | solution.py:190
  11.9 11.2 %all-to-all-start = ((bf16[128,8,384]{2,1,0:T(8,128)(2,1)}), bf16[128,8,384]{2,1,0:T(8,128)(2,1)S(1)}, u32[]{:S(2)}, u32[]{:S(2)}) async-start(bf16[128,8,384]{2,1,0:T(8,128)(2,1)} %bitcast.7), calls=%async_computation | async-start | bytes 1572864 | tf_op jit(solution)/shard_map/all_to_all | solution.py:611
  23.6 11.4 %prepare.1 = (bf16[5120,768]{1,0:T(8,128)(2,1)}, bf16[256,768]{1,0:T(8,128)(2,1)}, bf16[128,256]{1,0:T(8,128)(2,1)}) custom-call(s32[1]{0:T(128)} %bitcast.3.s_ref.mine, bf16[2,5120,128]{2,1,0:T(8,128)(2,1)} %bitcast.32, bf16[2,5120,128]{2,1,0:T(8,128)(2,1)} %bitcast.35, f32[2,5120]{1,0:T(2,128)} %bitcast.38, ...), custom_call_target="tpu_custom_call" | custom-call | tf_op jit(solution)/shard_map/prepare/pallas_call | solution.py:258
  35.1 3.8 %all-to-all-done = bf16[128,8,384]{2,1,0:T(8,128)(2,1)S(1)} async-done(((bf16[128,8,384]{2,1,0:T(8,128)(2,1)}), bf16[128,8,384]{2,1,0:T(8,128)(2,1)S(1)}, u32[]{:S(2)}, u32[]{:S(2)}) %all-to-all-start) | async-done | bytes 786464 | tf_op jit(solution)/shard_map/all_to_all | solution.py:611
  38.9 5.2 %meet.1 = (bf16[2,512,384]{2,1,0:T(8,128)(2,1)}, bf16[768,512]{1,0:T(8,128)(2,1)S(1)}, bf16[768,512]{1,0:T(8,128)(2,1)}) custom-call(s32[1]{0:T(128)} %bitcast.3.s_ref.mine, bf16[2,512,384]{2,1,0:T(8,128)(2,1)S(1)} %bitcast.24, s32[144,2]{1,0:T(8,128)S(1)} %copy.12.columns, s32[2,144]{1,0:T(2,128)S(1)} %multiply_add_fusion.rows, ...), custom_call_target="tpu_custom_call" | custom-call | tf_op jit(solution)/shard_map/meet/pallas_call | solution.py:368
  44.2 6.1 %all-to-all-start.1 = ((bf16[128,8,384]{2,1,0:T(8,128)(2,1)}), bf16[128,8,384]{2,1,0:T(8,128)(2,1)S(1)}, u32[]{:S(2)}, u32[]{:S(2)}) async-start(bf16[128,8,384]{2,1,0:T(8,128)(2,1)} %bitcast.11), calls=%async_computation.1 | async-start | bytes 1572864 | tf_op jit(solution)/shard_map/all_to_all | solution.py:625
  50.4 9.0 %turn.1.t_ref = bf16[5120,768]{1,0:T(8,128)(2,1)} custom-call(bf16[3,128,5120]{2,1,0:T(8,128)(2,1)} %bitcast.27, bf16[3,128,5120]{2,1,0:T(8,128)(2,1)} %bitcast.29), custom_call_target="tpu_custom_call" | custom-call | tf_op jit(solution)/shard_map/turn/pallas_call | solution.py:291
  59.4 6.8 %all-to-all-done.1 = bf16[128,8,384]{2,1,0:T(8,128)(2,1)S(1)} async-done(((bf16[128,8,384]{2,1,0:T(8,128)(2,1)}), bf16[128,8,384]{2,1,0:T(8,128)(2,1)S(1)}, u32[]{:S(2)}, u32[]{:S(2)}) %all-to-all-start.1) | async-done | bytes 786464 | tf_op jit(solution)/shard_map/all_to_all | solution.py:625
  68.4 5.2 %piece.4 = (bf16[1280,384]{1,0:T(8,128)(2,1)}, bf16[1280,128]{1,0:T(8,128)(2,1)S(1)}) custom-call(s32[1]{0:T(128)} %bitcast.at_ref, bf16[5120,768]{1,0:T(8,128)(2,1)} %turn.1.t_ref, bf16[5120,768]{1,0:T(8,128)(2,1)} %get-tuple-element.28.w_ref, bf16[384,512]{1,0:T(8,128)(2,1)S(1)} %get-tuple-element.31.xs_ref, ...), custom_call_target="tpu_custom_call" | custom-call | tf_op jit(solution)/shard_map/piece/pallas_call | solution.py:449
  75.1 5.2 %piece.5 = (bf16[1280,384]{1,0:T(8,128)(2,1)}, bf16[1280,128]{1,0:T(8,128)(2,1)S(1)}) custom-call(s32[1]{0:T(128)} %bitcast.13.at_ref, bf16[5120,768]{1,0:T(8,128)(2,1)} %turn.1.t_ref, bf16[5120,768]{1,0:T(8,128)(2,1)} %get-tuple-element.28.w_ref, bf16[384,512]{1,0:T(8,128)(2,1)S(1)} %get-tuple-element.31.xs_ref, ...), custom_call_target="tpu_custom_call" | custom-call | tf_op jit(solution)/shard_map/piece/pallas_call | solution.py:449
  80.3 5.2 %piece.6 = (bf16[1280,384]{1,0:T(8,128)(2,1)}, bf16[1280,128]{1,0:T(8,128)(2,1)S(1)}) custom-call(s32[1]{0:T(128)} %bitcast.14.at_ref, bf16[5120,768]{1,0:T(8,128)(2,1)} %turn.1.t_ref, bf16[5120,768]{1,0:T(8,128)(2,1)} %get-tuple-element.28.w_ref, bf16[384,512]{1,0:T(8,128)(2,1)S(1)} %get-tuple-element.31.xs_ref, ...), custom_call_target="tpu_custom_call" | custom-call | tf_op jit(solution)/shard_map/piece/pallas_call | solution.py:449
  86.4 2.4 %collective-permute-start.6 = (bf16[1280,384]{1,0:T(8,128)(2,1)}, bf16[1280,384]{1,0:T(8,128)(2,1)}, u32[]{:S(2)}, u32[]{:S(2)}) collective-permute-start(bf16[1280,384]{1,0:T(8,128)(2,1)} %get-tuple-element.36), channel_id=1, source_target_pairs={{0,48},{1,49},{2,50},{3,51},{4,52},{5,53},{6,54},{7,55},{8,56},{9,... | collective-permute-start | bytes 2949128 | tf_op jit(solution)/shard_map/ppermute | solution.py:570
  88.8 4.2 %piece.7 = (bf16[1280,384]{1,0:T(8,128)(2,1)S(1)}, bf16[1280,128]{1,0:T(8,128)(2,1)S(1)}) custom-call(s32[1]{0:T(128)} %bitcast.15.at_ref, bf16[5120,768]{1,0:T(8,128)(2,1)} %turn.1.t_ref, bf16[5120,768]{1,0:T(8,128)(2,1)} %get-tuple-element.28.w_ref, bf16[384,512]{1,0:T(8,128)(2,1)S(1)} %get-tuple-element.31.xs_ref, ...), custom_call_target="tpu_custom_call" | custom-call | tf_op jit(solution)/shard_map/piece/pallas_call | solution.py:449
  95.8 2.1 %collective-permute-start.21 = (bf16[1280,128]{1,0:T(8,128)(2,1)S(1)}, bf16[1280,128]{1,0:T(8,128)(2,1)S(1)}, u32[]{:S(2)}, u32[]{:S(2)}) collective-permute-start(bf16[1280,128]{1,0:T(8,128)(2,1)S(1)} %get-tuple-element.54), channel_id=1, source_target_pairs={{0,3},{1,0},{2,1},{3,2},{4,7},{5,4},{6,5},{7,6},{8,11},{9,8},{10,9... | collective-permute-start | bytes 983048 | tf_op jit(solution)/shard_map/ppermute | solution.py:570
  98.0 3.3 %collective-permute-done.5 = bf16[1280,384]{1,0:T(8,128)(2,1)} collective-permute-done((bf16[1280,384]{1,0:T(8,128)(2,1)}, bf16[1280,384]{1,0:T(8,128)(2,1)}, u32[]{:S(2)}, u32[]{:S(2)}) %collective-permute-start.5) | collective-permute-done | bytes 983072 | tf_op jit(solution)/shard_map/ppermute | solution.py:570
  101.2 2.8 %add_convert_fusion.3 = (bf16[320,384]{1,0:T(8,128)(2,1)}, bf16[320,384]{1,0:T(8,128)(2,1)}, bf16[320,384]{1,0:T(8,128)(2,1)}) fusion(bf16[1280,384]{1,0:T(8,128)(2,1)S(1)} %get-tuple-element.37, s32[]{:T(128)S(6)} %select_n.294, bf16[1280,384]{1,0:T(8,128)(2,1)} %collective-permute-done.6, bf16[1280,384]{1,0:T(8,128)(2,1)} %collective-permute-done.5, ...), kind=kLoop, calls=%fused_computation.6 | loop fusion | flops 2949120 | bytes 3686412 | tf_op jit(solution)/shard_map/convert_element_type | solution.py:584
  104.1 1.7 collective-permute-start.7
  106.9 2.1 %collective-permute-start.9 = (bf16[320,384]{1,0:T(8,128)(2,1)}, bf16[320,384]{1,0:T(8,128)(2,1)S(1)}, u32[]{:S(2)}, u32[]{:S(2)}) collective-permute-start(bf16[320,384]{1,0:T(8,128)(2,1)} %get-tuple-element.47), channel_id=1, source_target_pairs={{0,12},{1,13},{2,14},{3,15},{4,0},{5,1},{6,2},{7,3},{8,4},{9,5},{1... | collective-permute-start | bytes 737288 | tf_op jit(solution)/shard_map/ppermute | solution.py:570
  109.8 2.9 %collective-permute-done.20 = bf16[1280,128]{1,0:T(8,128)(2,1)S(1)} collective-permute-done((bf16[1280,128]{1,0:T(8,128)(2,1)S(1)}, bf16[1280,128]{1,0:T(8,128)(2,1)S(1)}, u32[]{:S(2)}, u32[]{:S(2)}) %collective-permute-start.20) | collective-permute-done | bytes 327712 | tf_op jit(solution)/shard_map/ppermute | solution.py:570
  114.8 3.2 %collective-permute-start.24 = (bf16[320,128]{1,0:T(8,128)(2,1)S(1)}, bf16[320,128]{1,0:T(8,128)(2,1)}, u32[]{:S(2)}, u32[]{:S(2)}) collective-permute-start(bf16[320,128]{1,0:T(8,128)(2,1)S(1)} %get-tuple-element.50), channel_id=1, source_target_pairs={{0,12},{1,13},{2,14},{3,15},{4,0},{5,1},{6,2},{7,3},{8,4},{9,5},{1... | collective-permute-start | bytes 245768 | tf_op jit(solution)/shard_map/ppermute | solution.py:570
  118.1 1.6 add_convert_fusion
  122.0 2.3 %collective-permute-start.12 = (bf16[320,384]{1,0:T(8,128)(2,1)S(1)}, bf16[320,384]{1,0:T(8,128)(2,1)S(1)}, u32[]{:S(2)}, u32[]{:S(2)}) collective-permute-start(bf16[320,384]{1,0:T(8,128)(2,1)S(1)} %add_convert_fusion), channel_id=1, source_target_pairs={{0,3},{1,0},{2,1},{3,2},{4,7},{5,4},{6,5},{7,6},{8,11},{9,8},{10,9... | collective-permute-start | bytes 737288 | tf_op jit(solution)/shard_map/ppermute | solution.py:570
  127.6 2.0 %collective-permute-start.27 = (bf16[320,128]{1,0:T(8,128)(2,1)S(1)}, bf16[320,128]{1,0:T(8,128)(2,1)S(1)}, u32[]{:S(2)}, u32[]{:S(2)}) collective-permute-start(bf16[320,128]{1,0:T(8,128)(2,1)S(1)} %add_convert_fusion.5), channel_id=1, source_target_pairs={{0,48},{1,49},{2,50},{3,51},{4,52},{5,53},{6,54},{7,55},{8,56},{9,... | collective-permute-start | bytes 245768 | tf_op jit(solution)/shard_map/ppermute | solution.py:570
  132.1 1.9 %collective-permute-start.15 = (bf16[320,384]{1,0:T(8,128)(2,1)S(1)}, bf16[320,384]{1,0:T(8,128)(2,1)S(1)}, u32[]{:S(2)}, u32[]{:S(2)}) collective-permute-start(bf16[320,384]{1,0:T(8,128)(2,1)S(1)} %fusion), channel_id=1, source_target_pairs={{0,12},{1,13},{2,14},{3,15},{4,0},{5,1},{6,2},{7,3},{8,4},{9,5},{1... | collective-permute-start | bytes 737288 | tf_op jit(solution)/shard_map/ppermute | solution.py:570
  134.8 2.1 %collective-permute-start.29 = (bf16[320,128]{1,0:T(8,128)(2,1)S(1)}, bf16[320,128]{1,0:T(8,128)(2,1)S(1)}, u32[]{:S(2)}, u32[]{:S(2)}) collective-permute-start(bf16[320,128]{1,0:T(8,128)(2,1)S(1)} %add_convert_fusion.4), channel_id=1, source_target_pairs={{0,8},{1,9},{2,10},{3,11},{4,12},{5,13},{6,14},{7,15},{8,0},{9,1},... | collective-permute-start | bytes 245768 | tf_op jit(solution)/shard_map/ppermute | solution.py:570
  136.9 4.5 %collective-permute-done.13 = bf16[320,384]{1,0:T(8,128)(2,1)S(1)} collective-permute-done((bf16[320,384]{1,0:T(8,128)(2,1)S(1)}, bf16[320,384]{1,0:T(8,128)(2,1)S(1)}, u32[]{:S(2)}, u32[]{:S(2)}) %collective-permute-start.13) | collective-permute-done | bytes 245792 | tf_op jit(solution)/shard_map/ppermute | solution.py:570
  142.0 3.2 %collective-permute-start.18 = (bf16[1280,384]{1,0:T(8,128)(2,1)S(1)}, bf16[1280,384]{1,0:T(8,128)(2,1)S(1)}, u32[]{:S(2)}, u32[]{:S(2)}) collective-permute-start(bf16[1280,384]{1,0:T(8,128)(2,1)S(1)} %pad_maximum_fusion.ref.refs_0_), channel_id=1, source_target_pairs={{0,48},{1,49},{2,50},{3,51},{4,52},{5,53},{6,54},{7,55},{8,56},{9,... | collective-permute-start | bytes 2949128 | tf_op jit(solution)/shard_map/ppermute | solution.py:570
  145.2 1.6 collective-permute-done.30
  149.1 7.1 %collective-permute-done.33.ref.refs_7_ = bf16[1280,128]{1,0:T(8,128)(2,1)S(1)} collective-permute-done((bf16[1280,128]{1,0:T(8,128)(2,1)S(1)}, bf16[1280,128]{1,0:T(8,128)(2,1)S(1)}, u32[]{:S(2)}, u32[]{:S(2)}) %collective-permute-start.33) | collective-permute-done | bytes 327712 | tf_op jit(solution)/shard_map/ppermute | solution.py:570
  156.1 1.9 %collective-permute-start.32 = (bf16[1280,128]{1,0:T(8,128)(2,1)S(1)}, bf16[1280,128]{1,0:T(8,128)(2,1)S(1)}, u32[]{:S(2)}, u32[]{:S(2)}) collective-permute-start(bf16[1280,128]{1,0:T(8,128)(2,1)S(1)} %pad_maximum_fusion.1.ref.refs_4_), channel_id=1, source_target_pairs={{0,2},{1,3},{2,0},{3,1},{4,6},{5,7},{6,4},{7,5},{8,10},{9,11},{10,... | collective-permute-start | bytes 983048 | tf_op jit(solution)/shard_map/ppermute | solution.py:570
  159.2 8.6 %collective-permute-done.16.ref.refs_1_ = bf16[1280,384]{1,0:T(8,128)(2,1)S(1)} collective-permute-done((bf16[1280,384]{1,0:T(8,128)(2,1)S(1)}, bf16[1280,384]{1,0:T(8,128)(2,1)S(1)}, u32[]{:S(2)}, u32[]{:S(2)}) %collective-permute-start.16) | collective-permute-done | bytes 983072 | tf_op jit(solution)/shard_map/ppermute | solution.py:570
  168.1 5.1 %finish.1 = (bf16[2,5120,128]{2,1,0:T(8,128)(2,1)}, bf16[2,5120,128]{2,1,0:T(8,128)(2,1)}) custom-call(s32[2,4,4]{2,1,0:T(4,128)S(1)} %pad_add_fusion.at, bf16[1280,384]{1,0:T(8,128)(2,1)S(1)} %pad_maximum_fusion.ref.refs_0_, bf16[1280,384]{1,0:T(8,128)(2,1)S(1)} %collective-permute-done.16.ref.refs_1_, ...), custom_call_target="tpu_custom_call" | custom-call | tf_op jit(solution)/shard_map/finish/pallas_call | solution.py:534
  (91 shorter events, 25.6 us)
Async XLA Ops:
  0.6 23.0 %collective-permute-start = (bf16[2,5120,128]{2,1,0:T(8,128)(2,1)}, bf16[2,5120,128]{2,1,0:T(8,128)(2,1)S(1)}, u32[]{:S(2)}, u32[]{:S(2)}) collective-permute-start(bf16[2,5120,128]{2,1,0:T(8,128)(2,1)} %bitcast.30), channel_id=1, source_target_pairs={{0,64},{64,0},{1,65},{65,1},{2,66},{66,2},{3,67},{67,3},{4,68},{68... | collective-permute-start | bytes 7864328 | tf_op jit(solution)/shard_map/ppermute | solution.py:607
  0.7 22.9 %collective-permute-start.1 = (bf16[2,5120,128]{2,1,0:T(8,128)(2,1)}, bf16[2,5120,128]{2,1,0:T(8,128)(2,1)}, u32[]{:S(2)}, u32[]{:S(2)}) collective-permute-start(bf16[2,5120,128]{2,1,0:T(8,128)(2,1)} %bitcast.33), channel_id=1, source_target_pairs={{0,64},{64,0},{1,65},{65,1},{2,66},{66,2},{3,67},{67,3},{4,68},{68... | collective-permute-start | bytes 7864328 | tf_op jit(solution)/shard_map/ppermute | solution.py:608
  1.2 22.4 %collective-permute-start.2 = (f32[2,5120]{1,0:T(2,128)}, f32[2,5120]{1,0:T(2,128)S(1)}, u32[]{:S(2)}, u32[]{:S(2)}) collective-permute-start(f32[2,5120]{1,0:T(2,128)} %bitcast.36), channel_id=1, source_target_pairs={{0,64},{64,0},{1,65},{65,1},{2,66},{66,2},{3,67},{67,3},{4,68},{68... | collective-permute-start | bytes 122888 | tf_op jit(solution)/shard_map/ppermute | solution.py:609
  11.9 27.1 %all-to-all-start = ((bf16[128,8,384]{2,1,0:T(8,128)(2,1)}), bf16[128,8,384]{2,1,0:T(8,128)(2,1)S(1)}, u32[]{:S(2)}, u32[]{:S(2)}) async-start(bf16[128,8,384]{2,1,0:T(8,128)(2,1)} %bitcast.7), calls=%async_computation | async-start | bytes 1572864 | tf_op jit(solution)/shard_map/all_to_all | solution.py:611
  44.2 22.1 %collective-permute-start.3 = (bf16[768,512]{1,0:T(8,128)(2,1)}, bf16[768,512]{1,0:T(8,128)(2,1)S(1)}, u32[]{:S(2)}, u32[]{:S(2)}) collective-permute-start(bf16[768,512]{1,0:T(8,128)(2,1)} %get-tuple-element.30), channel_id=1, source_target_pairs={{0,64},{64,0},{1,65},{65,1},{2,66},{66,2},{3,67},{67,3},{4,68},{68... | collective-permute-start | bytes 2359304 | tf_op jit(solution)/shard_map/ppermute | solution.py:624
  44.2 22.0 %all-to-all-start.1 = ((bf16[128,8,384]{2,1,0:T(8,128)(2,1)}), bf16[128,8,384]{2,1,0:T(8,128)(2,1)S(1)}, u32[]{:S(2)}, u32[]{:S(2)}) async-start(bf16[128,8,384]{2,1,0:T(8,128)(2,1)} %bitcast.11), calls=%async_computation.1 | async-start | bytes 1572864 | tf_op jit(solution)/shard_map/all_to_all | solution.py:625
  73.7 22.1 %collective-permute-start.4 = (bf16[1280,384]{1,0:T(8,128)(2,1)}, bf16[1280,384]{1,0:T(8,128)(2,1)}, u32[]{:S(2)}, u32[]{:S(2)}) collective-permute-start(bf16[1280,384]{1,0:T(8,128)(2,1)} %get-tuple-element.34), channel_id=1, source_target_pairs={{0,32},{1,33},{2,34},{3,35},{4,36},{5,37},{6,38},{7,39},{8,40},{9,... | collective-permute-start | bytes 2949128 | tf_op jit(solution)/shard_map/ppermute | solution.py:570
  85.5 15.7 %collective-permute-start.5 = (bf16[1280,384]{1,0:T(8,128)(2,1)}, bf16[1280,384]{1,0:T(8,128)(2,1)}, u32[]{:S(2)}, u32[]{:S(2)}) collective-permute-start(bf16[1280,384]{1,0:T(8,128)(2,1)} %get-tuple-element.35), channel_id=1, source_target_pairs={{0,16},{1,17},{2,18},{3,19},{4,20},{5,21},{6,22},{7,23},{8,24},{9,... | collective-permute-start | bytes 2949128 | tf_op jit(solution)/shard_map/ppermute | solution.py:570
  86.4 14.8 %collective-permute-start.6 = (bf16[1280,384]{1,0:T(8,128)(2,1)}, bf16[1280,384]{1,0:T(8,128)(2,1)}, u32[]{:S(2)}, u32[]{:S(2)}) collective-permute-start(bf16[1280,384]{1,0:T(8,128)(2,1)} %get-tuple-element.36), channel_id=1, source_target_pairs={{0,48},{1,49},{2,50},{3,51},{4,52},{5,53},{6,54},{7,55},{8,56},{9,... | collective-permute-start | bytes 2949128 | tf_op jit(solution)/shard_map/ppermute | solution.py:570
  93.3 13.6 %collective-permute-start.19 = (bf16[1280,128]{1,0:T(8,128)(2,1)S(1)}, bf16[1280,128]{1,0:T(8,128)(2,1)S(1)}, u32[]{:S(2)}, u32[]{:S(2)}) collective-permute-start(bf16[1280,128]{1,0:T(8,128)(2,1)S(1)} %get-tuple-element.52), channel_id=1, source_target_pairs={{0,2},{1,3},{2,0},{3,1},{4,6},{5,7},{6,4},{7,5},{8,10},{9,11},{10,... | collective-permute-start | bytes 983048 | tf_op jit(solution)/shard_map/ppermute | solution.py:570
  94.7 17.9 %collective-permute-start.20 = (bf16[1280,128]{1,0:T(8,128)(2,1)S(1)}, bf16[1280,128]{1,0:T(8,128)(2,1)S(1)}, u32[]{:S(2)}, u32[]{:S(2)}) collective-permute-start(bf16[1280,128]{1,0:T(8,128)(2,1)S(1)} %get-tuple-element.55), channel_id=1, source_target_pairs={{0,1},{1,2},{2,3},{3,0},{4,5},{5,6},{6,7},{7,4},{8,9},{9,10},{10,1... | collective-permute-start | bytes 983048 | tf_op jit(solution)/shard_map/ppermute | solution.py:570
  95.8 16.8 %collective-permute-start.21 = (bf16[1280,128]{1,0:T(8,128)(2,1)S(1)}, bf16[1280,128]{1,0:T(8,128)(2,1)S(1)}, u32[]{:S(2)}, u32[]{:S(2)}) collective-permute-start(bf16[1280,128]{1,0:T(8,128)(2,1)S(1)} %get-tuple-element.54), channel_id=1, source_target_pairs={{0,3},{1,0},{2,1},{3,2},{4,7},{5,4},{6,5},{7,6},{8,11},{9,8},{10,9... | collective-permute-start | bytes 983048 | tf_op jit(solution)/shard_map/ppermute | solution.py:570
  104.1 10.8 %collective-permute-start.7 = (bf16[320,384]{1,0:T(8,128)(2,1)}, bf16[320,384]{1,0:T(8,128)(2,1)}, u32[]{:S(2)}, u32[]{:S(2)}) collective-permute-start(bf16[320,384]{1,0:T(8,128)(2,1)} %get-tuple-element.46), channel_id=1, source_target_pairs={{0,8},{1,9},{2,10},{3,11},{4,12},{5,13},{6,14},{7,15},{8,0},{9,1},... | collective-permute-start | bytes 737288 | tf_op jit(solution)/shard_map/ppermute | solution.py:570
  105.8 12.3 %collective-permute-start.8 = (bf16[320,384]{1,0:T(8,128)(2,1)}, bf16[320,384]{1,0:T(8,128)(2,1)}, u32[]{:S(2)}, u32[]{:S(2)}) collective-permute-start(bf16[320,384]{1,0:T(8,128)(2,1)} %get-tuple-element.48), channel_id=1, source_target_pairs={{0,4},{1,5},{2,6},{3,7},{4,8},{5,9},{6,10},{7,11},{8,12},{9,13},{1... | collective-permute-start | bytes 737288 | tf_op jit(solution)/shard_map/ppermute | solution.py:570
  106.9 11.2 %collective-permute-start.9 = (bf16[320,384]{1,0:T(8,128)(2,1)}, bf16[320,384]{1,0:T(8,128)(2,1)S(1)}, u32[]{:S(2)}, u32[]{:S(2)}) collective-permute-start(bf16[320,384]{1,0:T(8,128)(2,1)} %get-tuple-element.47), channel_id=1, source_target_pairs={{0,12},{1,13},{2,14},{3,15},{4,0},{5,1},{6,2},{7,3},{8,4},{9,5},{1... | collective-permute-start | bytes 737288 | tf_op jit(solution)/shard_map/ppermute | solution.py:570
  113.4 8.6 %collective-permute-start.22 = (bf16[320,128]{1,0:T(8,128)(2,1)S(1)}, bf16[320,128]{1,0:T(8,128)(2,1)S(1)}, u32[]{:S(2)}, u32[]{:S(2)}) collective-permute-start(bf16[320,128]{1,0:T(8,128)(2,1)S(1)} %get-tuple-element.49), channel_id=1, source_target_pairs={{0,8},{1,9},{2,10},{3,11},{4,12},{5,13},{6,14},{7,15},{8,0},{9,1},... | collective-permute-start | bytes 245768 | tf_op jit(solution)/shard_map/ppermute | solution.py:570
  114.8 9.6 %collective-permute-start.23 = (bf16[320,128]{1,0:T(8,128)(2,1)}, bf16[320,128]{1,0:T(8,128)(2,1)S(1)}, u32[]{:S(2)}, u32[]{:S(2)}) collective-permute-start(bf16[320,128]{1,0:T(8,128)(2,1)} %get-tuple-element.51), channel_id=1, source_target_pairs={{0,4},{1,5},{2,6},{3,7},{4,8},{5,9},{6,10},{7,11},{8,12},{9,13},{1... | collective-permute-start | bytes 245768 | tf_op jit(solution)/shard_map/ppermute | solution.py:570
  114.8 9.6 %collective-permute-start.24 = (bf16[320,128]{1,0:T(8,128)(2,1)S(1)}, bf16[320,128]{1,0:T(8,128)(2,1)}, u32[]{:S(2)}, u32[]{:S(2)}) collective-permute-start(bf16[320,128]{1,0:T(8,128)(2,1)S(1)} %get-tuple-element.50), channel_id=1, source_target_pairs={{0,12},{1,13},{2,14},{3,15},{4,0},{5,1},{6,2},{7,3},{8,4},{9,5},{1... | collective-permute-start | bytes 245768 | tf_op jit(solution)/shard_map/ppermute | solution.py:570
  119.7 7.9 %collective-permute-start.10 = (bf16[320,384]{1,0:T(8,128)(2,1)S(1)}, bf16[320,384]{1,0:T(8,128)(2,1)S(1)}, u32[]{:S(2)}, u32[]{:S(2)}) collective-permute-start(bf16[320,384]{1,0:T(8,128)(2,1)S(1)} %add_convert_fusion), channel_id=1, source_target_pairs={{0,2},{1,3},{2,0},{3,1},{4,6},{5,7},{6,4},{7,5},{8,10},{9,11},{10,... | collective-permute-start | bytes 737288 | tf_op jit(solution)/shard_map/ppermute | solution.py:570
  121.1 9.0 %collective-permute-start.11 = (bf16[320,384]{1,0:T(8,128)(2,1)S(1)}, bf16[320,384]{1,0:T(8,128)(2,1)S(1)}, u32[]{:S(2)}, u32[]{:S(2)}) collective-permute-start(bf16[320,384]{1,0:T(8,128)(2,1)S(1)} %add_convert_fusion), channel_id=1, source_target_pairs={{0,1},{1,2},{2,3},{3,0},{4,5},{5,6},{6,7},{7,4},{8,9},{9,10},{10,1... | collective-permute-start | bytes 737288 | tf_op jit(solution)/shard_map/ppermute | solution.py:570
  122.0 8.1 %collective-permute-start.12 = (bf16[320,384]{1,0:T(8,128)(2,1)S(1)}, bf16[320,384]{1,0:T(8,128)(2,1)S(1)}, u32[]{:S(2)}, u32[]{:S(2)}) collective-permute-start(bf16[320,384]{1,0:T(8,128)(2,1)S(1)} %add_convert_fusion), channel_id=1, source_target_pairs={{0,3},{1,0},{2,1},{3,2},{4,7},{5,4},{6,5},{7,6},{8,11},{9,8},{10,9... | collective-permute-start | bytes 737288 | tf_op jit(solution)/shard_map/ppermute | solution.py:570
  130.5 11.0 %collective-permute-start.13 = (bf16[320,384]{1,0:T(8,128)(2,1)S(1)}, bf16[320,384]{1,0:T(8,128)(2,1)S(1)}, u32[]{:S(2)}, u32[]{:S(2)}) collective-permute-start(bf16[320,384]{1,0:T(8,128)(2,1)S(1)} %fusion), channel_id=1, source_target_pairs={{0,4},{1,5},{2,6},{3,7},{4,8},{5,9},{6,10},{7,11},{8,12},{9,13},{1... | collective-permute-start | bytes 737288 | tf_op jit(solution)/shard_map/ppermute | solution.py:570
  130.5 10.9 %collective-permute-start.14 = (bf16[320,384]{1,0:T(8,128)(2,1)S(1)}, bf16[320,384]{1,0:T(8,128)(2,1)S(1)}, u32[]{:S(2)}, u32[]{:S(2)}) collective-permute-start(bf16[320,384]{1,0:T(8,128)(2,1)S(1)} %fusion), channel_id=1, source_target_pairs={{0,8},{1,9},{2,10},{3,11},{4,12},{5,13},{6,14},{7,15},{8,0},{9,1},... | collective-permute-start | bytes 737288 | tf_op jit(solution)/shard_map/ppermute | solution.py:570
  132.1 9.6 %collective-permute-start.15 = (bf16[320,384]{1,0:T(8,128)(2,1)S(1)}, bf16[320,384]{1,0:T(8,128)(2,1)S(1)}, u32[]{:S(2)}, u32[]{:S(2)}) collective-permute-start(bf16[320,384]{1,0:T(8,128)(2,1)S(1)} %fusion), channel_id=1, source_target_pairs={{0,12},{1,13},{2,14},{3,15},{4,0},{5,1},{6,2},{7,3},{8,4},{9,5},{1... | collective-permute-start | bytes 737288 | tf_op jit(solution)/shard_map/ppermute | solution.py:570
  134.1 11.1 %collective-permute-start.28 = (bf16[320,128]{1,0:T(8,128)(2,1)S(1)}, bf16[320,128]{1,0:T(8,128)(2,1)S(1)}, u32[]{:S(2)}, u32[]{:S(2)}) collective-permute-start(bf16[320,128]{1,0:T(8,128)(2,1)S(1)} %add_convert_fusion.4), channel_id=1, source_target_pairs={{0,4},{1,5},{2,6},{3,7},{4,8},{5,9},{6,10},{7,11},{8,12},{9,13},{1... | collective-permute-start | bytes 245768 | tf_op jit(solution)/shard_map/ppermute | solution.py:570
  134.8 10.4 %collective-permute-start.29 = (bf16[320,128]{1,0:T(8,128)(2,1)S(1)}, bf16[320,128]{1,0:T(8,128)(2,1)S(1)}, u32[]{:S(2)}, u32[]{:S(2)}) collective-permute-start(bf16[320,128]{1,0:T(8,128)(2,1)S(1)} %add_convert_fusion.4), channel_id=1, source_target_pairs={{0,8},{1,9},{2,10},{3,11},{4,12},{5,13},{6,14},{7,15},{8,0},{9,1},... | collective-permute-start | bytes 245768 | tf_op jit(solution)/shard_map/ppermute | solution.py:570
  141.9 25.9 %collective-permute-start.16 = (bf16[1280,384]{1,0:T(8,128)(2,1)S(1)}, bf16[1280,384]{1,0:T(8,128)(2,1)S(1)}, u32[]{:S(2)}, u32[]{:S(2)}) collective-permute-start(bf16[1280,384]{1,0:T(8,128)(2,1)S(1)} %pad_maximum_fusion.ref.refs_0_), channel_id=1, source_target_pairs={{0,16},{1,17},{2,18},{3,19},{4,20},{5,21},{6,22},{7,23},{8,24},{9,... | collective-permute-start | bytes 2949128 | tf_op jit(solution)/shard_map/ppermute | solution.py:570
  142.0 25.9 %collective-permute-start.18 = (bf16[1280,384]{1,0:T(8,128)(2,1)S(1)}, bf16[1280,384]{1,0:T(8,128)(2,1)S(1)}, u32[]{:S(2)}, u32[]{:S(2)}) collective-permute-start(bf16[1280,384]{1,0:T(8,128)(2,1)S(1)} %pad_maximum_fusion.ref.refs_0_), channel_id=1, source_target_pairs={{0,48},{1,49},{2,50},{3,51},{4,52},{5,53},{6,54},{7,55},{8,56},{9,... | collective-permute-start | bytes 2949128 | tf_op jit(solution)/shard_map/ppermute | solution.py:570
  145.2 22.9 %collective-permute-start.17 = (bf16[1280,384]{1,0:T(8,128)(2,1)S(1)}, bf16[1280,384]{1,0:T(8,128)(2,1)S(1)}, u32[]{:S(2)}, u32[]{:S(2)}) collective-permute-start(bf16[1280,384]{1,0:T(8,128)(2,1)S(1)} %pad_maximum_fusion.ref.refs_0_), channel_id=1, source_target_pairs={{0,32},{1,33},{2,34},{3,35},{4,36},{5,37},{6,38},{7,39},{8,40},{9,... | collective-permute-start | bytes 2949128 | tf_op jit(solution)/shard_map/ppermute | solution.py:570
  146.9 9.2 %collective-permute-start.33 = (bf16[1280,128]{1,0:T(8,128)(2,1)S(1)}, bf16[1280,128]{1,0:T(8,128)(2,1)S(1)}, u32[]{:S(2)}, u32[]{:S(2)}) collective-permute-start(bf16[1280,128]{1,0:T(8,128)(2,1)S(1)} %pad_maximum_fusion.1.ref.refs_4_), channel_id=1, source_target_pairs={{0,3},{1,0},{2,1},{3,2},{4,7},{5,4},{6,5},{7,6},{8,11},{9,8},{10,9... | collective-permute-start | bytes 983048 | tf_op jit(solution)/shard_map/ppermute | solution.py:570
  147.8 11.2 %collective-permute-start.31 = (bf16[1280,128]{1,0:T(8,128)(2,1)S(1)}, bf16[1280,128]{1,0:T(8,128)(2,1)S(1)}, u32[]{:S(2)}, u32[]{:S(2)}) collective-permute-start(bf16[1280,128]{1,0:T(8,128)(2,1)S(1)} %pad_maximum_fusion.1.ref.refs_4_), channel_id=1, source_target_pairs={{0,1},{1,2},{2,3},{3,0},{4,5},{5,6},{6,7},{7,4},{8,9},{9,10},{10,1... | collective-permute-start | bytes 983048 | tf_op jit(solution)/shard_map/ppermute | solution.py:570
  156.1 11.9 %collective-permute-start.32 = (bf16[1280,128]{1,0:T(8,128)(2,1)S(1)}, bf16[1280,128]{1,0:T(8,128)(2,1)S(1)}, u32[]{:S(2)}, u32[]{:S(2)}) collective-permute-start(bf16[1280,128]{1,0:T(8,128)(2,1)S(1)} %pad_maximum_fusion.1.ref.refs_4_), channel_id=1, source_target_pairs={{0,2},{1,3},{2,0},{3,1},{4,6},{5,7},{6,4},{7,5},{8,10},{9,11},{10,... | collective-permute-start | bytes 983048 | tf_op jit(solution)/shard_map/ppermute | solution.py:570
  (7 other events, 71.0 us)

commit v3 on v2

--- a/solution.py
+++ b/solution.py
@@ -38,8 +38,16 @@
     return jnp.sum(values, axis=1, keepdims=True)
 
 
-def row_stage(proj, cot, square_sum, gram_low, gram_high, feature_count):
+def row_stage(proj, cot, square_sum, grams, feature_count):
     k = cot[0].shape[1]
+
+    def activated(pre):
+        r = lax.rsqrt(square_sum * (1.0 / feature_count) + norm_eps)
+        h = r * pre
+        return r, h, (h * jax.nn.sigmoid(h)).astype(bf16)
+
+    first_layer = activated(proj[0][0])
+    gram_low, gram_high = grams()
 
     def cut(g, i, j):
         return g[i * k : (i + 1) * k, j * k : (j + 1) * k].astype(bf16)
@@ -58,12 +66,10 @@
 
     hidden, active, inverse, full = [], [], [], []
     for l in range(4):
-        r = lax.rsqrt(square_sum * (1.0 / feature_count) + norm_eps)
         pre = proj[l][0]
         for i in range(l):
             pre = pre + dot(active[i], ugd[(i, l)])
-        h = r * pre
-        a = (h * jax.nn.sigmoid(h)).astype(bf16)
+        r, h, a = activated(pre) if l else first_layer
         hidden.append(h)
         active.append(a)
         inverse.append(r)
@@ -342,10 +348,14 @@
         to_start = place(t0)
         to_start_next = place(t0 + 1)
         to_end = place(t1 + 1)
-        for copy in copies:
-            copy.wait()
+
+        def grams():
+            for copy in copies:
+                copy.wait()
+            return low[...], high[...]
+
         active, back, less, mix_first, mix_second = row_stage(
-            proj, cot, square_sum, low[...], high[...], features
+            proj, cot, square_sum, grams, features
         )
         for s in range(2):
             l0, l1 = 2 * s, 2 * s + 1
@@ -488,17 +498,16 @@
     known = [squares(major[i]) for i in early] + [squares(minor[i]) for i in early]
 
     def kernel(at, *refs):
-        ins, known, (down, up) = refs[:8], refs[8:14], refs[14:]
-        group = pl.program_id(0)
-
-        def run(which, out):
+        ins, known, (down, up, out, sems) = refs[:8], refs[8:14], refs[14:]
+
+        def run(which, group, columns):
             sums = [None] * 4
             for i in range(4):
                 if i == late:
-                    v = ins[which * 4 + i][...].astype(f32)
+                    v = ins[which * 4 + i][:, columns].astype(f32)
                     v = jnp.sum((v * v).reshape(4, part // 8, 8, k), axis=1)
                 else:
-                    v = known[which * 3 + early.index(i)][...]
+                    v = known[which * 3 + early.index(i)][:, :, columns]
                 sums[i] = ring_sum(v[0], v[2], v[1], v[3])
             total = ring_sum(sums[0], sums[2], sums[1], sums[3])
             mean = jnp.sum(total) * (1.0 / (features * k))
@@ -506,46 +515,30 @@
             for i in range(4):
                 for j in range(4):
                     row = pl.multiple_of(at[which, i, j], 16)
-                    v = ins[which * 4 + i][j * part : (j + 1) * part, :].astype(f32)
-                    out[0, pl.ds(row, part), :] = (v * scale).astype(bf16)
-
-        @pl.when(group < 2)
-        def _():
-            run(0, down)
-
-        @pl.when(group == 2)
-        def _():
-            run(0, up)
-
-        @pl.when(group == 3)
-        def _():
-            run(1, up)
-
-    def specs(shape, columns):
-        zeros = (0,) * (len(shape) - 1)
-        return pl.BlockSpec(shape, lambda g, at: (*zeros, columns(g)))
-
-    def clipped(g):
-        return jnp.minimum(g, 2)
-
-    def fixed(g):
-        return 0
-
-    return pl.pallas_call(
-        kernel,
-        grid_spec=pltpu.PrefetchScalarGridSpec(
-            num_scalar_prefetch=1,
-            grid=(4,),
-            in_specs=[specs((quarter, k), clipped)] * 4
-            + [specs((quarter, k), fixed)] * 4
-            + [specs((4, 8, k), clipped)] * 3
-            + [specs((4, 8, k), fixed)] * 3,
-            out_specs=[
-                pl.BlockSpec((1, features, k), lambda g, at: (jnp.minimum(g, 1), 0, 0)),
-                pl.BlockSpec((1, features, k), lambda g, at: (jnp.maximum(g - 2, 0), 0, 0)),
-            ],
-        ),
+                    v = ins[which * 4 + i][j * part : (j + 1) * part, columns].astype(f32)
+                    out[group, pl.ds(row, part), :] = (v * scale).astype(bf16)
+
+        copies = []
+        for group in range(4):
+            which = group // 3
+            run(which, group, slice(0, k) if which else slice(group * k, (group + 1) * k))
+            target = (down, up)[group // 2].at[group % 2]
+            copies.append(pltpu.make_async_copy(out.at[group], target, sems.at[group]))
+            copies[-1].start()
+        for copy in copies:
+            copy.wait()
+
+    local_ref = pl.BlockSpec(memory_space=pltpu.VMEM)
+    far_ref = pl.BlockSpec(memory_space=pl.ANY)
+    return pl.pallas_call(
+        kernel,
+        in_specs=[pl.BlockSpec(memory_space=pltpu.SMEM)] + [local_ref] * 14,
+        out_specs=[far_ref] * 2,
         out_shape=[jax.ShapeDtypeStruct((2, features, k), bf16)] * 2,
+        scratch_shapes=[
+            pltpu.VMEM((4, features, k), bf16),
+            pltpu.SemaphoreType.DMA((4,)),
+        ],
         compiler_params=pltpu.CompilerParams(vmem_limit_bytes=16 << 20),
         name="finish",
     )(starts, *blocks, *known)

time: 174 us -> 173 us (level)
  no operation moved by 1% of the time
where the time goes in v3:
time: 173 us; the launch traced here: 172 us
  Pallas kernels  61.4 us (35%)
  starting transfers between devices  59.2 us (34%)
  waiting for transfers between devices  40.6 us (23%)
  other arithmetic  7.23 us (4%)
  local copies, waits for them, and re-layouts  1.98 us (1%)
    ppermute x30, starting transfers between devices, hop(): return lax.ppermute(values, ('section', 'peer'), pairs)  41.2 us
    ppermute x30, waiting for transfers between devices, hop(): return lax.ppermute(values, ('section', 'peer'), pairs)  29.9 us
    pallas_call x4, Pallas kernels, piece(): pl.pallas_call(kernel, in_specs=[pl.BlockSpec(memory_space=pltpu.SMEM)] +...  19.8 us
    pallas_call x1, Pallas kernels, prepare(): pl.pallas_call(kernel, grid_spec=pltpu.PrefetchScalarGridSpec(num_scalar_...  11.4 us
    all_to_all x1, starting transfers between devices, local(): lax.all_to_all(sent.reshape(rows, 8, 3 * k), ('section', 'peer'), 0, 0, t...  11.2 us
    pallas_call x1, Pallas kernels, front(): pl.pallas_call(kernel, grid=(steps,), in_specs=[pl.BlockSpec((lanes, rows...  10.5 us
    pallas_call x1, Pallas kernels, turn(): pl.pallas_call(kernel, grid=(features // block,), in_specs=[spec, spec],...  8.99 us
    all_to_all x1, waiting for transfers between devices, local(): lax.all_to_all(out.reshape(rows, 8, 3 * k), ('section', 'peer'), 0, 0, ti...  6.83 us
  transfers between devices with their start and end apart: 36, of which 12 were waited for; matrix products, arithmetic and copies ran while one was open for 5% of the time, Pallas kernels for 27%

profile of v3, /device:TPU:0, one launch (start us, length us, event | category | flops | bytes accessed | tf_op | source)
XLA Modules:
  0.0 171.7 jit_solution(9035858586984030848)
XLA Ops:
  1.3 10.5 %front.1 = bf16[1024,384]{1,0:T(8,128)(2,1)} custom-call(bf16[3,128,5120]{2,1,0:T(8,128)(2,1)} %bitcast.26, bf16[3,128,5120]{2,1,0:T(8,128)(2,1)} %bitcast.28, bf16[2,5120,128]{2,1,0:T(8,128)(2,1)} %bitcast.31, bf16[2,5120,128]{2,1,0:T(8,128)(2,1)} %bitcast.34, f32[2,5120]{1,0:T(2,128)} %bitcast.37), custom_call_target="tpu_custom_call" | custom-call | tf_op jit(solution)/shard_map/front/pallas_call | solution.py:196
  11.9 11.2 %all-to-all-start = ((bf16[128,8,384]{2,1,0:T(8,128)(2,1)}), bf16[128,8,384]{2,1,0:T(8,128)(2,1)S(1)}, u32[]{:S(2)}, u32[]{:S(2)}) async-start(bf16[128,8,384]{2,1,0:T(8,128)(2,1)} %bitcast.7), calls=%async_computation | async-start | bytes 1572864 | tf_op jit(solution)/shard_map/all_to_all | solution.py:604
  23.6 11.4 %prepare.1 = (bf16[5120,768]{1,0:T(8,128)(2,1)}, bf16[256,768]{1,0:T(8,128)(2,1)}, bf16[128,256]{1,0:T(8,128)(2,1)}) custom-call(s32[1]{0:T(128)} %bitcast.3.s_ref.mine, bf16[2,5120,128]{2,1,0:T(8,128)(2,1)} %bitcast.32, bf16[2,5120,128]{2,1,0:T(8,128)(2,1)} %bitcast.35, f32[2,5120]{1,0:T(2,128)} %bitcast.38, ...), custom_call_target="tpu_custom_call" | custom-call | tf_op jit(solution)/shard_map/prepare/pallas_call | solution.py:264
  35.1 3.8 %all-to-all-done = bf16[128,8,384]{2,1,0:T(8,128)(2,1)S(1)} async-done(((bf16[128,8,384]{2,1,0:T(8,128)(2,1)}), bf16[128,8,384]{2,1,0:T(8,128)(2,1)S(1)}, u32[]{:S(2)}, u32[]{:S(2)}) %all-to-all-start) | async-done | bytes 786464 | tf_op jit(solution)/shard_map/all_to_all | solution.py:604
  38.9 5.2 %meet.1 = (bf16[2,512,384]{2,1,0:T(8,128)(2,1)}, bf16[768,512]{1,0:T(8,128)(2,1)S(1)}, bf16[768,512]{1,0:T(8,128)(2,1)}) custom-call(s32[1]{0:T(128)} %bitcast.3.s_ref.mine, bf16[2,512,384]{2,1,0:T(8,128)(2,1)S(1)} %bitcast.24, s32[144,2]{1,0:T(8,128)S(1)} %copy.12.columns, s32[2,144]{1,0:T(2,128)S(1)} %multiply_add_fusion.rows, ...), custom_call_target="tpu_custom_call" | custom-call | tf_op jit(solution)/shard_map/meet/pallas_call | solution.py:378
  44.2 6.1 %all-to-all-start.1 = ((bf16[128,8,384]{2,1,0:T(8,128)(2,1)}), bf16[128,8,384]{2,1,0:T(8,128)(2,1)S(1)}, u32[]{:S(2)}, u32[]{:S(2)}) async-start(bf16[128,8,384]{2,1,0:T(8,128)(2,1)} %bitcast.11), calls=%async_computation.1 | async-start | bytes 1572864 | tf_op jit(solution)/shard_map/all_to_all | solution.py:618
  50.4 9.0 %turn.1.t_ref = bf16[5120,768]{1,0:T(8,128)(2,1)} custom-call(bf16[3,128,5120]{2,1,0:T(8,128)(2,1)} %bitcast.27, bf16[3,128,5120]{2,1,0:T(8,128)(2,1)} %bitcast.29), custom_call_target="tpu_custom_call" | custom-call | tf_op jit(solution)/shard_map/turn/pallas_call | solution.py:297
  59.4 6.8 %all-to-all-done.1 = bf16[128,8,384]{2,1,0:T(8,128)(2,1)S(1)} async-done(((bf16[128,8,384]{2,1,0:T(8,128)(2,1)}), bf16[128,8,384]{2,1,0:T(8,128)(2,1)S(1)}, u32[]{:S(2)}, u32[]{:S(2)}) %all-to-all-start.1) | async-done | bytes 786464 | tf_op jit(solution)/shard_map/all_to_all | solution.py:618
  68.4 5.2 %piece.4 = (bf16[1280,384]{1,0:T(8,128)(2,1)}, bf16[1280,128]{1,0:T(8,128)(2,1)S(1)}) custom-call(s32[1]{0:T(128)} %bitcast.at_ref, bf16[5120,768]{1,0:T(8,128)(2,1)} %turn.1.t_ref, bf16[5120,768]{1,0:T(8,128)(2,1)} %get-tuple-element.28.w_ref, bf16[384,512]{1,0:T(8,128)(2,1)S(1)} %get-tuple-element.31.xs_ref, ...), custom_call_target="tpu_custom_call" | custom-call | tf_op jit(solution)/shard_map/piece/pallas_call | solution.py:459
  75.1 5.2 %piece.5 = (bf16[1280,384]{1,0:T(8,128)(2,1)}, bf16[1280,128]{1,0:T(8,128)(2,1)S(1)}) custom-call(s32[1]{0:T(128)} %bitcast.13.at_ref, bf16[5120,768]{1,0:T(8,128)(2,1)} %turn.1.t_ref, bf16[5120,768]{1,0:T(8,128)(2,1)} %get-tuple-element.28.w_ref, bf16[384,512]{1,0:T(8,128)(2,1)S(1)} %get-tuple-element.31.xs_ref, ...), custom_call_target="tpu_custom_call" | custom-call | tf_op jit(solution)/shard_map/piece/pallas_call | solution.py:459
  80.3 5.2 %piece.6 = (bf16[1280,384]{1,0:T(8,128)(2,1)}, bf16[1280,128]{1,0:T(8,128)(2,1)S(1)}) custom-call(s32[1]{0:T(128)} %bitcast.14.at_ref, bf16[5120,768]{1,0:T(8,128)(2,1)} %turn.1.t_ref, bf16[5120,768]{1,0:T(8,128)(2,1)} %get-tuple-element.28.w_ref, bf16[384,512]{1,0:T(8,128)(2,1)S(1)} %get-tuple-element.31.xs_ref, ...), custom_call_target="tpu_custom_call" | custom-call | tf_op jit(solution)/shard_map/piece/pallas_call | solution.py:459
  86.4 2.4 %collective-permute-start.6 = (bf16[1280,384]{1,0:T(8,128)(2,1)}, bf16[1280,384]{1,0:T(8,128)(2,1)}, u32[]{:S(2)}, u32[]{:S(2)}) collective-permute-start(bf16[1280,384]{1,0:T(8,128)(2,1)} %get-tuple-element.36), channel_id=1, source_target_pairs={{0,48},{1,49},{2,50},{3,51},{4,52},{5,53},{6,54},{7,55},{8,56},{9,... | collective-permute-start | bytes 2949128 | tf_op jit(solution)/shard_map/ppermute | solution.py:563
  88.8 4.2 %piece.7 = (bf16[1280,384]{1,0:T(8,128)(2,1)S(1)}, bf16[1280,128]{1,0:T(8,128)(2,1)S(1)}) custom-call(s32[1]{0:T(128)} %bitcast.15.at_ref, bf16[5120,768]{1,0:T(8,128)(2,1)} %turn.1.t_ref, bf16[5120,768]{1,0:T(8,128)(2,1)} %get-tuple-element.28.w_ref, bf16[384,512]{1,0:T(8,128)(2,1)S(1)} %get-tuple-element.31.xs_ref, ...), custom_call_target="tpu_custom_call" | custom-call | tf_op jit(solution)/shard_map/piece/pallas_call | solution.py:459
  95.8 2.1 %collective-permute-start.21 = (bf16[1280,128]{1,0:T(8,128)(2,1)S(1)}, bf16[1280,128]{1,0:T(8,128)(2,1)S(1)}, u32[]{:S(2)}, u32[]{:S(2)}) collective-permute-start(bf16[1280,128]{1,0:T(8,128)(2,1)S(1)} %get-tuple-element.54), channel_id=1, source_target_pairs={{0,3},{1,0},{2,1},{3,2},{4,7},{5,4},{6,5},{7,6},{8,11},{9,8},{10,9... | collective-permute-start | bytes 983048 | tf_op jit(solution)/shard_map/ppermute | solution.py:563
  97.9 3.2 %collective-permute-done.5 = bf16[1280,384]{1,0:T(8,128)(2,1)} collective-permute-done((bf16[1280,384]{1,0:T(8,128)(2,1)}, bf16[1280,384]{1,0:T(8,128)(2,1)}, u32[]{:S(2)}, u32[]{:S(2)}) %collective-permute-start.5) | collective-permute-done | bytes 983072 | tf_op jit(solution)/shard_map/ppermute | solution.py:563
  101.2 2.8 %add_convert_fusion.3 = (bf16[320,384]{1,0:T(8,128)(2,1)}, bf16[320,384]{1,0:T(8,128)(2,1)}, bf16[320,384]{1,0:T(8,128)(2,1)}) fusion(bf16[1280,384]{1,0:T(8,128)(2,1)S(1)} %get-tuple-element.37, s32[]{:T(128)S(6)} %select_n.294, bf16[1280,384]{1,0:T(8,128)(2,1)} %collective-permute-done.6, bf16[1280,384]{1,0:T(8,128)(2,1)} %collective-permute-done.5, ...), kind=kLoop, calls=%fused_computation.6 | loop fusion | flops 2949120 | bytes 3686412 | tf_op jit(solution)/shard_map/convert_element_type | solution.py:577
  104.0 1.7 collective-permute-start.7
  106.9 2.1 %collective-permute-start.9 = (bf16[320,384]{1,0:T(8,128)(2,1)}, bf16[320,384]{1,0:T(8,128)(2,1)S(1)}, u32[]{:S(2)}, u32[]{:S(2)}) collective-permute-start(bf16[320,384]{1,0:T(8,128)(2,1)} %get-tuple-element.47), channel_id=1, source_target_pairs={{0,12},{1,13},{2,14},{3,15},{4,0},{5,1},{6,2},{7,3},{8,4},{9,5},{1... | collective-permute-start | bytes 737288 | tf_op jit(solution)/shard_map/ppermute | solution.py:563
  109.7 2.9 %collective-permute-done.20 = bf16[1280,128]{1,0:T(8,128)(2,1)S(1)} collective-permute-done((bf16[1280,128]{1,0:T(8,128)(2,1)S(1)}, bf16[1280,128]{1,0:T(8,128)(2,1)S(1)}, u32[]{:S(2)}, u32[]{:S(2)}) %collective-permute-start.20) | collective-permute-done | bytes 327712 | tf_op jit(solution)/shard_map/ppermute | solution.py:563
  114.8 3.2 %collective-permute-start.24 = (bf16[320,128]{1,0:T(8,128)(2,1)S(1)}, bf16[320,128]{1,0:T(8,128)(2,1)}, u32[]{:S(2)}, u32[]{:S(2)}) collective-permute-start(bf16[320,128]{1,0:T(8,128)(2,1)S(1)} %get-tuple-element.50), channel_id=1, source_target_pairs={{0,12},{1,13},{2,14},{3,15},{4,0},{5,1},{6,2},{7,3},{8,4},{9,5},{1... | collective-permute-start | bytes 245768 | tf_op jit(solution)/shard_map/ppermute | solution.py:563
  118.0 1.6 add_convert_fusion
  122.0 2.3 %collective-permute-start.12 = (bf16[320,384]{1,0:T(8,128)(2,1)S(1)}, bf16[320,384]{1,0:T(8,128)(2,1)S(1)}, u32[]{:S(2)}, u32[]{:S(2)}) collective-permute-start(bf16[320,384]{1,0:T(8,128)(2,1)S(1)} %add_convert_fusion), channel_id=1, source_target_pairs={{0,3},{1,0},{2,1},{3,2},{4,7},{5,4},{6,5},{7,6},{8,11},{9,8},{10,9... | collective-permute-start | bytes 737288 | tf_op jit(solution)/shard_map/ppermute | solution.py:563
  127.5 2.0 %collective-permute-start.27 = (bf16[320,128]{1,0:T(8,128)(2,1)S(1)}, bf16[320,128]{1,0:T(8,128)(2,1)S(1)}, u32[]{:S(2)}, u32[]{:S(2)}) collective-permute-start(bf16[320,128]{1,0:T(8,128)(2,1)S(1)} %add_convert_fusion.5), channel_id=1, source_target_pairs={{0,48},{1,49},{2,50},{3,51},{4,52},{5,53},{6,54},{7,55},{8,56},{9,... | collective-permute-start | bytes 245768 | tf_op jit(solution)/shard_map/ppermute | solution.py:563
  132.1 1.9 %collective-permute-start.15 = (bf16[320,384]{1,0:T(8,128)(2,1)S(1)}, bf16[320,384]{1,0:T(8,128)(2,1)S(1)}, u32[]{:S(2)}, u32[]{:S(2)}) collective-permute-start(bf16[320,384]{1,0:T(8,128)(2,1)S(1)} %fusion), channel_id=1, source_target_pairs={{0,12},{1,13},{2,14},{3,15},{4,0},{5,1},{6,2},{7,3},{8,4},{9,5},{1... | collective-permute-start | bytes 737288 | tf_op jit(solution)/shard_map/ppermute | solution.py:563
  134.7 2.1 %collective-permute-start.29 = (bf16[320,128]{1,0:T(8,128)(2,1)S(1)}, bf16[320,128]{1,0:T(8,128)(2,1)S(1)}, u32[]{:S(2)}, u32[]{:S(2)}) collective-permute-start(bf16[320,128]{1,0:T(8,128)(2,1)S(1)} %add_convert_fusion.4), channel_id=1, source_target_pairs={{0,8},{1,9},{2,10},{3,11},{4,12},{5,13},{6,14},{7,15},{8,0},{9,1},... | collective-permute-start | bytes 245768 | tf_op jit(solution)/shard_map/ppermute | solution.py:563
  136.9 4.5 %collective-permute-done.13 = bf16[320,384]{1,0:T(8,128)(2,1)S(1)} collective-permute-done((bf16[320,384]{1,0:T(8,128)(2,1)S(1)}, bf16[320,384]{1,0:T(8,128)(2,1)S(1)}, u32[]{:S(2)}, u32[]{:S(2)}) %collective-permute-start.13) | collective-permute-done | bytes 245792 | tf_op jit(solution)/shard_map/ppermute | solution.py:563
  141.9 3.2 %collective-permute-start.18 = (bf16[1280,384]{1,0:T(8,128)(2,1)S(1)}, bf16[1280,384]{1,0:T(8,128)(2,1)S(1)}, u32[]{:S(2)}, u32[]{:S(2)}) collective-permute-start(bf16[1280,384]{1,0:T(8,128)(2,1)S(1)} %pad_maximum_fusion.ref.refs_0_), channel_id=1, source_target_pairs={{0,48},{1,49},{2,50},{3,51},{4,52},{5,53},{6,54},{7,55},{8,56},{9,... | collective-permute-start | bytes 2949128 | tf_op jit(solution)/shard_map/ppermute | solution.py:563
  145.2 1.6 collective-permute-done.30
  149.0 7.1 %collective-permute-done.33.ref.refs_7_ = bf16[1280,128]{1,0:T(8,128)(2,1)S(1)} collective-permute-done((bf16[1280,128]{1,0:T(8,128)(2,1)S(1)}, bf16[1280,128]{1,0:T(8,128)(2,1)S(1)}, u32[]{:S(2)}, u32[]{:S(2)}) %collective-permute-start.33) | collective-permute-done | bytes 327712 | tf_op jit(solution)/shard_map/ppermute | solution.py:563
  156.1 1.9 %collective-permute-start.32 = (bf16[1280,128]{1,0:T(8,128)(2,1)S(1)}, bf16[1280,128]{1,0:T(8,128)(2,1)S(1)}, u32[]{:S(2)}, u32[]{:S(2)}) collective-permute-start(bf16[1280,128]{1,0:T(8,128)(2,1)S(1)} %pad_maximum_fusion.1.ref.refs_4_), channel_id=1, source_target_pairs={{0,2},{1,3},{2,0},{3,1},{4,6},{5,7},{6,4},{7,5},{8,10},{9,11},{10,... | collective-permute-start | bytes 983048 | tf_op jit(solution)/shard_map/ppermute | solution.py:563
  159.1 8.6 %collective-permute-done.16.ref.refs_1_ = bf16[1280,384]{1,0:T(8,128)(2,1)S(1)} collective-permute-done((bf16[1280,384]{1,0:T(8,128)(2,1)S(1)}, bf16[1280,384]{1,0:T(8,128)(2,1)S(1)}, u32[]{:S(2)}, u32[]{:S(2)}) %collective-permute-start.16) | collective-permute-done | bytes 983072 | tf_op jit(solution)/shard_map/ppermute | solution.py:563
  168.0 3.5 %finish.1 = (bf16[2,5120,128]{2,1,0:T(8,128)(2,1)}, bf16[2,5120,128]{2,1,0:T(8,128)(2,1)}) custom-call(s32[2,4,4]{2,1,0:T(4,128)S(1)} %pad_add_fusion.at, bf16[1280,384]{1,0:T(8,128)(2,1)S(1)} %pad_maximum_fusion.ref.refs_0_, bf16[1280,384]{1,0:T(8,128)(2,1)S(1)} %collective-permute-done.16.ref.refs_1_, ...), custom_call_target="tpu_custom_call" | custom-call | tf_op jit(solution)/shard_map/finish/pallas_call | solution.py:533
  (91 shorter events, 25.6 us)
Async XLA Ops:
  0.6 23.0 %collective-permute-start = (bf16[2,5120,128]{2,1,0:T(8,128)(2,1)}, bf16[2,5120,128]{2,1,0:T(8,128)(2,1)S(1)}, u32[]{:S(2)}, u32[]{:S(2)}) collective-permute-start(bf16[2,5120,128]{2,1,0:T(8,128)(2,1)} %bitcast.30), channel_id=1, source_target_pairs={{0,64},{64,0},{1,65},{65,1},{2,66},{66,2},{3,67},{67,3},{4,68},{68... | collective-permute-start | bytes 7864328 | tf_op jit(solution)/shard_map/ppermute | solution.py:600
  0.7 22.9 %collective-permute-start.1 = (bf16[2,5120,128]{2,1,0:T(8,128)(2,1)}, bf16[2,5120,128]{2,1,0:T(8,128)(2,1)}, u32[]{:S(2)}, u32[]{:S(2)}) collective-permute-start(bf16[2,5120,128]{2,1,0:T(8,128)(2,1)} %bitcast.33), channel_id=1, source_target_pairs={{0,64},{64,0},{1,65},{65,1},{2,66},{66,2},{3,67},{67,3},{4,68},{68... | collective-permute-start | bytes 7864328 | tf_op jit(solution)/shard_map/ppermute | solution.py:601
  1.2 22.4 %collective-permute-start.2 = (f32[2,5120]{1,0:T(2,128)}, f32[2,5120]{1,0:T(2,128)S(1)}, u32[]{:S(2)}, u32[]{:S(2)}) collective-permute-start(f32[2,5120]{1,0:T(2,128)} %bitcast.36), channel_id=1, source_target_pairs={{0,64},{64,0},{1,65},{65,1},{2,66},{66,2},{3,67},{67,3},{4,68},{68... | collective-permute-start | bytes 122888 | tf_op jit(solution)/shard_map/ppermute | solution.py:602
  11.9 27.1 %all-to-all-start = ((bf16[128,8,384]{2,1,0:T(8,128)(2,1)}), bf16[128,8,384]{2,1,0:T(8,128)(2,1)S(1)}, u32[]{:S(2)}, u32[]{:S(2)}) async-start(bf16[128,8,384]{2,1,0:T(8,128)(2,1)} %bitcast.7), calls=%async_computation | async-start | bytes 1572864 | tf_op jit(solution)/shard_map/all_to_all | solution.py:604
  44.1 22.1 %collective-permute-start.3 = (bf16[768,512]{1,0:T(8,128)(2,1)}, bf16[768,512]{1,0:T(8,128)(2,1)S(1)}, u32[]{:S(2)}, u32[]{:S(2)}) collective-permute-start(bf16[768,512]{1,0:T(8,128)(2,1)} %get-tuple-element.30), channel_id=1, source_target_pairs={{0,64},{64,0},{1,65},{65,1},{2,66},{66,2},{3,67},{67,3},{4,68},{68... | collective-permute-start | bytes 2359304 | tf_op jit(solution)/shard_map/ppermute | solution.py:617
  44.2 22.0 %all-to-all-start.1 = ((bf16[128,8,384]{2,1,0:T(8,128)(2,1)}), bf16[128,8,384]{2,1,0:T(8,128)(2,1)S(1)}, u32[]{:S(2)}, u32[]{:S(2)}) async-start(bf16[128,8,384]{2,1,0:T(8,128)(2,1)} %bitcast.11), calls=%async_computation.1 | async-start | bytes 1572864 | tf_op jit(solution)/shard_map/all_to_all | solution.py:618
  73.6 22.2 %collective-permute-start.4 = (bf16[1280,384]{1,0:T(8,128)(2,1)}, bf16[1280,384]{1,0:T(8,128)(2,1)}, u32[]{:S(2)}, u32[]{:S(2)}) collective-permute-start(bf16[1280,384]{1,0:T(8,128)(2,1)} %get-tuple-element.34), channel_id=1, source_target_pairs={{0,32},{1,33},{2,34},{3,35},{4,36},{5,37},{6,38},{7,39},{8,40},{9,... | collective-permute-start | bytes 2949128 | tf_op jit(solution)/shard_map/ppermute | solution.py:563
  85.5 15.7 %collective-permute-start.5 = (bf16[1280,384]{1,0:T(8,128)(2,1)}, bf16[1280,384]{1,0:T(8,128)(2,1)}, u32[]{:S(2)}, u32[]{:S(2)}) collective-permute-start(bf16[1280,384]{1,0:T(8,128)(2,1)} %get-tuple-element.35), channel_id=1, source_target_pairs={{0,16},{1,17},{2,18},{3,19},{4,20},{5,21},{6,22},{7,23},{8,24},{9,... | collective-permute-start | bytes 2949128 | tf_op jit(solution)/shard_map/ppermute | solution.py:563
  86.4 14.8 %collective-permute-start.6 = (bf16[1280,384]{1,0:T(8,128)(2,1)}, bf16[1280,384]{1,0:T(8,128)(2,1)}, u32[]{:S(2)}, u32[]{:S(2)}) collective-permute-start(bf16[1280,384]{1,0:T(8,128)(2,1)} %get-tuple-element.36), channel_id=1, source_target_pairs={{0,48},{1,49},{2,50},{3,51},{4,52},{5,53},{6,54},{7,55},{8,56},{9,... | collective-permute-start | bytes 2949128 | tf_op jit(solution)/shard_map/ppermute | solution.py:563
  93.2 13.7 %collective-permute-start.19 = (bf16[1280,128]{1,0:T(8,128)(2,1)S(1)}, bf16[1280,128]{1,0:T(8,128)(2,1)S(1)}, u32[]{:S(2)}, u32[]{:S(2)}) collective-permute-start(bf16[1280,128]{1,0:T(8,128)(2,1)S(1)} %get-tuple-element.52), channel_id=1, source_target_pairs={{0,2},{1,3},{2,0},{3,1},{4,6},{5,7},{6,4},{7,5},{8,10},{9,11},{10,... | collective-permute-start | bytes 983048 | tf_op jit(solution)/shard_map/ppermute | solution.py:563
  94.7 17.9 %collective-permute-start.20 = (bf16[1280,128]{1,0:T(8,128)(2,1)S(1)}, bf16[1280,128]{1,0:T(8,128)(2,1)S(1)}, u32[]{:S(2)}, u32[]{:S(2)}) collective-permute-start(bf16[1280,128]{1,0:T(8,128)(2,1)S(1)} %get-tuple-element.55), channel_id=1, source_target_pairs={{0,1},{1,2},{2,3},{3,0},{4,5},{5,6},{6,7},{7,4},{8,9},{9,10},{10,1... | collective-permute-start | bytes 983048 | tf_op jit(solution)/shard_map/ppermute | solution.py:563
  95.8 16.8 %collective-permute-start.21 = (bf16[1280,128]{1,0:T(8,128)(2,1)S(1)}, bf16[1280,128]{1,0:T(8,128)(2,1)S(1)}, u32[]{:S(2)}, u32[]{:S(2)}) collective-permute-start(bf16[1280,128]{1,0:T(8,128)(2,1)S(1)} %get-tuple-element.54), channel_id=1, source_target_pairs={{0,3},{1,0},{2,1},{3,2},{4,7},{5,4},{6,5},{7,6},{8,11},{9,8},{10,9... | collective-permute-start | bytes 983048 | tf_op jit(solution)/shard_map/ppermute | solution.py:563
  104.0 10.8 %collective-permute-start.7 = (bf16[320,384]{1,0:T(8,128)(2,1)}, bf16[320,384]{1,0:T(8,128)(2,1)}, u32[]{:S(2)}, u32[]{:S(2)}) collective-permute-start(bf16[320,384]{1,0:T(8,128)(2,1)} %get-tuple-element.46), channel_id=1, source_target_pairs={{0,8},{1,9},{2,10},{3,11},{4,12},{5,13},{6,14},{7,15},{8,0},{9,1},... | collective-permute-start | bytes 737288 | tf_op jit(solution)/shard_map/ppermute | solution.py:563
  105.7 12.3 %collective-permute-start.8 = (bf16[320,384]{1,0:T(8,128)(2,1)}, bf16[320,384]{1,0:T(8,128)(2,1)}, u32[]{:S(2)}, u32[]{:S(2)}) collective-permute-start(bf16[320,384]{1,0:T(8,128)(2,1)} %get-tuple-element.48), channel_id=1, source_target_pairs={{0,4},{1,5},{2,6},{3,7},{4,8},{5,9},{6,10},{7,11},{8,12},{9,13},{1... | collective-permute-start | bytes 737288 | tf_op jit(solution)/shard_map/ppermute | solution.py:563
  106.9 11.2 %collective-permute-start.9 = (bf16[320,384]{1,0:T(8,128)(2,1)}, bf16[320,384]{1,0:T(8,128)(2,1)S(1)}, u32[]{:S(2)}, u32[]{:S(2)}) collective-permute-start(bf16[320,384]{1,0:T(8,128)(2,1)} %get-tuple-element.47), channel_id=1, source_target_pairs={{0,12},{1,13},{2,14},{3,15},{4,0},{5,1},{6,2},{7,3},{8,4},{9,5},{1... | collective-permute-start | bytes 737288 | tf_op jit(solution)/shard_map/ppermute | solution.py:563
  113.3 8.6 %collective-permute-start.22 = (bf16[320,128]{1,0:T(8,128)(2,1)S(1)}, bf16[320,128]{1,0:T(8,128)(2,1)S(1)}, u32[]{:S(2)}, u32[]{:S(2)}) collective-permute-start(bf16[320,128]{1,0:T(8,128)(2,1)S(1)} %get-tuple-element.49), channel_id=1, source_target_pairs={{0,8},{1,9},{2,10},{3,11},{4,12},{5,13},{6,14},{7,15},{8,0},{9,1},... | collective-permute-start | bytes 245768 | tf_op jit(solution)/shard_map/ppermute | solution.py:563
  114.8 9.6 %collective-permute-start.23 = (bf16[320,128]{1,0:T(8,128)(2,1)}, bf16[320,128]{1,0:T(8,128)(2,1)S(1)}, u32[]{:S(2)}, u32[]{:S(2)}) collective-permute-start(bf16[320,128]{1,0:T(8,128)(2,1)} %get-tuple-element.51), channel_id=1, source_target_pairs={{0,4},{1,5},{2,6},{3,7},{4,8},{5,9},{6,10},{7,11},{8,12},{9,13},{1... | collective-permute-start | bytes 245768 | tf_op jit(solution)/shard_map/ppermute | solution.py:563
  114.8 9.6 %collective-permute-start.24 = (bf16[320,128]{1,0:T(8,128)(2,1)S(1)}, bf16[320,128]{1,0:T(8,128)(2,1)}, u32[]{:S(2)}, u32[]{:S(2)}) collective-permute-start(bf16[320,128]{1,0:T(8,128)(2,1)S(1)} %get-tuple-element.50), channel_id=1, source_target_pairs={{0,12},{1,13},{2,14},{3,15},{4,0},{5,1},{6,2},{7,3},{8,4},{9,5},{1... | collective-permute-start | bytes 245768 | tf_op jit(solution)/shard_map/ppermute | solution.py:563
  119.6 7.9 %collective-permute-start.10 = (bf16[320,384]{1,0:T(8,128)(2,1)S(1)}, bf16[320,384]{1,0:T(8,128)(2,1)S(1)}, u32[]{:S(2)}, u32[]{:S(2)}) collective-permute-start(bf16[320,384]{1,0:T(8,128)(2,1)S(1)} %add_convert_fusion), channel_id=1, source_target_pairs={{0,2},{1,3},{2,0},{3,1},{4,6},{5,7},{6,4},{7,5},{8,10},{9,11},{10,... | collective-permute-start | bytes 737288 | tf_op jit(solution)/shard_map/ppermute | solution.py:563
  121.1 9.0 %collective-permute-start.11 = (bf16[320,384]{1,0:T(8,128)(2,1)S(1)}, bf16[320,384]{1,0:T(8,128)(2,1)S(1)}, u32[]{:S(2)}, u32[]{:S(2)}) collective-permute-start(bf16[320,384]{1,0:T(8,128)(2,1)S(1)} %add_convert_fusion), channel_id=1, source_target_pairs={{0,1},{1,2},{2,3},{3,0},{4,5},{5,6},{6,7},{7,4},{8,9},{9,10},{10,1... | collective-permute-start | bytes 737288 | tf_op jit(solution)/shard_map/ppermute | solution.py:563
  122.0 8.1 %collective-permute-start.12 = (bf16[320,384]{1,0:T(8,128)(2,1)S(1)}, bf16[320,384]{1,0:T(8,128)(2,1)S(1)}, u32[]{:S(2)}, u32[]{:S(2)}) collective-permute-start(bf16[320,384]{1,0:T(8,128)(2,1)S(1)} %add_convert_fusion), channel_id=1, source_target_pairs={{0,3},{1,0},{2,1},{3,2},{4,7},{5,4},{6,5},{7,6},{8,11},{9,8},{10,9... | collective-permute-start | bytes 737288 | tf_op jit(solution)/shard_map/ppermute | solution.py:563
  130.4 11.0 %collective-permute-start.13 = (bf16[320,384]{1,0:T(8,128)(2,1)S(1)}, bf16[320,384]{1,0:T(8,128)(2,1)S(1)}, u32[]{:S(2)}, u32[]{:S(2)}) collective-permute-start(bf16[320,384]{1,0:T(8,128)(2,1)S(1)} %fusion), channel_id=1, source_target_pairs={{0,4},{1,5},{2,6},{3,7},{4,8},{5,9},{6,10},{7,11},{8,12},{9,13},{1... | collective-permute-start | bytes 737288 | tf_op jit(solution)/shard_map/ppermute | solution.py:563
  130.5 10.9 %collective-permute-start.14 = (bf16[320,384]{1,0:T(8,128)(2,1)S(1)}, bf16[320,384]{1,0:T(8,128)(2,1)S(1)}, u32[]{:S(2)}, u32[]{:S(2)}) collective-permute-start(bf16[320,384]{1,0:T(8,128)(2,1)S(1)} %fusion), channel_id=1, source_target_pairs={{0,8},{1,9},{2,10},{3,11},{4,12},{5,13},{6,14},{7,15},{8,0},{9,1},... | collective-permute-start | bytes 737288 | tf_op jit(solution)/shard_map/ppermute | solution.py:563
  132.1 9.6 %collective-permute-start.15 = (bf16[320,384]{1,0:T(8,128)(2,1)S(1)}, bf16[320,384]{1,0:T(8,128)(2,1)S(1)}, u32[]{:S(2)}, u32[]{:S(2)}) collective-permute-start(bf16[320,384]{1,0:T(8,128)(2,1)S(1)} %fusion), channel_id=1, source_target_pairs={{0,12},{1,13},{2,14},{3,15},{4,0},{5,1},{6,2},{7,3},{8,4},{9,5},{1... | collective-permute-start | bytes 737288 | tf_op jit(solution)/shard_map/ppermute | solution.py:563
  134.1 11.1 %collective-permute-start.28 = (bf16[320,128]{1,0:T(8,128)(2,1)S(1)}, bf16[320,128]{1,0:T(8,128)(2,1)S(1)}, u32[]{:S(2)}, u32[]{:S(2)}) collective-permute-start(bf16[320,128]{1,0:T(8,128)(2,1)S(1)} %add_convert_fusion.4), channel_id=1, source_target_pairs={{0,4},{1,5},{2,6},{3,7},{4,8},{5,9},{6,10},{7,11},{8,12},{9,13},{1... | collective-permute-start | bytes 245768 | tf_op jit(solution)/shard_map/ppermute | solution.py:563
  134.7 10.4 %collective-permute-start.29 = (bf16[320,128]{1,0:T(8,128)(2,1)S(1)}, bf16[320,128]{1,0:T(8,128)(2,1)S(1)}, u32[]{:S(2)}, u32[]{:S(2)}) collective-permute-start(bf16[320,128]{1,0:T(8,128)(2,1)S(1)} %add_convert_fusion.4), channel_id=1, source_target_pairs={{0,8},{1,9},{2,10},{3,11},{4,12},{5,13},{6,14},{7,15},{8,0},{9,1},... | collective-permute-start | bytes 245768 | tf_op jit(solution)/shard_map/ppermute | solution.py:563
  141.8 25.9 %collective-permute-start.16 = (bf16[1280,384]{1,0:T(8,128)(2,1)S(1)}, bf16[1280,384]{1,0:T(8,128)(2,1)S(1)}, u32[]{:S(2)}, u32[]{:S(2)}) collective-permute-start(bf16[1280,384]{1,0:T(8,128)(2,1)S(1)} %pad_maximum_fusion.ref.refs_0_), channel_id=1, source_target_pairs={{0,16},{1,17},{2,18},{3,19},{4,20},{5,21},{6,22},{7,23},{8,24},{9,... | collective-permute-start | bytes 2949128 | tf_op jit(solution)/shard_map/ppermute | solution.py:563
  141.9 25.9 %collective-permute-start.18 = (bf16[1280,384]{1,0:T(8,128)(2,1)S(1)}, bf16[1280,384]{1,0:T(8,128)(2,1)S(1)}, u32[]{:S(2)}, u32[]{:S(2)}) collective-permute-start(bf16[1280,384]{1,0:T(8,128)(2,1)S(1)} %pad_maximum_fusion.ref.refs_0_), channel_id=1, source_target_pairs={{0,48},{1,49},{2,50},{3,51},{4,52},{5,53},{6,54},{7,55},{8,56},{9,... | collective-permute-start | bytes 2949128 | tf_op jit(solution)/shard_map/ppermute | solution.py:563
  145.2 22.9 %collective-permute-start.17 = (bf16[1280,384]{1,0:T(8,128)(2,1)S(1)}, bf16[1280,384]{1,0:T(8,128)(2,1)S(1)}, u32[]{:S(2)}, u32[]{:S(2)}) collective-permute-start(bf16[1280,384]{1,0:T(8,128)(2,1)S(1)} %pad_maximum_fusion.ref.refs_0_), channel_id=1, source_target_pairs={{0,32},{1,33},{2,34},{3,35},{4,36},{5,37},{6,38},{7,39},{8,40},{9,... | collective-permute-start | bytes 2949128 | tf_op jit(solution)/shard_map/ppermute | solution.py:563
  146.8 9.2 %collective-permute-start.33 = (bf16[1280,128]{1,0:T(8,128)(2,1)S(1)}, bf16[1280,128]{1,0:T(8,128)(2,1)S(1)}, u32[]{:S(2)}, u32[]{:S(2)}) collective-permute-start(bf16[1280,128]{1,0:T(8,128)(2,1)S(1)} %pad_maximum_fusion.1.ref.refs_4_), channel_id=1, source_target_pairs={{0,3},{1,0},{2,1},{3,2},{4,7},{5,4},{6,5},{7,6},{8,11},{9,8},{10,9... | collective-permute-start | bytes 983048 | tf_op jit(solution)/shard_map/ppermute | solution.py:563
  147.7 11.2 %collective-permute-start.31 = (bf16[1280,128]{1,0:T(8,128)(2,1)S(1)}, bf16[1280,128]{1,0:T(8,128)(2,1)S(1)}, u32[]{:S(2)}, u32[]{:S(2)}) collective-permute-start(bf16[1280,128]{1,0:T(8,128)(2,1)S(1)} %pad_maximum_fusion.1.ref.refs_4_), channel_id=1, source_target_pairs={{0,1},{1,2},{2,3},{3,0},{4,5},{5,6},{6,7},{7,4},{8,9},{9,10},{10,1... | collective-permute-start | bytes 983048 | tf_op jit(solution)/shard_map/ppermute | solution.py:563
  156.1 11.9 %collective-permute-start.32 = (bf16[1280,128]{1,0:T(8,128)(2,1)S(1)}, bf16[1280,128]{1,0:T(8,128)(2,1)S(1)}, u32[]{:S(2)}, u32[]{:S(2)}) collective-permute-start(bf16[1280,128]{1,0:T(8,128)(2,1)S(1)} %pad_maximum_fusion.1.ref.refs_4_), channel_id=1, source_target_pairs={{0,2},{1,3},{2,0},{3,1},{4,6},{5,7},{6,4},{7,5},{8,10},{9,11},{10,... | collective-permute-start | bytes 983048 | tf_op jit(solution)/shard_map/ppermute | solution.py:563
  (7 other events, 71.0 us)

commit v4 on v3

--- a/solution.py
+++ b/solution.py
@@ -146,7 +146,7 @@
 def front(x, c, down, up, gain):
     lanes, rows, features = x.shape
     k = down.shape[2]
-    block = 1024
+    block = 1280
     steps = features // block
     total = lanes * rows
 
@@ -549,7 +549,7 @@
 
 
 MAJOR = ((0, 1, 2), (1, 2, 0))
-MINOR = ((2, 1, 0), (2, 0, 1))
+MINOR = ((2, 0, 1), (2, 0, 1))
 
 
 def hop(values, order, stage, by):

time: 173 us -> 171 us (0.988)
  waiting for transfers between devices: 40.6 us -> 35.2 us
  starting transfers between devices: 59.2 us -> 64 us
    ppermute x30, waiting for transfers between devices: 29.9 us -> 24.5 us  [hop(): return lax.ppermute(values, ('section', 'peer'), pairs)]
    ppermute x30, starting transfers between devices: 41.2 us -> 46 us  [hop(): return lax.ppermute(values, ('section', 'peer'), pairs)]
  transfers between devices with their start and end apart: 36 -> 36, of which waited for: 12 -> 11; matrix products, arithmetic and copies ran while one was open for 5% -> 5% of each run, Pallas kernels for 27% -> 27%
where the time goes in v4:
time: 171 us
  starting transfers between devices  64 us (37%)
  Pallas kernels  61 us (36%)
  waiting for transfers between devices  35.2 us (21%)
  other arithmetic  7.23 us (4%)
  local copies, waits for them, and re-layouts  1.98 us (1%)
    ppermute x30, starting transfers between devices, hop(): return lax.ppermute(values, ('section', 'peer'), pairs)  46 us
    ppermute x30, waiting for transfers between devices, hop(): return lax.ppermute(values, ('section', 'peer'), pairs)  24.5 us
    pallas_call x4, Pallas kernels, piece(): pl.pallas_call(kernel, in_specs=[pl.BlockSpec(memory_space=pltpu.SMEM)] +...  19.8 us
    pallas_call x1, Pallas kernels, prepare(): pl.pallas_call(kernel, grid_spec=pltpu.PrefetchScalarGridSpec(num_scalar_...  11.4 us
    all_to_all x1, starting transfers between devices, local(): lax.all_to_all(sent.reshape(rows, 8, 3 * k), ('section', 'peer'), 0, 0, t...  11.2 us
    pallas_call x1, Pallas kernels, front(): pl.pallas_call(kernel, grid=(steps,), in_specs=[pl.BlockSpec((lanes, rows...  10.1 us
    pallas_call x1, Pallas kernels, turn(): pl.pallas_call(kernel, grid=(features // block,), in_specs=[spec, spec],...  8.99 us
    all_to_all x1, waiting for transfers between devices, local(): lax.all_to_all(out.reshape(rows, 8, 3 * k), ('section', 'peer'), 0, 0, ti...  6.83 us
  transfers between devices with their start and end apart: 36, of which 11 were waited for; matrix products, arithmetic and copies ran while one was open for 5% of the time, Pallas kernels for 27%

profile of v4, /device:TPU:0, one launch (start us, length us, event | category | flops | bytes accessed | tf_op | source)
XLA Modules:
  0.0 170.6 jit_solution(14207536606320248810)
XLA Ops:
  1.3 10.1 %front.1 = bf16[1024,384]{1,0:T(8,128)(2,1)} custom-call(bf16[3,128,5120]{2,1,0:T(8,128)(2,1)} %bitcast.26, bf16[3,128,5120]{2,1,0:T(8,128)(2,1)} %bitcast.28, bf16[2,5120,128]{2,1,0:T(8,128)(2,1)} %bitcast.31, bf16[2,5120,128]{2,1,0:T(8,128)(2,1)} %bitcast.34, f32[2,5120]{1,0:T(2,128)} %bitcast.37), custom_call_target="tpu_custom_call" | custom-call | tf_op jit(solution)/shard_map/front/pallas_call | solution.py:196
  11.4 11.2 %all-to-all-start = ((bf16[128,8,384]{2,1,0:T(8,128)(2,1)}), bf16[128,8,384]{2,1,0:T(8,128)(2,1)S(1)}, u32[]{:S(2)}, u32[]{:S(2)}) async-start(bf16[128,8,384]{2,1,0:T(8,128)(2,1)} %bitcast.7), calls=%async_computation | async-start | bytes 1572864 | tf_op jit(solution)/shard_map/all_to_all | solution.py:604
  23.2 11.4 %prepare.1 = (bf16[5120,768]{1,0:T(8,128)(2,1)}, bf16[256,768]{1,0:T(8,128)(2,1)}, bf16[128,256]{1,0:T(8,128)(2,1)}) custom-call(s32[1]{0:T(128)} %bitcast.3.s_ref.mine, bf16[2,5120,128]{2,1,0:T(8,128)(2,1)} %bitcast.32, bf16[2,5120,128]{2,1,0:T(8,128)(2,1)} %bitcast.35, f32[2,5120]{1,0:T(2,128)} %bitcast.38, ...), custom_call_target="tpu_custom_call" | custom-call | tf_op jit(solution)/shard_map/prepare/pallas_call | solution.py:264
  34.6 3.8 %all-to-all-done = bf16[128,8,384]{2,1,0:T(8,128)(2,1)S(1)} async-done(((bf16[128,8,384]{2,1,0:T(8,128)(2,1)}), bf16[128,8,384]{2,1,0:T(8,128)(2,1)S(1)}, u32[]{:S(2)}, u32[]{:S(2)}) %all-to-all-start) | async-done | bytes 786464 | tf_op jit(solution)/shard_map/all_to_all | solution.py:604
  38.5 5.2 %meet.1 = (bf16[2,512,384]{2,1,0:T(8,128)(2,1)}, bf16[768,512]{1,0:T(8,128)(2,1)S(1)}, bf16[768,512]{1,0:T(8,128)(2,1)}) custom-call(s32[1]{0:T(128)} %bitcast.3.s_ref.mine, bf16[2,512,384]{2,1,0:T(8,128)(2,1)S(1)} %bitcast.24, s32[144,2]{1,0:T(8,128)S(1)} %copy.12.columns, s32[2,144]{1,0:T(2,128)S(1)} %multiply_add_fusion.rows, ...), custom_call_target="tpu_custom_call" | custom-call | tf_op jit(solution)/shard_map/meet/pallas_call | solution.py:378
  43.8 6.1 %all-to-all-start.1 = ((bf16[128,8,384]{2,1,0:T(8,128)(2,1)}), bf16[128,8,384]{2,1,0:T(8,128)(2,1)S(1)}, u32[]{:S(2)}, u32[]{:S(2)}) async-start(bf16[128,8,384]{2,1,0:T(8,128)(2,1)} %bitcast.11), calls=%async_computation.1 | async-start | bytes 1572864 | tf_op jit(solution)/shard_map/all_to_all | solution.py:618
  49.9 9.0 %turn.1.t_ref = bf16[5120,768]{1,0:T(8,128)(2,1)} custom-call(bf16[3,128,5120]{2,1,0:T(8,128)(2,1)} %bitcast.27, bf16[3,128,5120]{2,1,0:T(8,128)(2,1)} %bitcast.29), custom_call_target="tpu_custom_call" | custom-call | tf_op jit(solution)/shard_map/turn/pallas_call | solution.py:297
  58.9 6.8 %all-to-all-done.1 = bf16[128,8,384]{2,1,0:T(8,128)(2,1)S(1)} async-done(((bf16[128,8,384]{2,1,0:T(8,128)(2,1)}), bf16[128,8,384]{2,1,0:T(8,128)(2,1)S(1)}, u32[]{:S(2)}, u32[]{:S(2)}) %all-to-all-start.1) | async-done | bytes 786464 | tf_op jit(solution)/shard_map/all_to_all | solution.py:618
  67.9 5.2 %piece.4 = (bf16[1280,384]{1,0:T(8,128)(2,1)}, bf16[1280,128]{1,0:T(8,128)(2,1)S(1)}) custom-call(s32[1]{0:T(128)} %bitcast.at_ref, bf16[5120,768]{1,0:T(8,128)(2,1)} %turn.1.t_ref, bf16[5120,768]{1,0:T(8,128)(2,1)} %get-tuple-element.28.w_ref, bf16[384,512]{1,0:T(8,128)(2,1)S(1)} %get-tuple-element.31.xs_ref, ...), custom_call_target="tpu_custom_call" | custom-call | tf_op jit(solution)/shard_map/piece/pallas_call | solution.py:459
  74.6 5.2 %piece.5 = (bf16[1280,384]{1,0:T(8,128)(2,1)}, bf16[1280,128]{1,0:T(8,128)(2,1)S(1)}) custom-call(s32[1]{0:T(128)} %bitcast.13.at_ref, bf16[5120,768]{1,0:T(8,128)(2,1)} %turn.1.t_ref, bf16[5120,768]{1,0:T(8,128)(2,1)} %get-tuple-element.28.w_ref, bf16[384,512]{1,0:T(8,128)(2,1)S(1)} %get-tuple-element.31.xs_ref, ...), custom_call_target="tpu_custom_call" | custom-call | tf_op jit(solution)/shard_map/piece/pallas_call | solution.py:459
  79.8 5.2 %piece.6 = (bf16[1280,384]{1,0:T(8,128)(2,1)}, bf16[1280,128]{1,0:T(8,128)(2,1)S(1)}) custom-call(s32[1]{0:T(128)} %bitcast.14.at_ref, bf16[5120,768]{1,0:T(8,128)(2,1)} %turn.1.t_ref, bf16[5120,768]{1,0:T(8,128)(2,1)} %get-tuple-element.28.w_ref, bf16[384,512]{1,0:T(8,128)(2,1)S(1)} %get-tuple-element.31.xs_ref, ...), custom_call_target="tpu_custom_call" | custom-call | tf_op jit(solution)/shard_map/piece/pallas_call | solution.py:459
  85.9 2.4 %collective-permute-start.6 = (bf16[1280,384]{1,0:T(8,128)(2,1)}, bf16[1280,384]{1,0:T(8,128)(2,1)}, u32[]{:S(2)}, u32[]{:S(2)}) collective-permute-start(bf16[1280,384]{1,0:T(8,128)(2,1)} %get-tuple-element.36), channel_id=1, source_target_pairs={{0,48},{1,49},{2,50},{3,51},{4,52},{5,53},{6,54},{7,55},{8,56},{9,... | collective-permute-start | bytes 2949128 | tf_op jit(solution)/shard_map/ppermute | solution.py:563
  88.3 4.2 %piece.7 = (bf16[1280,384]{1,0:T(8,128)(2,1)S(1)}, bf16[1280,128]{1,0:T(8,128)(2,1)S(1)}) custom-call(s32[1]{0:T(128)} %bitcast.15.at_ref, bf16[5120,768]{1,0:T(8,128)(2,1)} %turn.1.t_ref, bf16[5120,768]{1,0:T(8,128)(2,1)} %get-tuple-element.28.w_ref, bf16[384,512]{1,0:T(8,128)(2,1)S(1)} %get-tuple-element.31.xs_ref, ...), custom_call_target="tpu_custom_call" | custom-call | tf_op jit(solution)/shard_map/piece/pallas_call | solution.py:459
  95.3 2.1 %collective-permute-start.21 = (bf16[1280,128]{1,0:T(8,128)(2,1)S(1)}, bf16[1280,128]{1,0:T(8,128)(2,1)S(1)}, u32[]{:S(2)}, u32[]{:S(2)}) collective-permute-start(bf16[1280,128]{1,0:T(8,128)(2,1)S(1)} %get-tuple-element.54), channel_id=1, source_target_pairs={{0,3},{1,0},{2,1},{3,2},{4,7},{5,4},{6,5},{7,6},{8,11},{9,8},{10,9... | collective-permute-start | bytes 983048 | tf_op jit(solution)/shard_map/ppermute | solution.py:563
  97.5 3.2 %collective-permute-done.5 = bf16[1280,384]{1,0:T(8,128)(2,1)} collective-permute-done((bf16[1280,384]{1,0:T(8,128)(2,1)}, bf16[1280,384]{1,0:T(8,128)(2,1)}, u32[]{:S(2)}, u32[]{:S(2)}) %collective-permute-start.5) | collective-permute-done | bytes 983072 | tf_op jit(solution)/shard_map/ppermute | solution.py:563
  100.7 2.8 %add_convert_fusion.3 = (bf16[320,384]{1,0:T(8,128)(2,1)}, bf16[320,384]{1,0:T(8,128)(2,1)}, bf16[320,384]{1,0:T(8,128)(2,1)}) fusion(bf16[1280,384]{1,0:T(8,128)(2,1)S(1)} %get-tuple-element.37, s32[]{:T(128)S(6)} %select_n.291, bf16[1280,384]{1,0:T(8,128)(2,1)} %collective-permute-done.6, bf16[1280,384]{1,0:T(8,128)(2,1)} %collective-permute-done.5, ...), kind=kLoop, calls=%fused_computation.6 | loop fusion | flops 2949120 | bytes 3686412 | tf_op jit(solution)/shard_map/convert_element_type | solution.py:577
  103.6 1.7 collective-permute-start.7
  106.4 2.1 %collective-permute-start.9 = (bf16[320,384]{1,0:T(8,128)(2,1)}, bf16[320,384]{1,0:T(8,128)(2,1)S(1)}, u32[]{:S(2)}, u32[]{:S(2)}) collective-permute-start(bf16[320,384]{1,0:T(8,128)(2,1)} %get-tuple-element.47), channel_id=1, source_target_pairs={{0,12},{1,13},{2,14},{3,15},{4,0},{5,1},{6,2},{7,3},{8,4},{9,5},{1... | collective-permute-start | bytes 737288 | tf_op jit(solution)/shard_map/ppermute | solution.py:563
  109.3 2.9 %collective-permute-done.20 = bf16[1280,128]{1,0:T(8,128)(2,1)S(1)} collective-permute-done((bf16[1280,128]{1,0:T(8,128)(2,1)S(1)}, bf16[1280,128]{1,0:T(8,128)(2,1)S(1)}, u32[]{:S(2)}, u32[]{:S(2)}) %collective-permute-start.20) | collective-permute-done | bytes 327712 | tf_op jit(solution)/shard_map/ppermute | solution.py:563
  114.1 3.0 %collective-permute-start.24 = (bf16[320,128]{1,0:T(8,128)(2,1)S(1)}, bf16[320,128]{1,0:T(8,128)(2,1)}, u32[]{:S(2)}, u32[]{:S(2)}) collective-permute-start(bf16[320,128]{1,0:T(8,128)(2,1)S(1)} %get-tuple-element.50), channel_id=1, source_target_pairs={{0,48},{1,49},{2,50},{3,51},{4,52},{5,53},{6,54},{7,55},{8,56},{9,... | collective-permute-start | bytes 245768 | tf_op jit(solution)/shard_map/ppermute | solution.py:563
  118.8 1.7 collective-permute-start.10
  120.7 3.0 %collective-permute-start.12 = (bf16[320,384]{1,0:T(8,128)(2,1)S(1)}, bf16[320,384]{1,0:T(8,128)(2,1)S(1)}, u32[]{:S(2)}, u32[]{:S(2)}) collective-permute-start(bf16[320,384]{1,0:T(8,128)(2,1)S(1)} %add_convert_fusion), channel_id=1, source_target_pairs={{0,3},{1,0},{2,1},{3,2},{4,7},{5,4},{6,5},{7,6},{8,11},{9,8},{10,9... | collective-permute-start | bytes 737288 | tf_op jit(solution)/shard_map/ppermute | solution.py:563
  126.7 2.4 %collective-permute-start.27 = (bf16[320,128]{1,0:T(8,128)(2,1)S(1)}, bf16[320,128]{1,0:T(8,128)(2,1)S(1)}, u32[]{:S(2)}, u32[]{:S(2)}) collective-permute-start(bf16[320,128]{1,0:T(8,128)(2,1)S(1)} %add_convert_fusion.5), channel_id=1, source_target_pairs={{0,12},{1,13},{2,14},{3,15},{4,0},{5,1},{6,2},{7,3},{8,4},{9,5},{1... | collective-permute-start | bytes 245768 | tf_op jit(solution)/shard_map/ppermute | solution.py:563
  129.7 1.6 collective-permute-start.14
  131.3 2.2 %collective-permute-start.15 = (bf16[320,384]{1,0:T(8,128)(2,1)S(1)}, bf16[320,384]{1,0:T(8,128)(2,1)S(1)}, u32[]{:S(2)}, u32[]{:S(2)}) collective-permute-start(bf16[320,384]{1,0:T(8,128)(2,1)S(1)} %fusion), channel_id=1, source_target_pairs={{0,12},{1,13},{2,14},{3,15},{4,0},{5,1},{6,2},{7,3},{8,4},{9,5},{1... | collective-permute-start | bytes 737288 | tf_op jit(solution)/shard_map/ppermute | solution.py:563
  133.7 3.1 %collective-permute-start.29 = (bf16[320,128]{1,0:T(8,128)(2,1)S(1)}, bf16[320,128]{1,0:T(8,128)(2,1)S(1)}, u32[]{:S(2)}, u32[]{:S(2)}) collective-permute-start(bf16[320,128]{1,0:T(8,128)(2,1)S(1)} %add_convert_fusion.4), channel_id=1, source_target_pairs={{0,32},{1,33},{2,34},{3,35},{4,36},{5,37},{6,38},{7,39},{8,40},{9,... | collective-permute-start | bytes 245768 | tf_op jit(solution)/shard_map/ppermute | solution.py:563
  136.8 2.8 %collective-permute-done.13 = bf16[320,384]{1,0:T(8,128)(2,1)S(1)} collective-permute-done((bf16[320,384]{1,0:T(8,128)(2,1)S(1)}, bf16[320,384]{1,0:T(8,128)(2,1)S(1)}, u32[]{:S(2)}, u32[]{:S(2)}) %collective-permute-start.13) | collective-permute-done | bytes 245792 | tf_op jit(solution)/shard_map/ppermute | solution.py:563
  141.9 2.1 %collective-permute-start.18 = (bf16[1280,384]{1,0:T(8,128)(2,1)S(1)}, bf16[1280,384]{1,0:T(8,128)(2,1)S(1)}, u32[]{:S(2)}, u32[]{:S(2)}) collective-permute-start(bf16[1280,384]{1,0:T(8,128)(2,1)S(1)} %pad_maximum_fusion.ref.refs_0_), channel_id=1, source_target_pairs={{0,48},{1,49},{2,50},{3,51},{4,52},{5,53},{6,54},{7,55},{8,56},{9,... | collective-permute-start | bytes 2949128 | tf_op jit(solution)/shard_map/ppermute | solution.py:563
  146.8 5.3 %collective-permute-done.33.ref.refs_7_ = bf16[1280,128]{1,0:T(8,128)(2,1)S(1)} collective-permute-done((bf16[1280,128]{1,0:T(8,128)(2,1)S(1)}, bf16[1280,128]{1,0:T(8,128)(2,1)S(1)}, u32[]{:S(2)}, u32[]{:S(2)}) %collective-permute-start.33) | collective-permute-done | bytes 327712 | tf_op jit(solution)/shard_map/ppermute | solution.py:563
  152.1 4.5 %collective-permute-start.32 = (bf16[1280,128]{1,0:T(8,128)(2,1)S(1)}, bf16[1280,128]{1,0:T(8,128)(2,1)S(1)}, u32[]{:S(2)}, u32[]{:S(2)}) collective-permute-start(bf16[1280,128]{1,0:T(8,128)(2,1)S(1)} %pad_maximum_fusion.1.ref.refs_4_), channel_id=1, source_target_pairs={{0,2},{1,3},{2,0},{3,1},{4,6},{5,7},{6,4},{7,5},{8,10},{9,11},{10,... | collective-permute-start | bytes 983048 | tf_op jit(solution)/shard_map/ppermute | solution.py:563
  158.2 8.4 %collective-permute-done.16.ref.refs_1_ = bf16[1280,384]{1,0:T(8,128)(2,1)S(1)} collective-permute-done((bf16[1280,384]{1,0:T(8,128)(2,1)S(1)}, bf16[1280,384]{1,0:T(8,128)(2,1)S(1)}, u32[]{:S(2)}, u32[]{:S(2)}) %collective-permute-start.16) | collective-permute-done | bytes 983072 | tf_op jit(solution)/shard_map/ppermute | solution.py:563
  166.9 3.5 %finish.1 = (bf16[2,5120,128]{2,1,0:T(8,128)(2,1)}, bf16[2,5120,128]{2,1,0:T(8,128)(2,1)}) custom-call(s32[2,4,4]{2,1,0:T(4,128)S(1)} %pad_add_fusion.at, bf16[1280,384]{1,0:T(8,128)(2,1)S(1)} %pad_maximum_fusion.ref.refs_0_, bf16[1280,384]{1,0:T(8,128)(2,1)S(1)} %collective-permute-done.16.ref.refs_1_, ...), custom_call_target="tpu_custom_call" | custom-call | tf_op jit(solution)/shard_map/finish/pallas_call | solution.py:533
  (91 shorter events, 24.9 us)
Async XLA Ops:
  0.6 22.6 %collective-permute-start = (bf16[2,5120,128]{2,1,0:T(8,128)(2,1)}, bf16[2,5120,128]{2,1,0:T(8,128)(2,1)S(1)}, u32[]{:S(2)}, u32[]{:S(2)}) collective-permute-start(bf16[2,5120,128]{2,1,0:T(8,128)(2,1)} %bitcast.30), channel_id=1, source_target_pairs={{0,64},{64,0},{1,65},{65,1},{2,66},{66,2},{3,67},{67,3},{4,68},{68... | collective-permute-start | bytes 7864328 | tf_op jit(solution)/shard_map/ppermute | solution.py:600
  0.7 22.5 %collective-permute-start.1 = (bf16[2,5120,128]{2,1,0:T(8,128)(2,1)}, bf16[2,5120,128]{2,1,0:T(8,128)(2,1)}, u32[]{:S(2)}, u32[]{:S(2)}) collective-permute-start(bf16[2,5120,128]{2,1,0:T(8,128)(2,1)} %bitcast.33), channel_id=1, source_target_pairs={{0,64},{64,0},{1,65},{65,1},{2,66},{66,2},{3,67},{67,3},{4,68},{68... | collective-permute-start | bytes 7864328 | tf_op jit(solution)/shard_map/ppermute | solution.py:601
  1.2 21.9 %collective-permute-start.2 = (f32[2,5120]{1,0:T(2,128)}, f32[2,5120]{1,0:T(2,128)S(1)}, u32[]{:S(2)}, u32[]{:S(2)}) collective-permute-start(f32[2,5120]{1,0:T(2,128)} %bitcast.36), channel_id=1, source_target_pairs={{0,64},{64,0},{1,65},{65,1},{2,66},{66,2},{3,67},{67,3},{4,68},{68... | collective-permute-start | bytes 122888 | tf_op jit(solution)/shard_map/ppermute | solution.py:602
  11.4 27.1 %all-to-all-start = ((bf16[128,8,384]{2,1,0:T(8,128)(2,1)}), bf16[128,8,384]{2,1,0:T(8,128)(2,1)S(1)}, u32[]{:S(2)}, u32[]{:S(2)}) async-start(bf16[128,8,384]{2,1,0:T(8,128)(2,1)} %bitcast.7), calls=%async_computation | async-start | bytes 1572864 | tf_op jit(solution)/shard_map/all_to_all | solution.py:604
  43.7 22.1 %collective-permute-start.3 = (bf16[768,512]{1,0:T(8,128)(2,1)}, bf16[768,512]{1,0:T(8,128)(2,1)S(1)}, u32[]{:S(2)}, u32[]{:S(2)}) collective-permute-start(bf16[768,512]{1,0:T(8,128)(2,1)} %get-tuple-element.30), channel_id=1, source_target_pairs={{0,64},{64,0},{1,65},{65,1},{2,66},{66,2},{3,67},{67,3},{4,68},{68... | collective-permute-start | bytes 2359304 | tf_op jit(solution)/shard_map/ppermute | solution.py:617
  43.8 22.0 %all-to-all-start.1 = ((bf16[128,8,384]{2,1,0:T(8,128)(2,1)}), bf16[128,8,384]{2,1,0:T(8,128)(2,1)S(1)}, u32[]{:S(2)}, u32[]{:S(2)}) async-start(bf16[128,8,384]{2,1,0:T(8,128)(2,1)} %bitcast.11), calls=%async_computation.1 | async-start | bytes 1572864 | tf_op jit(solution)/shard_map/all_to_all | solution.py:618
  73.2 22.2 %collective-permute-start.4 = (bf16[1280,384]{1,0:T(8,128)(2,1)}, bf16[1280,384]{1,0:T(8,128)(2,1)}, u32[]{:S(2)}, u32[]{:S(2)}) collective-permute-start(bf16[1280,384]{1,0:T(8,128)(2,1)} %get-tuple-element.34), channel_id=1, source_target_pairs={{0,32},{1,33},{2,34},{3,35},{4,36},{5,37},{6,38},{7,39},{8,40},{9,... | collective-permute-start | bytes 2949128 | tf_op jit(solution)/shard_map/ppermute | solution.py:563
  85.0 15.7 %collective-permute-start.5 = (bf16[1280,384]{1,0:T(8,128)(2,1)}, bf16[1280,384]{1,0:T(8,128)(2,1)}, u32[]{:S(2)}, u32[]{:S(2)}) collective-permute-start(bf16[1280,384]{1,0:T(8,128)(2,1)} %get-tuple-element.35), channel_id=1, source_target_pairs={{0,16},{1,17},{2,18},{3,19},{4,20},{5,21},{6,22},{7,23},{8,24},{9,... | collective-permute-start | bytes 2949128 | tf_op jit(solution)/shard_map/ppermute | solution.py:563
  85.9 14.8 %collective-permute-start.6 = (bf16[1280,384]{1,0:T(8,128)(2,1)}, bf16[1280,384]{1,0:T(8,128)(2,1)}, u32[]{:S(2)}, u32[]{:S(2)}) collective-permute-start(bf16[1280,384]{1,0:T(8,128)(2,1)} %get-tuple-element.36), channel_id=1, source_target_pairs={{0,48},{1,49},{2,50},{3,51},{4,52},{5,53},{6,54},{7,55},{8,56},{9,... | collective-permute-start | bytes 2949128 | tf_op jit(solution)/shard_map/ppermute | solution.py:563
  92.8 13.7 %collective-permute-start.19 = (bf16[1280,128]{1,0:T(8,128)(2,1)S(1)}, bf16[1280,128]{1,0:T(8,128)(2,1)S(1)}, u32[]{:S(2)}, u32[]{:S(2)}) collective-permute-start(bf16[1280,128]{1,0:T(8,128)(2,1)S(1)} %get-tuple-element.52), channel_id=1, source_target_pairs={{0,2},{1,3},{2,0},{3,1},{4,6},{5,7},{6,4},{7,5},{8,10},{9,11},{10,... | collective-permute-start | bytes 983048 | tf_op jit(solution)/shard_map/ppermute | solution.py:563
  94.2 17.9 %collective-permute-start.20 = (bf16[1280,128]{1,0:T(8,128)(2,1)S(1)}, bf16[1280,128]{1,0:T(8,128)(2,1)S(1)}, u32[]{:S(2)}, u32[]{:S(2)}) collective-permute-start(bf16[1280,128]{1,0:T(8,128)(2,1)S(1)} %get-tuple-element.55), channel_id=1, source_target_pairs={{0,1},{1,2},{2,3},{3,0},{4,5},{5,6},{6,7},{7,4},{8,9},{9,10},{10,1... | collective-permute-start | bytes 983048 | tf_op jit(solution)/shard_map/ppermute | solution.py:563
  95.3 16.8 %collective-permute-start.21 = (bf16[1280,128]{1,0:T(8,128)(2,1)S(1)}, bf16[1280,128]{1,0:T(8,128)(2,1)S(1)}, u32[]{:S(2)}, u32[]{:S(2)}) collective-permute-start(bf16[1280,128]{1,0:T(8,128)(2,1)S(1)} %get-tuple-element.54), channel_id=1, source_target_pairs={{0,3},{1,0},{2,1},{3,2},{4,7},{5,4},{6,5},{7,6},{8,11},{9,8},{10,9... | collective-permute-start | bytes 983048 | tf_op jit(solution)/shard_map/ppermute | solution.py:563
  103.6 10.6 %collective-permute-start.7 = (bf16[320,384]{1,0:T(8,128)(2,1)}, bf16[320,384]{1,0:T(8,128)(2,1)}, u32[]{:S(2)}, u32[]{:S(2)}) collective-permute-start(bf16[320,384]{1,0:T(8,128)(2,1)} %get-tuple-element.46), channel_id=1, source_target_pairs={{0,8},{1,9},{2,10},{3,11},{4,12},{5,13},{6,14},{7,15},{8,0},{9,1},... | collective-permute-start | bytes 737288 | tf_op jit(solution)/shard_map/ppermute | solution.py:563
  105.3 11.9 %collective-permute-start.8 = (bf16[320,384]{1,0:T(8,128)(2,1)}, bf16[320,384]{1,0:T(8,128)(2,1)}, u32[]{:S(2)}, u32[]{:S(2)}) collective-permute-start(bf16[320,384]{1,0:T(8,128)(2,1)} %get-tuple-element.48), channel_id=1, source_target_pairs={{0,4},{1,5},{2,6},{3,7},{4,8},{5,9},{6,10},{7,11},{8,12},{9,13},{1... | collective-permute-start | bytes 737288 | tf_op jit(solution)/shard_map/ppermute | solution.py:563
  106.4 10.8 %collective-permute-start.9 = (bf16[320,384]{1,0:T(8,128)(2,1)}, bf16[320,384]{1,0:T(8,128)(2,1)S(1)}, u32[]{:S(2)}, u32[]{:S(2)}) collective-permute-start(bf16[320,384]{1,0:T(8,128)(2,1)} %get-tuple-element.47), channel_id=1, source_target_pairs={{0,12},{1,13},{2,14},{3,15},{4,0},{5,1},{6,2},{7,3},{8,4},{9,5},{1... | collective-permute-start | bytes 737288 | tf_op jit(solution)/shard_map/ppermute | solution.py:563
  112.9 7.8 %collective-permute-start.22 = (bf16[320,128]{1,0:T(8,128)(2,1)S(1)}, bf16[320,128]{1,0:T(8,128)(2,1)S(1)}, u32[]{:S(2)}, u32[]{:S(2)}) collective-permute-start(bf16[320,128]{1,0:T(8,128)(2,1)S(1)} %get-tuple-element.49), channel_id=1, source_target_pairs={{0,32},{1,33},{2,34},{3,35},{4,36},{5,37},{6,38},{7,39},{8,40},{9,... | collective-permute-start | bytes 245768 | tf_op jit(solution)/shard_map/ppermute | solution.py:563
  113.9 9.8 %collective-permute-start.23 = (bf16[320,128]{1,0:T(8,128)(2,1)}, bf16[320,128]{1,0:T(8,128)(2,1)S(1)}, u32[]{:S(2)}, u32[]{:S(2)}) collective-permute-start(bf16[320,128]{1,0:T(8,128)(2,1)} %get-tuple-element.51), channel_id=1, source_target_pairs={{0,16},{1,17},{2,18},{3,19},{4,20},{5,21},{6,22},{7,23},{8,24},{9,... | collective-permute-start | bytes 245768 | tf_op jit(solution)/shard_map/ppermute | solution.py:563
  114.1 9.6 %collective-permute-start.24 = (bf16[320,128]{1,0:T(8,128)(2,1)S(1)}, bf16[320,128]{1,0:T(8,128)(2,1)}, u32[]{:S(2)}, u32[]{:S(2)}) collective-permute-start(bf16[320,128]{1,0:T(8,128)(2,1)S(1)} %get-tuple-element.50), channel_id=1, source_target_pairs={{0,48},{1,49},{2,50},{3,51},{4,52},{5,53},{6,54},{7,55},{8,56},{9,... | collective-permute-start | bytes 245768 | tf_op jit(solution)/shard_map/ppermute | solution.py:563
  118.8 7.9 %collective-permute-start.10 = (bf16[320,384]{1,0:T(8,128)(2,1)S(1)}, bf16[320,384]{1,0:T(8,128)(2,1)S(1)}, u32[]{:S(2)}, u32[]{:S(2)}) collective-permute-start(bf16[320,384]{1,0:T(8,128)(2,1)S(1)} %add_convert_fusion), channel_id=1, source_target_pairs={{0,2},{1,3},{2,0},{3,1},{4,6},{5,7},{6,4},{7,5},{8,10},{9,11},{10,... | collective-permute-start | bytes 737288 | tf_op jit(solution)/shard_map/ppermute | solution.py:563
  120.5 8.7 %collective-permute-start.11 = (bf16[320,384]{1,0:T(8,128)(2,1)S(1)}, bf16[320,384]{1,0:T(8,128)(2,1)S(1)}, u32[]{:S(2)}, u32[]{:S(2)}) collective-permute-start(bf16[320,384]{1,0:T(8,128)(2,1)S(1)} %add_convert_fusion), channel_id=1, source_target_pairs={{0,1},{1,2},{2,3},{3,0},{4,5},{5,6},{6,7},{7,4},{8,9},{9,10},{10,1... | collective-permute-start | bytes 737288 | tf_op jit(solution)/shard_map/ppermute | solution.py:563
  120.7 8.5 %collective-permute-start.12 = (bf16[320,384]{1,0:T(8,128)(2,1)S(1)}, bf16[320,384]{1,0:T(8,128)(2,1)S(1)}, u32[]{:S(2)}, u32[]{:S(2)}) collective-permute-start(bf16[320,384]{1,0:T(8,128)(2,1)S(1)} %add_convert_fusion), channel_id=1, source_target_pairs={{0,3},{1,0},{2,1},{3,2},{4,7},{5,4},{6,5},{7,6},{8,11},{9,8},{10,9... | collective-permute-start | bytes 737288 | tf_op jit(solution)/shard_map/ppermute | solution.py:563
  125.9 7.6 %collective-permute-start.26 = (bf16[320,128]{1,0:T(8,128)(2,1)S(1)}, bf16[320,128]{1,0:T(8,128)(2,1)S(1)}, u32[]{:S(2)}, u32[]{:S(2)}) collective-permute-start(bf16[320,128]{1,0:T(8,128)(2,1)S(1)} %add_convert_fusion.5), channel_id=1, source_target_pairs={{0,4},{1,5},{2,6},{3,7},{4,8},{5,9},{6,10},{7,11},{8,12},{9,13},{1... | collective-permute-start | bytes 245768 | tf_op jit(solution)/shard_map/ppermute | solution.py:563
  129.6 10.1 %collective-permute-start.13 = (bf16[320,384]{1,0:T(8,128)(2,1)S(1)}, bf16[320,384]{1,0:T(8,128)(2,1)S(1)}, u32[]{:S(2)}, u32[]{:S(2)}) collective-permute-start(bf16[320,384]{1,0:T(8,128)(2,1)S(1)} %fusion), channel_id=1, source_target_pairs={{0,4},{1,5},{2,6},{3,7},{4,8},{5,9},{6,10},{7,11},{8,12},{9,13},{1... | collective-permute-start | bytes 737288 | tf_op jit(solution)/shard_map/ppermute | solution.py:563
  129.7 10.8 %collective-permute-start.14 = (bf16[320,384]{1,0:T(8,128)(2,1)S(1)}, bf16[320,384]{1,0:T(8,128)(2,1)S(1)}, u32[]{:S(2)}, u32[]{:S(2)}) collective-permute-start(bf16[320,384]{1,0:T(8,128)(2,1)S(1)} %fusion), channel_id=1, source_target_pairs={{0,8},{1,9},{2,10},{3,11},{4,12},{5,13},{6,14},{7,15},{8,0},{9,1},... | collective-permute-start | bytes 737288 | tf_op jit(solution)/shard_map/ppermute | solution.py:563
  131.3 9.3 %collective-permute-start.15 = (bf16[320,384]{1,0:T(8,128)(2,1)S(1)}, bf16[320,384]{1,0:T(8,128)(2,1)S(1)}, u32[]{:S(2)}, u32[]{:S(2)}) collective-permute-start(bf16[320,384]{1,0:T(8,128)(2,1)S(1)} %fusion), channel_id=1, source_target_pairs={{0,12},{1,13},{2,14},{3,15},{4,0},{5,1},{6,2},{7,3},{8,4},{9,5},{1... | collective-permute-start | bytes 737288 | tf_op jit(solution)/shard_map/ppermute | solution.py:563
  133.5 10.5 %collective-permute-start.28 = (bf16[320,128]{1,0:T(8,128)(2,1)S(1)}, bf16[320,128]{1,0:T(8,128)(2,1)S(1)}, u32[]{:S(2)}, u32[]{:S(2)}) collective-permute-start(bf16[320,128]{1,0:T(8,128)(2,1)S(1)} %add_convert_fusion.4), channel_id=1, source_target_pairs={{0,16},{1,17},{2,18},{3,19},{4,20},{5,21},{6,22},{7,23},{8,24},{9,... | collective-permute-start | bytes 245768 | tf_op jit(solution)/shard_map/ppermute | solution.py:563
  133.7 10.8 %collective-permute-start.29 = (bf16[320,128]{1,0:T(8,128)(2,1)S(1)}, bf16[320,128]{1,0:T(8,128)(2,1)S(1)}, u32[]{:S(2)}, u32[]{:S(2)}) collective-permute-start(bf16[320,128]{1,0:T(8,128)(2,1)S(1)} %add_convert_fusion.4), channel_id=1, source_target_pairs={{0,32},{1,33},{2,34},{3,35},{4,36},{5,37},{6,38},{7,39},{8,40},{9,... | collective-permute-start | bytes 245768 | tf_op jit(solution)/shard_map/ppermute | solution.py:563
  140.7 25.9 %collective-permute-start.16 = (bf16[1280,384]{1,0:T(8,128)(2,1)S(1)}, bf16[1280,384]{1,0:T(8,128)(2,1)S(1)}, u32[]{:S(2)}, u32[]{:S(2)}) collective-permute-start(bf16[1280,384]{1,0:T(8,128)(2,1)S(1)} %pad_maximum_fusion.ref.refs_0_), channel_id=1, source_target_pairs={{0,16},{1,17},{2,18},{3,19},{4,20},{5,21},{6,22},{7,23},{8,24},{9,... | collective-permute-start | bytes 2949128 | tf_op jit(solution)/shard_map/ppermute | solution.py:563
  141.9 24.8 %collective-permute-start.18 = (bf16[1280,384]{1,0:T(8,128)(2,1)S(1)}, bf16[1280,384]{1,0:T(8,128)(2,1)S(1)}, u32[]{:S(2)}, u32[]{:S(2)}) collective-permute-start(bf16[1280,384]{1,0:T(8,128)(2,1)S(1)} %pad_maximum_fusion.ref.refs_0_), channel_id=1, source_target_pairs={{0,48},{1,49},{2,50},{3,51},{4,52},{5,53},{6,54},{7,55},{8,56},{9,... | collective-permute-start | bytes 2949128 | tf_op jit(solution)/shard_map/ppermute | solution.py:563
  144.0 22.9 %collective-permute-start.17 = (bf16[1280,384]{1,0:T(8,128)(2,1)S(1)}, bf16[1280,384]{1,0:T(8,128)(2,1)S(1)}, u32[]{:S(2)}, u32[]{:S(2)}) collective-permute-start(bf16[1280,384]{1,0:T(8,128)(2,1)S(1)} %pad_maximum_fusion.ref.refs_0_), channel_id=1, source_target_pairs={{0,32},{1,33},{2,34},{3,35},{4,36},{5,37},{6,38},{7,39},{8,40},{9,... | collective-permute-start | bytes 2949128 | tf_op jit(solution)/shard_map/ppermute | solution.py:563
  146.3 11.8 %collective-permute-start.31 = (bf16[1280,128]{1,0:T(8,128)(2,1)S(1)}, bf16[1280,128]{1,0:T(8,128)(2,1)S(1)}, u32[]{:S(2)}, u32[]{:S(2)}) collective-permute-start(bf16[1280,128]{1,0:T(8,128)(2,1)S(1)} %pad_maximum_fusion.1.ref.refs_4_), channel_id=1, source_target_pairs={{0,1},{1,2},{2,3},{3,0},{4,5},{5,6},{6,7},{7,4},{8,9},{9,10},{10,1... | collective-permute-start | bytes 983048 | tf_op jit(solution)/shard_map/ppermute | solution.py:563
  152.1 14.8 %collective-permute-start.32 = (bf16[1280,128]{1,0:T(8,128)(2,1)S(1)}, bf16[1280,128]{1,0:T(8,128)(2,1)S(1)}, u32[]{:S(2)}, u32[]{:S(2)}) collective-permute-start(bf16[1280,128]{1,0:T(8,128)(2,1)S(1)} %pad_maximum_fusion.1.ref.refs_4_), channel_id=1, source_target_pairs={{0,2},{1,3},{2,0},{3,1},{4,6},{5,7},{6,4},{7,5},{8,10},{9,11},{10,... | collective-permute-start | bytes 983048 | tf_op jit(solution)/shard_map/ppermute | solution.py:563
  (7 other events, 69.4 us)

commit v5 on v4

--- a/solution.py
+++ b/solution.py
@@ -42,7 +42,7 @@
     k = cot[0].shape[1]
 
     def activated(pre):
-        r = lax.rsqrt(square_sum * (1.0 / feature_count) + norm_eps)
+        r = lax.rsqrt(jnp.maximum(square_sum, 0.0) * (1.0 / feature_count) + norm_eps)
         h = r * pre
         return r, h, (h * jax.nn.sigmoid(h)).astype(bf16)
 

time: 171 us -> 171 us (level)
  no operation moved by 1% of the time
where the time goes in v5:
time: 171 us
  starting transfers between devices  63.6 us (37%)
  Pallas kernels  61 us (36%)
  waiting for transfers between devices  35.5 us (21%)
  other arithmetic  7.23 us (4%)
  local copies, waits for them, and re-layouts  1.98 us (1%)
    ppermute x30, starting transfers between devices, hop(): return lax.ppermute(values, ('section', 'peer'), pairs)  45.6 us
    ppermute x30, waiting for transfers between devices, hop(): return lax.ppermute(values, ('section', 'peer'), pairs)  24.8 us
    pallas_call x4, Pallas kernels, piece(): pl.pallas_call(kernel, in_specs=[pl.BlockSpec(memory_space=pltpu.SMEM)] +...  19.9 us
    pallas_call x1, Pallas kernels, prepare(): pl.pallas_call(kernel, grid_spec=pltpu.PrefetchScalarGridSpec(num_scalar_...  11.4 us
    all_to_all x1, starting transfers between devices, local(): lax.all_to_all(sent.reshape(rows, 8, 3 * k), ('section', 'peer'), 0, 0, t...  11.2 us
    pallas_call x1, Pallas kernels, front(): pl.pallas_call(kernel, grid=(steps,), in_specs=[pl.BlockSpec((lanes, rows...  10.1 us
    pallas_call x1, Pallas kernels, turn(): pl.pallas_call(kernel, grid=(features // block,), in_specs=[spec, spec],...  8.99 us
    all_to_all x1, waiting for transfers between devices, local(): lax.all_to_all(out.reshape(rows, 8, 3 * k), ('section', 'peer'), 0, 0, ti...  6.83 us
  transfers between devices with their start and end apart: 36, of which 11 were waited for; matrix products, arithmetic and copies ran while one was open for 5% of the time, Pallas kernels for 27%

profile of v5, /device:TPU:0, one launch (start us, length us, event | category | flops | bytes accessed | tf_op | source)
XLA Modules:
  0.0 170.6 jit_solution(4563723711723237899)
XLA Ops:
  1.3 10.1 %front.1 = bf16[1024,384]{1,0:T(8,128)(2,1)} custom-call(bf16[3,128,5120]{2,1,0:T(8,128)(2,1)} %bitcast.26, bf16[3,128,5120]{2,1,0:T(8,128)(2,1)} %bitcast.28, bf16[2,5120,128]{2,1,0:T(8,128)(2,1)} %bitcast.31, bf16[2,5120,128]{2,1,0:T(8,128)(2,1)} %bitcast.34, f32[2,5120]{1,0:T(2,128)} %bitcast.37), custom_call_target="tpu_custom_call" | custom-call | tf_op jit(solution)/shard_map/front/pallas_call | solution.py:196
  11.4 11.2 %all-to-all-start = ((bf16[128,8,384]{2,1,0:T(8,128)(2,1)}), bf16[128,8,384]{2,1,0:T(8,128)(2,1)S(1)}, u32[]{:S(2)}, u32[]{:S(2)}) async-start(bf16[128,8,384]{2,1,0:T(8,128)(2,1)} %bitcast.7), calls=%async_computation | async-start | bytes 1572864 | tf_op jit(solution)/shard_map/all_to_all | solution.py:604
  23.2 11.4 %prepare.1 = (bf16[5120,768]{1,0:T(8,128)(2,1)}, bf16[256,768]{1,0:T(8,128)(2,1)}, bf16[128,256]{1,0:T(8,128)(2,1)}) custom-call(s32[1]{0:T(128)} %bitcast.3.s_ref.mine, bf16[2,5120,128]{2,1,0:T(8,128)(2,1)} %bitcast.32, bf16[2,5120,128]{2,1,0:T(8,128)(2,1)} %bitcast.35, f32[2,5120]{1,0:T(2,128)} %bitcast.38, ...), custom_call_target="tpu_custom_call" | custom-call | tf_op jit(solution)/shard_map/prepare/pallas_call | solution.py:264
  34.6 3.8 %all-to-all-done = bf16[128,8,384]{2,1,0:T(8,128)(2,1)S(1)} async-done(((bf16[128,8,384]{2,1,0:T(8,128)(2,1)}), bf16[128,8,384]{2,1,0:T(8,128)(2,1)S(1)}, u32[]{:S(2)}, u32[]{:S(2)}) %all-to-all-start) | async-done | bytes 786464 | tf_op jit(solution)/shard_map/all_to_all | solution.py:604
  38.5 5.2 %meet.1 = (bf16[2,512,384]{2,1,0:T(8,128)(2,1)}, bf16[768,512]{1,0:T(8,128)(2,1)S(1)}, bf16[768,512]{1,0:T(8,128)(2,1)}) custom-call(s32[1]{0:T(128)} %bitcast.3.s_ref.mine, bf16[2,512,384]{2,1,0:T(8,128)(2,1)S(1)} %bitcast.24, s32[144,2]{1,0:T(8,128)S(1)} %copy.12.columns, s32[2,144]{1,0:T(2,128)S(1)} %multiply_add_fusion.rows, ...), custom_call_target="tpu_custom_call" | custom-call | tf_op jit(solution)/shard_map/meet/pallas_call | solution.py:378
  43.8 6.1 %all-to-all-start.1 = ((bf16[128,8,384]{2,1,0:T(8,128)(2,1)}), bf16[128,8,384]{2,1,0:T(8,128)(2,1)S(1)}, u32[]{:S(2)}, u32[]{:S(2)}) async-start(bf16[128,8,384]{2,1,0:T(8,128)(2,1)} %bitcast.11), calls=%async_computation.1 | async-start | bytes 1572864 | tf_op jit(solution)/shard_map/all_to_all | solution.py:618
  49.9 9.0 %turn.1.t_ref = bf16[5120,768]{1,0:T(8,128)(2,1)} custom-call(bf16[3,128,5120]{2,1,0:T(8,128)(2,1)} %bitcast.27, bf16[3,128,5120]{2,1,0:T(8,128)(2,1)} %bitcast.29), custom_call_target="tpu_custom_call" | custom-call | tf_op jit(solution)/shard_map/turn/pallas_call | solution.py:297
  58.9 6.8 %all-to-all-done.1 = bf16[128,8,384]{2,1,0:T(8,128)(2,1)S(1)} async-done(((bf16[128,8,384]{2,1,0:T(8,128)(2,1)}), bf16[128,8,384]{2,1,0:T(8,128)(2,1)S(1)}, u32[]{:S(2)}, u32[]{:S(2)}) %all-to-all-start.1) | async-done | bytes 786464 | tf_op jit(solution)/shard_map/all_to_all | solution.py:618
  67.9 5.2 %piece.4 = (bf16[1280,384]{1,0:T(8,128)(2,1)}, bf16[1280,128]{1,0:T(8,128)(2,1)S(1)}) custom-call(s32[1]{0:T(128)} %bitcast.at_ref, bf16[5120,768]{1,0:T(8,128)(2,1)} %turn.1.t_ref, bf16[5120,768]{1,0:T(8,128)(2,1)} %get-tuple-element.28.w_ref, bf16[384,512]{1,0:T(8,128)(2,1)S(1)} %get-tuple-element.31.xs_ref, ...), custom_call_target="tpu_custom_call" | custom-call | tf_op jit(solution)/shard_map/piece/pallas_call | solution.py:459
  74.6 5.2 %piece.5 = (bf16[1280,384]{1,0:T(8,128)(2,1)}, bf16[1280,128]{1,0:T(8,128)(2,1)S(1)}) custom-call(s32[1]{0:T(128)} %bitcast.13.at_ref, bf16[5120,768]{1,0:T(8,128)(2,1)} %turn.1.t_ref, bf16[5120,768]{1,0:T(8,128)(2,1)} %get-tuple-element.28.w_ref, bf16[384,512]{1,0:T(8,128)(2,1)S(1)} %get-tuple-element.31.xs_ref, ...), custom_call_target="tpu_custom_call" | custom-call | tf_op jit(solution)/shard_map/piece/pallas_call | solution.py:459
  79.8 5.2 %piece.6 = (bf16[1280,384]{1,0:T(8,128)(2,1)}, bf16[1280,128]{1,0:T(8,128)(2,1)S(1)}) custom-call(s32[1]{0:T(128)} %bitcast.14.at_ref, bf16[5120,768]{1,0:T(8,128)(2,1)} %turn.1.t_ref, bf16[5120,768]{1,0:T(8,128)(2,1)} %get-tuple-element.28.w_ref, bf16[384,512]{1,0:T(8,128)(2,1)S(1)} %get-tuple-element.31.xs_ref, ...), custom_call_target="tpu_custom_call" | custom-call | tf_op jit(solution)/shard_map/piece/pallas_call | solution.py:459
  85.9 2.4 %collective-permute-start.6 = (bf16[1280,384]{1,0:T(8,128)(2,1)}, bf16[1280,384]{1,0:T(8,128)(2,1)}, u32[]{:S(2)}, u32[]{:S(2)}) collective-permute-start(bf16[1280,384]{1,0:T(8,128)(2,1)} %get-tuple-element.36), channel_id=1, source_target_pairs={{0,48},{1,49},{2,50},{3,51},{4,52},{5,53},{6,54},{7,55},{8,56},{9,... | collective-permute-start | bytes 2949128 | tf_op jit(solution)/shard_map/ppermute | solution.py:563
  88.4 4.2 %piece.7 = (bf16[1280,384]{1,0:T(8,128)(2,1)S(1)}, bf16[1280,128]{1,0:T(8,128)(2,1)S(1)}) custom-call(s32[1]{0:T(128)} %bitcast.15.at_ref, bf16[5120,768]{1,0:T(8,128)(2,1)} %turn.1.t_ref, bf16[5120,768]{1,0:T(8,128)(2,1)} %get-tuple-element.28.w_ref, bf16[384,512]{1,0:T(8,128)(2,1)S(1)} %get-tuple-element.31.xs_ref, ...), custom_call_target="tpu_custom_call" | custom-call | tf_op jit(solution)/shard_map/piece/pallas_call | solution.py:459
  95.3 2.1 %collective-permute-start.21 = (bf16[1280,128]{1,0:T(8,128)(2,1)S(1)}, bf16[1280,128]{1,0:T(8,128)(2,1)S(1)}, u32[]{:S(2)}, u32[]{:S(2)}) collective-permute-start(bf16[1280,128]{1,0:T(8,128)(2,1)S(1)} %get-tuple-element.54), channel_id=1, source_target_pairs={{0,3},{1,0},{2,1},{3,2},{4,7},{5,4},{6,5},{7,6},{8,11},{9,8},{10,9... | collective-permute-start | bytes 983048 | tf_op jit(solution)/shard_map/ppermute | solution.py:563
  97.5 3.3 %collective-permute-done.5 = bf16[1280,384]{1,0:T(8,128)(2,1)} collective-permute-done((bf16[1280,384]{1,0:T(8,128)(2,1)}, bf16[1280,384]{1,0:T(8,128)(2,1)}, u32[]{:S(2)}, u32[]{:S(2)}) %collective-permute-start.5) | collective-permute-done | bytes 983072 | tf_op jit(solution)/shard_map/ppermute | solution.py:563
  100.7 2.8 %add_convert_fusion.3 = (bf16[320,384]{1,0:T(8,128)(2,1)}, bf16[320,384]{1,0:T(8,128)(2,1)}, bf16[320,384]{1,0:T(8,128)(2,1)}) fusion(bf16[1280,384]{1,0:T(8,128)(2,1)S(1)} %get-tuple-element.37, s32[]{:T(128)S(6)} %select_n.291, bf16[1280,384]{1,0:T(8,128)(2,1)} %collective-permute-done.6, bf16[1280,384]{1,0:T(8,128)(2,1)} %collective-permute-done.5, ...), kind=kLoop, calls=%fused_computation.6 | loop fusion | flops 2949120 | bytes 3686412 | tf_op jit(solution)/shard_map/convert_element_type | solution.py:577
  103.6 1.7 collective-permute-start.7
  106.4 2.1 %collective-permute-start.9 = (bf16[320,384]{1,0:T(8,128)(2,1)}, bf16[320,384]{1,0:T(8,128)(2,1)S(1)}, u32[]{:S(2)}, u32[]{:S(2)}) collective-permute-start(bf16[320,384]{1,0:T(8,128)(2,1)} %get-tuple-element.47), channel_id=1, source_target_pairs={{0,12},{1,13},{2,14},{3,15},{4,0},{5,1},{6,2},{7,3},{8,4},{9,5},{1... | collective-permute-start | bytes 737288 | tf_op jit(solution)/shard_map/ppermute | solution.py:563
  109.3 2.9 %collective-permute-done.20 = bf16[1280,128]{1,0:T(8,128)(2,1)S(1)} collective-permute-done((bf16[1280,128]{1,0:T(8,128)(2,1)S(1)}, bf16[1280,128]{1,0:T(8,128)(2,1)S(1)}, u32[]{:S(2)}, u32[]{:S(2)}) %collective-permute-start.20) | collective-permute-done | bytes 327712 | tf_op jit(solution)/shard_map/ppermute | solution.py:563
  114.1 3.0 %collective-permute-start.24 = (bf16[320,128]{1,0:T(8,128)(2,1)S(1)}, bf16[320,128]{1,0:T(8,128)(2,1)}, u32[]{:S(2)}, u32[]{:S(2)}) collective-permute-start(bf16[320,128]{1,0:T(8,128)(2,1)S(1)} %get-tuple-element.50), channel_id=1, source_target_pairs={{0,48},{1,49},{2,50},{3,51},{4,52},{5,53},{6,54},{7,55},{8,56},{9,... | collective-permute-start | bytes 245768 | tf_op jit(solution)/shard_map/ppermute | solution.py:563
  118.8 1.7 collective-permute-start.10
  120.7 3.0 %collective-permute-start.12 = (bf16[320,384]{1,0:T(8,128)(2,1)S(1)}, bf16[320,384]{1,0:T(8,128)(2,1)S(1)}, u32[]{:S(2)}, u32[]{:S(2)}) collective-permute-start(bf16[320,384]{1,0:T(8,128)(2,1)S(1)} %add_convert_fusion), channel_id=1, source_target_pairs={{0,3},{1,0},{2,1},{3,2},{4,7},{5,4},{6,5},{7,6},{8,11},{9,8},{10,9... | collective-permute-start | bytes 737288 | tf_op jit(solution)/shard_map/ppermute | solution.py:563
  126.7 2.4 %collective-permute-start.27 = (bf16[320,128]{1,0:T(8,128)(2,1)S(1)}, bf16[320,128]{1,0:T(8,128)(2,1)S(1)}, u32[]{:S(2)}, u32[]{:S(2)}) collective-permute-start(bf16[320,128]{1,0:T(8,128)(2,1)S(1)} %add_convert_fusion.5), channel_id=1, source_target_pairs={{0,12},{1,13},{2,14},{3,15},{4,0},{5,1},{6,2},{7,3},{8,4},{9,5},{1... | collective-permute-start | bytes 245768 | tf_op jit(solution)/shard_map/ppermute | solution.py:563
  131.3 2.2 %collective-permute-start.15 = (bf16[320,384]{1,0:T(8,128)(2,1)S(1)}, bf16[320,384]{1,0:T(8,128)(2,1)S(1)}, u32[]{:S(2)}, u32[]{:S(2)}) collective-permute-start(bf16[320,384]{1,0:T(8,128)(2,1)S(1)} %fusion), channel_id=1, source_target_pairs={{0,12},{1,13},{2,14},{3,15},{4,0},{5,1},{6,2},{7,3},{8,4},{9,5},{1... | collective-permute-start | bytes 737288 | tf_op jit(solution)/shard_map/ppermute | solution.py:563
  133.8 3.1 %collective-permute-start.29 = (bf16[320,128]{1,0:T(8,128)(2,1)S(1)}, bf16[320,128]{1,0:T(8,128)(2,1)S(1)}, u32[]{:S(2)}, u32[]{:S(2)}) collective-permute-start(bf16[320,128]{1,0:T(8,128)(2,1)S(1)} %add_convert_fusion.4), channel_id=1, source_target_pairs={{0,32},{1,33},{2,34},{3,35},{4,36},{5,37},{6,38},{7,39},{8,40},{9,... | collective-permute-start | bytes 245768 | tf_op jit(solution)/shard_map/ppermute | solution.py:563
  136.9 2.8 %collective-permute-done.13 = bf16[320,384]{1,0:T(8,128)(2,1)S(1)} collective-permute-done((bf16[320,384]{1,0:T(8,128)(2,1)S(1)}, bf16[320,384]{1,0:T(8,128)(2,1)S(1)}, u32[]{:S(2)}, u32[]{:S(2)}) %collective-permute-start.13) | collective-permute-done | bytes 245792 | tf_op jit(solution)/shard_map/ppermute | solution.py:563
  141.9 2.1 %collective-permute-start.18 = (bf16[1280,384]{1,0:T(8,128)(2,1)S(1)}, bf16[1280,384]{1,0:T(8,128)(2,1)S(1)}, u32[]{:S(2)}, u32[]{:S(2)}) collective-permute-start(bf16[1280,384]{1,0:T(8,128)(2,1)S(1)} %pad_maximum_fusion.ref.refs_0_), channel_id=1, source_target_pairs={{0,48},{1,49},{2,50},{3,51},{4,52},{5,53},{6,54},{7,55},{8,56},{9,... | collective-permute-start | bytes 2949128 | tf_op jit(solution)/shard_map/ppermute | solution.py:563
  146.8 5.3 %collective-permute-done.33.ref.refs_7_ = bf16[1280,128]{1,0:T(8,128)(2,1)S(1)} collective-permute-done((bf16[1280,128]{1,0:T(8,128)(2,1)S(1)}, bf16[1280,128]{1,0:T(8,128)(2,1)S(1)}, u32[]{:S(2)}, u32[]{:S(2)}) %collective-permute-start.33) | collective-permute-done | bytes 327712 | tf_op jit(solution)/shard_map/ppermute | solution.py:563
  152.1 4.3 %collective-permute-start.32 = (bf16[1280,128]{1,0:T(8,128)(2,1)S(1)}, bf16[1280,128]{1,0:T(8,128)(2,1)S(1)}, u32[]{:S(2)}, u32[]{:S(2)}) collective-permute-start(bf16[1280,128]{1,0:T(8,128)(2,1)S(1)} %pad_maximum_fusion.1.ref.refs_4_), channel_id=1, source_target_pairs={{0,2},{1,3},{2,0},{3,1},{4,6},{5,7},{6,4},{7,5},{8,10},{9,11},{10,... | collective-permute-start | bytes 983048 | tf_op jit(solution)/shard_map/ppermute | solution.py:563
  156.6 5.0 %collective-permute-done.31.ref.refs_5_ = bf16[1280,128]{1,0:T(8,128)(2,1)S(1)} collective-permute-done((bf16[1280,128]{1,0:T(8,128)(2,1)S(1)}, bf16[1280,128]{1,0:T(8,128)(2,1)S(1)}, u32[]{:S(2)}, u32[]{:S(2)}) %collective-permute-start.31) | collective-permute-done | bytes 327712 | tf_op jit(solution)/shard_map/ppermute | solution.py:563
  161.8 4.8 %collective-permute-done.16.ref.refs_1_ = bf16[1280,384]{1,0:T(8,128)(2,1)S(1)} collective-permute-done((bf16[1280,384]{1,0:T(8,128)(2,1)S(1)}, bf16[1280,384]{1,0:T(8,128)(2,1)S(1)}, u32[]{:S(2)}, u32[]{:S(2)}) %collective-permute-start.16) | collective-permute-done | bytes 983072 | tf_op jit(solution)/shard_map/ppermute | solution.py:563
  166.9 3.5 %finish.1 = (bf16[2,5120,128]{2,1,0:T(8,128)(2,1)}, bf16[2,5120,128]{2,1,0:T(8,128)(2,1)}) custom-call(s32[2,4,4]{2,1,0:T(4,128)S(1)} %pad_add_fusion.at, bf16[1280,384]{1,0:T(8,128)(2,1)S(1)} %pad_maximum_fusion.ref.refs_0_, bf16[1280,384]{1,0:T(8,128)(2,1)S(1)} %collective-permute-done.16.ref.refs_1_, ...), custom_call_target="tpu_custom_call" | custom-call | tf_op jit(solution)/shard_map/finish/pallas_call | solution.py:533
  (91 shorter events, 25.2 us)
Async XLA Ops:
  0.6 22.6 %collective-permute-start = (bf16[2,5120,128]{2,1,0:T(8,128)(2,1)}, bf16[2,5120,128]{2,1,0:T(8,128)(2,1)S(1)}, u32[]{:S(2)}, u32[]{:S(2)}) collective-permute-start(bf16[2,5120,128]{2,1,0:T(8,128)(2,1)} %bitcast.30), channel_id=1, source_target_pairs={{0,64},{64,0},{1,65},{65,1},{2,66},{66,2},{3,67},{67,3},{4,68},{68... | collective-permute-start | bytes 7864328 | tf_op jit(solution)/shard_map/ppermute | solution.py:600
  0.7 22.5 %collective-permute-start.1 = (bf16[2,5120,128]{2,1,0:T(8,128)(2,1)}, bf16[2,5120,128]{2,1,0:T(8,128)(2,1)}, u32[]{:S(2)}, u32[]{:S(2)}) collective-permute-start(bf16[2,5120,128]{2,1,0:T(8,128)(2,1)} %bitcast.33), channel_id=1, source_target_pairs={{0,64},{64,0},{1,65},{65,1},{2,66},{66,2},{3,67},{67,3},{4,68},{68... | collective-permute-start | bytes 7864328 | tf_op jit(solution)/shard_map/ppermute | solution.py:601
  1.2 21.9 %collective-permute-start.2 = (f32[2,5120]{1,0:T(2,128)}, f32[2,5120]{1,0:T(2,128)S(1)}, u32[]{:S(2)}, u32[]{:S(2)}) collective-permute-start(f32[2,5120]{1,0:T(2,128)} %bitcast.36), channel_id=1, source_target_pairs={{0,64},{64,0},{1,65},{65,1},{2,66},{66,2},{3,67},{67,3},{4,68},{68... | collective-permute-start | bytes 122888 | tf_op jit(solution)/shard_map/ppermute | solution.py:602
  11.4 27.1 %all-to-all-start = ((bf16[128,8,384]{2,1,0:T(8,128)(2,1)}), bf16[128,8,384]{2,1,0:T(8,128)(2,1)S(1)}, u32[]{:S(2)}, u32[]{:S(2)}) async-start(bf16[128,8,384]{2,1,0:T(8,128)(2,1)} %bitcast.7), calls=%async_computation | async-start | bytes 1572864 | tf_op jit(solution)/shard_map/all_to_all | solution.py:604
  43.7 22.1 %collective-permute-start.3 = (bf16[768,512]{1,0:T(8,128)(2,1)}, bf16[768,512]{1,0:T(8,128)(2,1)S(1)}, u32[]{:S(2)}, u32[]{:S(2)}) collective-permute-start(bf16[768,512]{1,0:T(8,128)(2,1)} %get-tuple-element.30), channel_id=1, source_target_pairs={{0,64},{64,0},{1,65},{65,1},{2,66},{66,2},{3,67},{67,3},{4,68},{68... | collective-permute-start | bytes 2359304 | tf_op jit(solution)/shard_map/ppermute | solution.py:617
  43.8 22.0 %all-to-all-start.1 = ((bf16[128,8,384]{2,1,0:T(8,128)(2,1)}), bf16[128,8,384]{2,1,0:T(8,128)(2,1)S(1)}, u32[]{:S(2)}, u32[]{:S(2)}) async-start(bf16[128,8,384]{2,1,0:T(8,128)(2,1)} %bitcast.11), calls=%async_computation.1 | async-start | bytes 1572864 | tf_op jit(solution)/shard_map/all_to_all | solution.py:618
  73.2 22.1 %collective-permute-start.4 = (bf16[1280,384]{1,0:T(8,128)(2,1)}, bf16[1280,384]{1,0:T(8,128)(2,1)}, u32[]{:S(2)}, u32[]{:S(2)}) collective-permute-start(bf16[1280,384]{1,0:T(8,128)(2,1)} %get-tuple-element.34), channel_id=1, source_target_pairs={{0,32},{1,33},{2,34},{3,35},{4,36},{5,37},{6,38},{7,39},{8,40},{9,... | collective-permute-start | bytes 2949128 | tf_op jit(solution)/shard_map/ppermute | solution.py:563
  85.0 15.7 %collective-permute-start.5 = (bf16[1280,384]{1,0:T(8,128)(2,1)}, bf16[1280,384]{1,0:T(8,128)(2,1)}, u32[]{:S(2)}, u32[]{:S(2)}) collective-permute-start(bf16[1280,384]{1,0:T(8,128)(2,1)} %get-tuple-element.35), channel_id=1, source_target_pairs={{0,16},{1,17},{2,18},{3,19},{4,20},{5,21},{6,22},{7,23},{8,24},{9,... | collective-permute-start | bytes 2949128 | tf_op jit(solution)/shard_map/ppermute | solution.py:563
  85.9 14.8 %collective-permute-start.6 = (bf16[1280,384]{1,0:T(8,128)(2,1)}, bf16[1280,384]{1,0:T(8,128)(2,1)}, u32[]{:S(2)}, u32[]{:S(2)}) collective-permute-start(bf16[1280,384]{1,0:T(8,128)(2,1)} %get-tuple-element.36), channel_id=1, source_target_pairs={{0,48},{1,49},{2,50},{3,51},{4,52},{5,53},{6,54},{7,55},{8,56},{9,... | collective-permute-start | bytes 2949128 | tf_op jit(solution)/shard_map/ppermute | solution.py:563
  92.8 13.6 %collective-permute-start.19 = (bf16[1280,128]{1,0:T(8,128)(2,1)S(1)}, bf16[1280,128]{1,0:T(8,128)(2,1)S(1)}, u32[]{:S(2)}, u32[]{:S(2)}) collective-permute-start(bf16[1280,128]{1,0:T(8,128)(2,1)S(1)} %get-tuple-element.52), channel_id=1, source_target_pairs={{0,2},{1,3},{2,0},{3,1},{4,6},{5,7},{6,4},{7,5},{8,10},{9,11},{10,... | collective-permute-start | bytes 983048 | tf_op jit(solution)/shard_map/ppermute | solution.py:563
  94.2 17.9 %collective-permute-start.20 = (bf16[1280,128]{1,0:T(8,128)(2,1)S(1)}, bf16[1280,128]{1,0:T(8,128)(2,1)S(1)}, u32[]{:S(2)}, u32[]{:S(2)}) collective-permute-start(bf16[1280,128]{1,0:T(8,128)(2,1)S(1)} %get-tuple-element.55), channel_id=1, source_target_pairs={{0,1},{1,2},{2,3},{3,0},{4,5},{5,6},{6,7},{7,4},{8,9},{9,10},{10,1... | collective-permute-start | bytes 983048 | tf_op jit(solution)/shard_map/ppermute | solution.py:563
  95.3 16.8 %collective-permute-start.21 = (bf16[1280,128]{1,0:T(8,128)(2,1)S(1)}, bf16[1280,128]{1,0:T(8,128)(2,1)S(1)}, u32[]{:S(2)}, u32[]{:S(2)}) collective-permute-start(bf16[1280,128]{1,0:T(8,128)(2,1)S(1)} %get-tuple-element.54), channel_id=1, source_target_pairs={{0,3},{1,0},{2,1},{3,2},{4,7},{5,4},{6,5},{7,6},{8,11},{9,8},{10,9... | collective-permute-start | bytes 983048 | tf_op jit(solution)/shard_map/ppermute | solution.py:563
  103.6 10.6 %collective-permute-start.7 = (bf16[320,384]{1,0:T(8,128)(2,1)}, bf16[320,384]{1,0:T(8,128)(2,1)}, u32[]{:S(2)}, u32[]{:S(2)}) collective-permute-start(bf16[320,384]{1,0:T(8,128)(2,1)} %get-tuple-element.46), channel_id=1, source_target_pairs={{0,8},{1,9},{2,10},{3,11},{4,12},{5,13},{6,14},{7,15},{8,0},{9,1},... | collective-permute-start | bytes 737288 | tf_op jit(solution)/shard_map/ppermute | solution.py:563
  105.3 11.9 %collective-permute-start.8 = (bf16[320,384]{1,0:T(8,128)(2,1)}, bf16[320,384]{1,0:T(8,128)(2,1)}, u32[]{:S(2)}, u32[]{:S(2)}) collective-permute-start(bf16[320,384]{1,0:T(8,128)(2,1)} %get-tuple-element.48), channel_id=1, source_target_pairs={{0,4},{1,5},{2,6},{3,7},{4,8},{5,9},{6,10},{7,11},{8,12},{9,13},{1... | collective-permute-start | bytes 737288 | tf_op jit(solution)/shard_map/ppermute | solution.py:563
  106.4 10.8 %collective-permute-start.9 = (bf16[320,384]{1,0:T(8,128)(2,1)}, bf16[320,384]{1,0:T(8,128)(2,1)S(1)}, u32[]{:S(2)}, u32[]{:S(2)}) collective-permute-start(bf16[320,384]{1,0:T(8,128)(2,1)} %get-tuple-element.47), channel_id=1, source_target_pairs={{0,12},{1,13},{2,14},{3,15},{4,0},{5,1},{6,2},{7,3},{8,4},{9,5},{1... | collective-permute-start | bytes 737288 | tf_op jit(solution)/shard_map/ppermute | solution.py:563
  112.9 7.8 %collective-permute-start.22 = (bf16[320,128]{1,0:T(8,128)(2,1)S(1)}, bf16[320,128]{1,0:T(8,128)(2,1)S(1)}, u32[]{:S(2)}, u32[]{:S(2)}) collective-permute-start(bf16[320,128]{1,0:T(8,128)(2,1)S(1)} %get-tuple-element.49), channel_id=1, source_target_pairs={{0,32},{1,33},{2,34},{3,35},{4,36},{5,37},{6,38},{7,39},{8,40},{9,... | collective-permute-start | bytes 245768 | tf_op jit(solution)/shard_map/ppermute | solution.py:563
  113.9 9.8 %collective-permute-start.23 = (bf16[320,128]{1,0:T(8,128)(2,1)}, bf16[320,128]{1,0:T(8,128)(2,1)S(1)}, u32[]{:S(2)}, u32[]{:S(2)}) collective-permute-start(bf16[320,128]{1,0:T(8,128)(2,1)} %get-tuple-element.51), channel_id=1, source_target_pairs={{0,16},{1,17},{2,18},{3,19},{4,20},{5,21},{6,22},{7,23},{8,24},{9,... | collective-permute-start | bytes 245768 | tf_op jit(solution)/shard_map/ppermute | solution.py:563
  114.1 9.6 %collective-permute-start.24 = (bf16[320,128]{1,0:T(8,128)(2,1)S(1)}, bf16[320,128]{1,0:T(8,128)(2,1)}, u32[]{:S(2)}, u32[]{:S(2)}) collective-permute-start(bf16[320,128]{1,0:T(8,128)(2,1)S(1)} %get-tuple-element.50), channel_id=1, source_target_pairs={{0,48},{1,49},{2,50},{3,51},{4,52},{5,53},{6,54},{7,55},{8,56},{9,... | collective-permute-start | bytes 245768 | tf_op jit(solution)/shard_map/ppermute | solution.py:563
  118.8 7.9 %collective-permute-start.10 = (bf16[320,384]{1,0:T(8,128)(2,1)S(1)}, bf16[320,384]{1,0:T(8,128)(2,1)S(1)}, u32[]{:S(2)}, u32[]{:S(2)}) collective-permute-start(bf16[320,384]{1,0:T(8,128)(2,1)S(1)} %add_convert_fusion), channel_id=1, source_target_pairs={{0,2},{1,3},{2,0},{3,1},{4,6},{5,7},{6,4},{7,5},{8,10},{9,11},{10,... | collective-permute-start | bytes 737288 | tf_op jit(solution)/shard_map/ppermute | solution.py:563
  120.5 8.7 %collective-permute-start.11 = (bf16[320,384]{1,0:T(8,128)(2,1)S(1)}, bf16[320,384]{1,0:T(8,128)(2,1)S(1)}, u32[]{:S(2)}, u32[]{:S(2)}) collective-permute-start(bf16[320,384]{1,0:T(8,128)(2,1)S(1)} %add_convert_fusion), channel_id=1, source_target_pairs={{0,1},{1,2},{2,3},{3,0},{4,5},{5,6},{6,7},{7,4},{8,9},{9,10},{10,1... | collective-permute-start | bytes 737288 | tf_op jit(solution)/shard_map/ppermute | solution.py:563
  120.7 8.5 %collective-permute-start.12 = (bf16[320,384]{1,0:T(8,128)(2,1)S(1)}, bf16[320,384]{1,0:T(8,128)(2,1)S(1)}, u32[]{:S(2)}, u32[]{:S(2)}) collective-permute-start(bf16[320,384]{1,0:T(8,128)(2,1)S(1)} %add_convert_fusion), channel_id=1, source_target_pairs={{0,3},{1,0},{2,1},{3,2},{4,7},{5,4},{6,5},{7,6},{8,11},{9,8},{10,9... | collective-permute-start | bytes 737288 | tf_op jit(solution)/shard_map/ppermute | solution.py:563
  125.8 7.7 %collective-permute-start.26 = (bf16[320,128]{1,0:T(8,128)(2,1)S(1)}, bf16[320,128]{1,0:T(8,128)(2,1)S(1)}, u32[]{:S(2)}, u32[]{:S(2)}) collective-permute-start(bf16[320,128]{1,0:T(8,128)(2,1)S(1)} %add_convert_fusion.5), channel_id=1, source_target_pairs={{0,4},{1,5},{2,6},{3,7},{4,8},{5,9},{6,10},{7,11},{8,12},{9,13},{1... | collective-permute-start | bytes 245768 | tf_op jit(solution)/shard_map/ppermute | solution.py:563
  129.6 10.1 %collective-permute-start.13 = (bf16[320,384]{1,0:T(8,128)(2,1)S(1)}, bf16[320,384]{1,0:T(8,128)(2,1)S(1)}, u32[]{:S(2)}, u32[]{:S(2)}) collective-permute-start(bf16[320,384]{1,0:T(8,128)(2,1)S(1)} %fusion), channel_id=1, source_target_pairs={{0,4},{1,5},{2,6},{3,7},{4,8},{5,9},{6,10},{7,11},{8,12},{9,13},{1... | collective-permute-start | bytes 737288 | tf_op jit(solution)/shard_map/ppermute | solution.py:563
  129.7 10.8 %collective-permute-start.14 = (bf16[320,384]{1,0:T(8,128)(2,1)S(1)}, bf16[320,384]{1,0:T(8,128)(2,1)S(1)}, u32[]{:S(2)}, u32[]{:S(2)}) collective-permute-start(bf16[320,384]{1,0:T(8,128)(2,1)S(1)} %fusion), channel_id=1, source_target_pairs={{0,8},{1,9},{2,10},{3,11},{4,12},{5,13},{6,14},{7,15},{8,0},{9,1},... | collective-permute-start | bytes 737288 | tf_op jit(solution)/shard_map/ppermute | solution.py:563
  131.3 9.3 %collective-permute-start.15 = (bf16[320,384]{1,0:T(8,128)(2,1)S(1)}, bf16[320,384]{1,0:T(8,128)(2,1)S(1)}, u32[]{:S(2)}, u32[]{:S(2)}) collective-permute-start(bf16[320,384]{1,0:T(8,128)(2,1)S(1)} %fusion), channel_id=1, source_target_pairs={{0,12},{1,13},{2,14},{3,15},{4,0},{5,1},{6,2},{7,3},{8,4},{9,5},{1... | collective-permute-start | bytes 737288 | tf_op jit(solution)/shard_map/ppermute | solution.py:563
  133.6 10.4 %collective-permute-start.28 = (bf16[320,128]{1,0:T(8,128)(2,1)S(1)}, bf16[320,128]{1,0:T(8,128)(2,1)S(1)}, u32[]{:S(2)}, u32[]{:S(2)}) collective-permute-start(bf16[320,128]{1,0:T(8,128)(2,1)S(1)} %add_convert_fusion.4), channel_id=1, source_target_pairs={{0,16},{1,17},{2,18},{3,19},{4,20},{5,21},{6,22},{7,23},{8,24},{9,... | collective-permute-start | bytes 245768 | tf_op jit(solution)/shard_map/ppermute | solution.py:563
  133.8 10.8 %collective-permute-start.29 = (bf16[320,128]{1,0:T(8,128)(2,1)S(1)}, bf16[320,128]{1,0:T(8,128)(2,1)S(1)}, u32[]{:S(2)}, u32[]{:S(2)}) collective-permute-start(bf16[320,128]{1,0:T(8,128)(2,1)S(1)} %add_convert_fusion.4), channel_id=1, source_target_pairs={{0,32},{1,33},{2,34},{3,35},{4,36},{5,37},{6,38},{7,39},{8,40},{9,... | collective-permute-start | bytes 245768 | tf_op jit(solution)/shard_map/ppermute | solution.py:563
  140.7 25.9 %collective-permute-start.16 = (bf16[1280,384]{1,0:T(8,128)(2,1)S(1)}, bf16[1280,384]{1,0:T(8,128)(2,1)S(1)}, u32[]{:S(2)}, u32[]{:S(2)}) collective-permute-start(bf16[1280,384]{1,0:T(8,128)(2,1)S(1)} %pad_maximum_fusion.ref.refs_0_), channel_id=1, source_target_pairs={{0,16},{1,17},{2,18},{3,19},{4,20},{5,21},{6,22},{7,23},{8,24},{9,... | collective-permute-start | bytes 2949128 | tf_op jit(solution)/shard_map/ppermute | solution.py:563
  141.9 24.8 %collective-permute-start.18 = (bf16[1280,384]{1,0:T(8,128)(2,1)S(1)}, bf16[1280,384]{1,0:T(8,128)(2,1)S(1)}, u32[]{:S(2)}, u32[]{:S(2)}) collective-permute-start(bf16[1280,384]{1,0:T(8,128)(2,1)S(1)} %pad_maximum_fusion.ref.refs_0_), channel_id=1, source_target_pairs={{0,48},{1,49},{2,50},{3,51},{4,52},{5,53},{6,54},{7,55},{8,56},{9,... | collective-permute-start | bytes 2949128 | tf_op jit(solution)/shard_map/ppermute | solution.py:563
  144.0 22.9 %collective-permute-start.17 = (bf16[1280,384]{1,0:T(8,128)(2,1)S(1)}, bf16[1280,384]{1,0:T(8,128)(2,1)S(1)}, u32[]{:S(2)}, u32[]{:S(2)}) collective-permute-start(bf16[1280,384]{1,0:T(8,128)(2,1)S(1)} %pad_maximum_fusion.ref.refs_0_), channel_id=1, source_target_pairs={{0,32},{1,33},{2,34},{3,35},{4,36},{5,37},{6,38},{7,39},{8,40},{9,... | collective-permute-start | bytes 2949128 | tf_op jit(solution)/shard_map/ppermute | solution.py:563
  146.3 15.3 %collective-permute-start.31 = (bf16[1280,128]{1,0:T(8,128)(2,1)S(1)}, bf16[1280,128]{1,0:T(8,128)(2,1)S(1)}, u32[]{:S(2)}, u32[]{:S(2)}) collective-permute-start(bf16[1280,128]{1,0:T(8,128)(2,1)S(1)} %pad_maximum_fusion.1.ref.refs_4_), channel_id=1, source_target_pairs={{0,1},{1,2},{2,3},{3,0},{4,5},{5,6},{6,7},{7,4},{8,9},{9,10},{10,1... | collective-permute-start | bytes 983048 | tf_op jit(solution)/shard_map/ppermute | solution.py:563
  152.1 14.8 %collective-permute-start.32 = (bf16[1280,128]{1,0:T(8,128)(2,1)S(1)}, bf16[1280,128]{1,0:T(8,128)(2,1)S(1)}, u32[]{:S(2)}, u32[]{:S(2)}) collective-permute-start(bf16[1280,128]{1,0:T(8,128)(2,1)S(1)} %pad_maximum_fusion.1.ref.refs_4_), channel_id=1, source_target_pairs={{0,2},{1,3},{2,0},{3,1},{4,6},{5,7},{6,4},{7,5},{8,10},{9,11},{10,... | collective-permute-start | bytes 983048 | tf_op jit(solution)/shard_map/ppermute | solution.py:563
  (7 other events, 69.4 us)

commit v6 on v5

--- a/solution.py
+++ b/solution.py
@@ -334,7 +334,8 @@
         at_end = pick(i1 + 1)
         lane = lax.broadcasted_iota(jnp.int32, (total, 1), 0) // group
         norm_row = i0 - 2 * lane + 6
-        sums = dot(pick(norm_row), rec[0]) + dot(pick(norm_row + 1), rec[0])
+        both = (grid == norm_row) | (grid == norm_row + 1)
+        sums = dot(both.astype(f32), rec[0])
         square_sum = jnp.concatenate(
             [sums[j * group : (j + 1) * group, j * k : (j + 1) * k] for j in range(lanes)], axis=0
         )[:, :1]
@@ -359,10 +360,10 @@
         )
         for s in range(2):
             l0, l1 = 2 * s, 2 * s + 1
-            out[s] = dot(to_start, joined([back[l0], back[l1], less[l0]])).astype(bf16)
+            near = dot(to_start, joined([back[l0], back[l1], less[l0]]))
             weighted = dot(to_start_next, less[l1])
             tail = dot(to_end, joined([active[l0], active[l1]]))
-            out[s] += joined([weighted, tail]).astype(bf16)
+            out[s] = (near + joined([weighted, tail])).astype(bf16)
         first_section = mine[0] == 0
         for i, (one, two) in enumerate(zip(mix_first, mix_second)):
             at = slice(i * k, (i + 1) * k)

time: 171 us -> 171 us (level)
  no operation moved by 1% of the time
where the time goes in v6:
time: 171 us
  starting transfers between devices  63.6 us (37%)
  Pallas kernels  60.9 us (36%)
  waiting for transfers between devices  35.5 us (21%)
  other arithmetic  7.23 us (4%)
  local copies, waits for them, and re-layouts  1.98 us (1%)
    ppermute x30, starting transfers between devices, hop(): return lax.ppermute(values, ('section', 'peer'), pairs)  45.6 us
    ppermute x30, waiting for transfers between devices, hop(): return lax.ppermute(values, ('section', 'peer'), pairs)  24.8 us
    pallas_call x4, Pallas kernels, piece(): pl.pallas_call(kernel, in_specs=[pl.BlockSpec(memory_space=pltpu.SMEM)] +...  19.9 us
    pallas_call x1, Pallas kernels, prepare(): pl.pallas_call(kernel, grid_spec=pltpu.PrefetchScalarGridSpec(num_scalar_...  11.4 us
    all_to_all x1, starting transfers between devices, local(): lax.all_to_all(sent.reshape(rows, 8, 3 * k), ('section', 'peer'), 0, 0, t...  11.2 us
    pallas_call x1, Pallas kernels, front(): pl.pallas_call(kernel, grid=(steps,), in_specs=[pl.BlockSpec((lanes, rows...  10.1 us
    pallas_call x1, Pallas kernels, turn(): pl.pallas_call(kernel, grid=(features // block,), in_specs=[spec, spec],...  8.99 us
    all_to_all x1, waiting for transfers between devices, local(): lax.all_to_all(out.reshape(rows, 8, 3 * k), ('section', 'peer'), 0, 0, ti...  6.83 us
  transfers between devices with their start and end apart: 36, of which 11 were waited for; matrix products, arithmetic and copies ran while one was open for 5% of the time, Pallas kernels for 27%

profile of v6, /device:TPU:0, one launch (start us, length us, event | category | flops | bytes accessed | tf_op | source)
XLA Modules:
  0.0 170.5 jit_solution(13392431309805065115)
XLA Ops:
  1.3 10.1 %front.1 = bf16[1024,384]{1,0:T(8,128)(2,1)} custom-call(bf16[3,128,5120]{2,1,0:T(8,128)(2,1)} %bitcast.26, bf16[3,128,5120]{2,1,0:T(8,128)(2,1)} %bitcast.28, bf16[2,5120,128]{2,1,0:T(8,128)(2,1)} %bitcast.31, bf16[2,5120,128]{2,1,0:T(8,128)(2,1)} %bitcast.34, f32[2,5120]{1,0:T(2,128)} %bitcast.37), custom_call_target="tpu_custom_call" | custom-call | tf_op jit(solution)/shard_map/front/pallas_call | solution.py:196
  11.4 11.2 %all-to-all-start = ((bf16[128,8,384]{2,1,0:T(8,128)(2,1)}), bf16[128,8,384]{2,1,0:T(8,128)(2,1)S(1)}, u32[]{:S(2)}, u32[]{:S(2)}) async-start(bf16[128,8,384]{2,1,0:T(8,128)(2,1)} %bitcast.7), calls=%async_computation | async-start | bytes 1572864 | tf_op jit(solution)/shard_map/all_to_all | solution.py:605
  23.2 11.4 %prepare.1 = (bf16[5120,768]{1,0:T(8,128)(2,1)}, bf16[256,768]{1,0:T(8,128)(2,1)}, bf16[128,256]{1,0:T(8,128)(2,1)}) custom-call(s32[1]{0:T(128)} %bitcast.3.s_ref.mine, bf16[2,5120,128]{2,1,0:T(8,128)(2,1)} %bitcast.32, bf16[2,5120,128]{2,1,0:T(8,128)(2,1)} %bitcast.35, f32[2,5120]{1,0:T(2,128)} %bitcast.38, ...), custom_call_target="tpu_custom_call" | custom-call | tf_op jit(solution)/shard_map/prepare/pallas_call | solution.py:264
  34.6 3.8 %all-to-all-done = bf16[128,8,384]{2,1,0:T(8,128)(2,1)S(1)} async-done(((bf16[128,8,384]{2,1,0:T(8,128)(2,1)}), bf16[128,8,384]{2,1,0:T(8,128)(2,1)S(1)}, u32[]{:S(2)}, u32[]{:S(2)}) %all-to-all-start) | async-done | bytes 786464 | tf_op jit(solution)/shard_map/all_to_all | solution.py:605
  38.5 5.1 %meet.1 = (bf16[2,512,384]{2,1,0:T(8,128)(2,1)}, bf16[768,512]{1,0:T(8,128)(2,1)S(1)}, bf16[768,512]{1,0:T(8,128)(2,1)}) custom-call(s32[1]{0:T(128)} %bitcast.3.s_ref.mine, bf16[2,512,384]{2,1,0:T(8,128)(2,1)S(1)} %bitcast.24, s32[144,2]{1,0:T(8,128)S(1)} %copy.12.columns, s32[2,144]{1,0:T(2,128)S(1)} %multiply_add_fusion.rows, ...), custom_call_target="tpu_custom_call" | custom-call | tf_op jit(solution)/shard_map/meet/pallas_call | solution.py:379
  43.7 6.1 %all-to-all-start.1 = ((bf16[128,8,384]{2,1,0:T(8,128)(2,1)}), bf16[128,8,384]{2,1,0:T(8,128)(2,1)S(1)}, u32[]{:S(2)}, u32[]{:S(2)}) async-start(bf16[128,8,384]{2,1,0:T(8,128)(2,1)} %bitcast.11), calls=%async_computation.1 | async-start | bytes 1572864 | tf_op jit(solution)/shard_map/all_to_all | solution.py:619
  49.9 9.0 %turn.1.t_ref = bf16[5120,768]{1,0:T(8,128)(2,1)} custom-call(bf16[3,128,5120]{2,1,0:T(8,128)(2,1)} %bitcast.27, bf16[3,128,5120]{2,1,0:T(8,128)(2,1)} %bitcast.29), custom_call_target="tpu_custom_call" | custom-call | tf_op jit(solution)/shard_map/turn/pallas_call | solution.py:297
  58.9 6.8 %all-to-all-done.1 = bf16[128,8,384]{2,1,0:T(8,128)(2,1)S(1)} async-done(((bf16[128,8,384]{2,1,0:T(8,128)(2,1)}), bf16[128,8,384]{2,1,0:T(8,128)(2,1)S(1)}, u32[]{:S(2)}, u32[]{:S(2)}) %all-to-all-start.1) | async-done | bytes 786464 | tf_op jit(solution)/shard_map/all_to_all | solution.py:619
  67.9 5.2 %piece.4 = (bf16[1280,384]{1,0:T(8,128)(2,1)}, bf16[1280,128]{1,0:T(8,128)(2,1)S(1)}) custom-call(s32[1]{0:T(128)} %bitcast.at_ref, bf16[5120,768]{1,0:T(8,128)(2,1)} %turn.1.t_ref, bf16[5120,768]{1,0:T(8,128)(2,1)} %get-tuple-element.28.w_ref, bf16[384,512]{1,0:T(8,128)(2,1)S(1)} %get-tuple-element.31.xs_ref, ...), custom_call_target="tpu_custom_call" | custom-call | tf_op jit(solution)/shard_map/piece/pallas_call | solution.py:460
  74.6 5.2 %piece.5 = (bf16[1280,384]{1,0:T(8,128)(2,1)}, bf16[1280,128]{1,0:T(8,128)(2,1)S(1)}) custom-call(s32[1]{0:T(128)} %bitcast.13.at_ref, bf16[5120,768]{1,0:T(8,128)(2,1)} %turn.1.t_ref, bf16[5120,768]{1,0:T(8,128)(2,1)} %get-tuple-element.28.w_ref, bf16[384,512]{1,0:T(8,128)(2,1)S(1)} %get-tuple-element.31.xs_ref, ...), custom_call_target="tpu_custom_call" | custom-call | tf_op jit(solution)/shard_map/piece/pallas_call | solution.py:460
  79.8 5.2 %piece.6 = (bf16[1280,384]{1,0:T(8,128)(2,1)}, bf16[1280,128]{1,0:T(8,128)(2,1)S(1)}) custom-call(s32[1]{0:T(128)} %bitcast.14.at_ref, bf16[5120,768]{1,0:T(8,128)(2,1)} %turn.1.t_ref, bf16[5120,768]{1,0:T(8,128)(2,1)} %get-tuple-element.28.w_ref, bf16[384,512]{1,0:T(8,128)(2,1)S(1)} %get-tuple-element.31.xs_ref, ...), custom_call_target="tpu_custom_call" | custom-call | tf_op jit(solution)/shard_map/piece/pallas_call | solution.py:460
  85.9 2.4 %collective-permute-start.6 = (bf16[1280,384]{1,0:T(8,128)(2,1)}, bf16[1280,384]{1,0:T(8,128)(2,1)}, u32[]{:S(2)}, u32[]{:S(2)}) collective-permute-start(bf16[1280,384]{1,0:T(8,128)(2,1)} %get-tuple-element.36), channel_id=1, source_target_pairs={{0,48},{1,49},{2,50},{3,51},{4,52},{5,53},{6,54},{7,55},{8,56},{9,... | collective-permute-start | bytes 2949128 | tf_op jit(solution)/shard_map/ppermute | solution.py:564
  88.3 4.2 %piece.7 = (bf16[1280,384]{1,0:T(8,128)(2,1)S(1)}, bf16[1280,128]{1,0:T(8,128)(2,1)S(1)}) custom-call(s32[1]{0:T(128)} %bitcast.15.at_ref, bf16[5120,768]{1,0:T(8,128)(2,1)} %turn.1.t_ref, bf16[5120,768]{1,0:T(8,128)(2,1)} %get-tuple-element.28.w_ref, bf16[384,512]{1,0:T(8,128)(2,1)S(1)} %get-tuple-element.31.xs_ref, ...), custom_call_target="tpu_custom_call" | custom-call | tf_op jit(solution)/shard_map/piece/pallas_call | solution.py:460
  95.3 2.1 %collective-permute-start.21 = (bf16[1280,128]{1,0:T(8,128)(2,1)S(1)}, bf16[1280,128]{1,0:T(8,128)(2,1)S(1)}, u32[]{:S(2)}, u32[]{:S(2)}) collective-permute-start(bf16[1280,128]{1,0:T(8,128)(2,1)S(1)} %get-tuple-element.54), channel_id=1, source_target_pairs={{0,3},{1,0},{2,1},{3,2},{4,7},{5,4},{6,5},{7,6},{8,11},{9,8},{10,9... | collective-permute-start | bytes 983048 | tf_op jit(solution)/shard_map/ppermute | solution.py:564
  97.4 3.3 %collective-permute-done.5 = bf16[1280,384]{1,0:T(8,128)(2,1)} collective-permute-done((bf16[1280,384]{1,0:T(8,128)(2,1)}, bf16[1280,384]{1,0:T(8,128)(2,1)}, u32[]{:S(2)}, u32[]{:S(2)}) %collective-permute-start.5) | collective-permute-done | bytes 983072 | tf_op jit(solution)/shard_map/ppermute | solution.py:564
  100.7 2.8 %add_convert_fusion.3 = (bf16[320,384]{1,0:T(8,128)(2,1)}, bf16[320,384]{1,0:T(8,128)(2,1)}, bf16[320,384]{1,0:T(8,128)(2,1)}) fusion(bf16[1280,384]{1,0:T(8,128)(2,1)S(1)} %get-tuple-element.37, s32[]{:T(128)S(6)} %select_n.291, bf16[1280,384]{1,0:T(8,128)(2,1)} %collective-permute-done.6, bf16[1280,384]{1,0:T(8,128)(2,1)} %collective-permute-done.5, ...), kind=kLoop, calls=%fused_computation.6 | loop fusion | flops 2949120 | bytes 3686412 | tf_op jit(solution)/shard_map/convert_element_type | solution.py:578
  103.5 1.7 collective-permute-start.7
  106.4 2.1 %collective-permute-start.9 = (bf16[320,384]{1,0:T(8,128)(2,1)}, bf16[320,384]{1,0:T(8,128)(2,1)S(1)}, u32[]{:S(2)}, u32[]{:S(2)}) collective-permute-start(bf16[320,384]{1,0:T(8,128)(2,1)} %get-tuple-element.47), channel_id=1, source_target_pairs={{0,12},{1,13},{2,14},{3,15},{4,0},{5,1},{6,2},{7,3},{8,4},{9,5},{1... | collective-permute-start | bytes 737288 | tf_op jit(solution)/shard_map/ppermute | solution.py:564
  109.2 2.9 %collective-permute-done.20 = bf16[1280,128]{1,0:T(8,128)(2,1)S(1)} collective-permute-done((bf16[1280,128]{1,0:T(8,128)(2,1)S(1)}, bf16[1280,128]{1,0:T(8,128)(2,1)S(1)}, u32[]{:S(2)}, u32[]{:S(2)}) %collective-permute-start.20) | collective-permute-done | bytes 327712 | tf_op jit(solution)/shard_map/ppermute | solution.py:564
  114.1 3.0 %collective-permute-start.24 = (bf16[320,128]{1,0:T(8,128)(2,1)S(1)}, bf16[320,128]{1,0:T(8,128)(2,1)}, u32[]{:S(2)}, u32[]{:S(2)}) collective-permute-start(bf16[320,128]{1,0:T(8,128)(2,1)S(1)} %get-tuple-element.50), channel_id=1, source_target_pairs={{0,48},{1,49},{2,50},{3,51},{4,52},{5,53},{6,54},{7,55},{8,56},{9,... | collective-permute-start | bytes 245768 | tf_op jit(solution)/shard_map/ppermute | solution.py:564
  118.7 1.7 collective-permute-start.10
  120.6 3.0 %collective-permute-start.12 = (bf16[320,384]{1,0:T(8,128)(2,1)S(1)}, bf16[320,384]{1,0:T(8,128)(2,1)S(1)}, u32[]{:S(2)}, u32[]{:S(2)}) collective-permute-start(bf16[320,384]{1,0:T(8,128)(2,1)S(1)} %add_convert_fusion), channel_id=1, source_target_pairs={{0,3},{1,0},{2,1},{3,2},{4,7},{5,4},{6,5},{7,6},{8,11},{9,8},{10,9... | collective-permute-start | bytes 737288 | tf_op jit(solution)/shard_map/ppermute | solution.py:564
  126.6 2.4 %collective-permute-start.27 = (bf16[320,128]{1,0:T(8,128)(2,1)S(1)}, bf16[320,128]{1,0:T(8,128)(2,1)S(1)}, u32[]{:S(2)}, u32[]{:S(2)}) collective-permute-start(bf16[320,128]{1,0:T(8,128)(2,1)S(1)} %add_convert_fusion.5), channel_id=1, source_target_pairs={{0,12},{1,13},{2,14},{3,15},{4,0},{5,1},{6,2},{7,3},{8,4},{9,5},{1... | collective-permute-start | bytes 245768 | tf_op jit(solution)/shard_map/ppermute | solution.py:564
  131.2 2.2 %collective-permute-start.15 = (bf16[320,384]{1,0:T(8,128)(2,1)S(1)}, bf16[320,384]{1,0:T(8,128)(2,1)S(1)}, u32[]{:S(2)}, u32[]{:S(2)}) collective-permute-start(bf16[320,384]{1,0:T(8,128)(2,1)S(1)} %fusion), channel_id=1, source_target_pairs={{0,12},{1,13},{2,14},{3,15},{4,0},{5,1},{6,2},{7,3},{8,4},{9,5},{1... | collective-permute-start | bytes 737288 | tf_op jit(solution)/shard_map/ppermute | solution.py:564
  133.7 3.1 %collective-permute-start.29 = (bf16[320,128]{1,0:T(8,128)(2,1)S(1)}, bf16[320,128]{1,0:T(8,128)(2,1)S(1)}, u32[]{:S(2)}, u32[]{:S(2)}) collective-permute-start(bf16[320,128]{1,0:T(8,128)(2,1)S(1)} %add_convert_fusion.4), channel_id=1, source_target_pairs={{0,32},{1,33},{2,34},{3,35},{4,36},{5,37},{6,38},{7,39},{8,40},{9,... | collective-permute-start | bytes 245768 | tf_op jit(solution)/shard_map/ppermute | solution.py:564
  136.8 2.8 %collective-permute-done.13 = bf16[320,384]{1,0:T(8,128)(2,1)S(1)} collective-permute-done((bf16[320,384]{1,0:T(8,128)(2,1)S(1)}, bf16[320,384]{1,0:T(8,128)(2,1)S(1)}, u32[]{:S(2)}, u32[]{:S(2)}) %collective-permute-start.13) | collective-permute-done | bytes 245792 | tf_op jit(solution)/shard_map/ppermute | solution.py:564
  141.8 2.1 %collective-permute-start.18 = (bf16[1280,384]{1,0:T(8,128)(2,1)S(1)}, bf16[1280,384]{1,0:T(8,128)(2,1)S(1)}, u32[]{:S(2)}, u32[]{:S(2)}) collective-permute-start(bf16[1280,384]{1,0:T(8,128)(2,1)S(1)} %pad_maximum_fusion.ref.refs_0_), channel_id=1, source_target_pairs={{0,48},{1,49},{2,50},{3,51},{4,52},{5,53},{6,54},{7,55},{8,56},{9,... | collective-permute-start | bytes 2949128 | tf_op jit(solution)/shard_map/ppermute | solution.py:564
  146.7 5.3 %collective-permute-done.33.ref.refs_7_ = bf16[1280,128]{1,0:T(8,128)(2,1)S(1)} collective-permute-done((bf16[1280,128]{1,0:T(8,128)(2,1)S(1)}, bf16[1280,128]{1,0:T(8,128)(2,1)S(1)}, u32[]{:S(2)}, u32[]{:S(2)}) %collective-permute-start.33) | collective-permute-done | bytes 327712 | tf_op jit(solution)/shard_map/ppermute | solution.py:564
  152.0 4.3 %collective-permute-start.32 = (bf16[1280,128]{1,0:T(8,128)(2,1)S(1)}, bf16[1280,128]{1,0:T(8,128)(2,1)S(1)}, u32[]{:S(2)}, u32[]{:S(2)}) collective-permute-start(bf16[1280,128]{1,0:T(8,128)(2,1)S(1)} %pad_maximum_fusion.1.ref.refs_4_), channel_id=1, source_target_pairs={{0,2},{1,3},{2,0},{3,1},{4,6},{5,7},{6,4},{7,5},{8,10},{9,11},{10,... | collective-permute-start | bytes 983048 | tf_op jit(solution)/shard_map/ppermute | solution.py:564
  156.5 5.0 %collective-permute-done.31.ref.refs_5_ = bf16[1280,128]{1,0:T(8,128)(2,1)S(1)} collective-permute-done((bf16[1280,128]{1,0:T(8,128)(2,1)S(1)}, bf16[1280,128]{1,0:T(8,128)(2,1)S(1)}, u32[]{:S(2)}, u32[]{:S(2)}) %collective-permute-start.31) | collective-permute-done | bytes 327712 | tf_op jit(solution)/shard_map/ppermute | solution.py:564
  161.7 4.8 %collective-permute-done.16.ref.refs_1_ = bf16[1280,384]{1,0:T(8,128)(2,1)S(1)} collective-permute-done((bf16[1280,384]{1,0:T(8,128)(2,1)S(1)}, bf16[1280,384]{1,0:T(8,128)(2,1)S(1)}, u32[]{:S(2)}, u32[]{:S(2)}) %collective-permute-start.16) | collective-permute-done | bytes 983072 | tf_op jit(solution)/shard_map/ppermute | solution.py:564
  166.8 3.5 %finish.1 = (bf16[2,5120,128]{2,1,0:T(8,128)(2,1)}, bf16[2,5120,128]{2,1,0:T(8,128)(2,1)}) custom-call(s32[2,4,4]{2,1,0:T(4,128)S(1)} %pad_add_fusion.at, bf16[1280,384]{1,0:T(8,128)(2,1)S(1)} %pad_maximum_fusion.ref.refs_0_, bf16[1280,384]{1,0:T(8,128)(2,1)S(1)} %collective-permute-done.16.ref.refs_1_, ...), custom_call_target="tpu_custom_call" | custom-call | tf_op jit(solution)/shard_map/finish/pallas_call | solution.py:534
  (91 shorter events, 25.2 us)
Async XLA Ops:
  0.6 22.6 %collective-permute-start = (bf16[2,5120,128]{2,1,0:T(8,128)(2,1)}, bf16[2,5120,128]{2,1,0:T(8,128)(2,1)S(1)}, u32[]{:S(2)}, u32[]{:S(2)}) collective-permute-start(bf16[2,5120,128]{2,1,0:T(8,128)(2,1)} %bitcast.30), channel_id=1, source_target_pairs={{0,64},{64,0},{1,65},{65,1},{2,66},{66,2},{3,67},{67,3},{4,68},{68... | collective-permute-start | bytes 7864328 | tf_op jit(solution)/shard_map/ppermute | solution.py:601
  0.7 22.5 %collective-permute-start.1 = (bf16[2,5120,128]{2,1,0:T(8,128)(2,1)}, bf16[2,5120,128]{2,1,0:T(8,128)(2,1)}, u32[]{:S(2)}, u32[]{:S(2)}) collective-permute-start(bf16[2,5120,128]{2,1,0:T(8,128)(2,1)} %bitcast.33), channel_id=1, source_target_pairs={{0,64},{64,0},{1,65},{65,1},{2,66},{66,2},{3,67},{67,3},{4,68},{68... | collective-permute-start | bytes 7864328 | tf_op jit(solution)/shard_map/ppermute | solution.py:602
  1.2 21.9 %collective-permute-start.2 = (f32[2,5120]{1,0:T(2,128)}, f32[2,5120]{1,0:T(2,128)S(1)}, u32[]{:S(2)}, u32[]{:S(2)}) collective-permute-start(f32[2,5120]{1,0:T(2,128)} %bitcast.36), channel_id=1, source_target_pairs={{0,64},{64,0},{1,65},{65,1},{2,66},{66,2},{3,67},{67,3},{4,68},{68... | collective-permute-start | bytes 122888 | tf_op jit(solution)/shard_map/ppermute | solution.py:603
  11.4 27.1 %all-to-all-start = ((bf16[128,8,384]{2,1,0:T(8,128)(2,1)}), bf16[128,8,384]{2,1,0:T(8,128)(2,1)S(1)}, u32[]{:S(2)}, u32[]{:S(2)}) async-start(bf16[128,8,384]{2,1,0:T(8,128)(2,1)} %bitcast.7), calls=%async_computation | async-start | bytes 1572864 | tf_op jit(solution)/shard_map/all_to_all | solution.py:605
  43.6 22.1 %collective-permute-start.3 = (bf16[768,512]{1,0:T(8,128)(2,1)}, bf16[768,512]{1,0:T(8,128)(2,1)S(1)}, u32[]{:S(2)}, u32[]{:S(2)}) collective-permute-start(bf16[768,512]{1,0:T(8,128)(2,1)} %get-tuple-element.30), channel_id=1, source_target_pairs={{0,64},{64,0},{1,65},{65,1},{2,66},{66,2},{3,67},{67,3},{4,68},{68... | collective-permute-start | bytes 2359304 | tf_op jit(solution)/shard_map/ppermute | solution.py:618
  43.7 22.0 %all-to-all-start.1 = ((bf16[128,8,384]{2,1,0:T(8,128)(2,1)}), bf16[128,8,384]{2,1,0:T(8,128)(2,1)S(1)}, u32[]{:S(2)}, u32[]{:S(2)}) async-start(bf16[128,8,384]{2,1,0:T(8,128)(2,1)} %bitcast.11), calls=%async_computation.1 | async-start | bytes 1572864 | tf_op jit(solution)/shard_map/all_to_all | solution.py:619
  73.1 22.1 %collective-permute-start.4 = (bf16[1280,384]{1,0:T(8,128)(2,1)}, bf16[1280,384]{1,0:T(8,128)(2,1)}, u32[]{:S(2)}, u32[]{:S(2)}) collective-permute-start(bf16[1280,384]{1,0:T(8,128)(2,1)} %get-tuple-element.34), channel_id=1, source_target_pairs={{0,32},{1,33},{2,34},{3,35},{4,36},{5,37},{6,38},{7,39},{8,40},{9,... | collective-permute-start | bytes 2949128 | tf_op jit(solution)/shard_map/ppermute | solution.py:564
  85.0 15.7 %collective-permute-start.5 = (bf16[1280,384]{1,0:T(8,128)(2,1)}, bf16[1280,384]{1,0:T(8,128)(2,1)}, u32[]{:S(2)}, u32[]{:S(2)}) collective-permute-start(bf16[1280,384]{1,0:T(8,128)(2,1)} %get-tuple-element.35), channel_id=1, source_target_pairs={{0,16},{1,17},{2,18},{3,19},{4,20},{5,21},{6,22},{7,23},{8,24},{9,... | collective-permute-start | bytes 2949128 | tf_op jit(solution)/shard_map/ppermute | solution.py:564
  85.9 14.8 %collective-permute-start.6 = (bf16[1280,384]{1,0:T(8,128)(2,1)}, bf16[1280,384]{1,0:T(8,128)(2,1)}, u32[]{:S(2)}, u32[]{:S(2)}) collective-permute-start(bf16[1280,384]{1,0:T(8,128)(2,1)} %get-tuple-element.36), channel_id=1, source_target_pairs={{0,48},{1,49},{2,50},{3,51},{4,52},{5,53},{6,54},{7,55},{8,56},{9,... | collective-permute-start | bytes 2949128 | tf_op jit(solution)/shard_map/ppermute | solution.py:564
  92.7 13.6 %collective-permute-start.19 = (bf16[1280,128]{1,0:T(8,128)(2,1)S(1)}, bf16[1280,128]{1,0:T(8,128)(2,1)S(1)}, u32[]{:S(2)}, u32[]{:S(2)}) collective-permute-start(bf16[1280,128]{1,0:T(8,128)(2,1)S(1)} %get-tuple-element.52), channel_id=1, source_target_pairs={{0,2},{1,3},{2,0},{3,1},{4,6},{5,7},{6,4},{7,5},{8,10},{9,11},{10,... | collective-permute-start | bytes 983048 | tf_op jit(solution)/shard_map/ppermute | solution.py:564
  94.2 17.9 %collective-permute-start.20 = (bf16[1280,128]{1,0:T(8,128)(2,1)S(1)}, bf16[1280,128]{1,0:T(8,128)(2,1)S(1)}, u32[]{:S(2)}, u32[]{:S(2)}) collective-permute-start(bf16[1280,128]{1,0:T(8,128)(2,1)S(1)} %get-tuple-element.55), channel_id=1, source_target_pairs={{0,1},{1,2},{2,3},{3,0},{4,5},{5,6},{6,7},{7,4},{8,9},{9,10},{10,1... | collective-permute-start | bytes 983048 | tf_op jit(solution)/shard_map/ppermute | solution.py:564
  95.3 16.8 %collective-permute-start.21 = (bf16[1280,128]{1,0:T(8,128)(2,1)S(1)}, bf16[1280,128]{1,0:T(8,128)(2,1)S(1)}, u32[]{:S(2)}, u32[]{:S(2)}) collective-permute-start(bf16[1280,128]{1,0:T(8,128)(2,1)S(1)} %get-tuple-element.54), channel_id=1, source_target_pairs={{0,3},{1,0},{2,1},{3,2},{4,7},{5,4},{6,5},{7,6},{8,11},{9,8},{10,9... | collective-permute-start | bytes 983048 | tf_op jit(solution)/shard_map/ppermute | solution.py:564
  103.5 10.6 %collective-permute-start.7 = (bf16[320,384]{1,0:T(8,128)(2,1)}, bf16[320,384]{1,0:T(8,128)(2,1)}, u32[]{:S(2)}, u32[]{:S(2)}) collective-permute-start(bf16[320,384]{1,0:T(8,128)(2,1)} %get-tuple-element.46), channel_id=1, source_target_pairs={{0,8},{1,9},{2,10},{3,11},{4,12},{5,13},{6,14},{7,15},{8,0},{9,1},... | collective-permute-start | bytes 737288 | tf_op jit(solution)/shard_map/ppermute | solution.py:564
  105.2 11.9 %collective-permute-start.8 = (bf16[320,384]{1,0:T(8,128)(2,1)}, bf16[320,384]{1,0:T(8,128)(2,1)}, u32[]{:S(2)}, u32[]{:S(2)}) collective-permute-start(bf16[320,384]{1,0:T(8,128)(2,1)} %get-tuple-element.48), channel_id=1, source_target_pairs={{0,4},{1,5},{2,6},{3,7},{4,8},{5,9},{6,10},{7,11},{8,12},{9,13},{1... | collective-permute-start | bytes 737288 | tf_op jit(solution)/shard_map/ppermute | solution.py:564
  106.4 10.8 %collective-permute-start.9 = (bf16[320,384]{1,0:T(8,128)(2,1)}, bf16[320,384]{1,0:T(8,128)(2,1)S(1)}, u32[]{:S(2)}, u32[]{:S(2)}) collective-permute-start(bf16[320,384]{1,0:T(8,128)(2,1)} %get-tuple-element.47), channel_id=1, source_target_pairs={{0,12},{1,13},{2,14},{3,15},{4,0},{5,1},{6,2},{7,3},{8,4},{9,5},{1... | collective-permute-start | bytes 737288 | tf_op jit(solution)/shard_map/ppermute | solution.py:564
  112.8 7.8 %collective-permute-start.22 = (bf16[320,128]{1,0:T(8,128)(2,1)S(1)}, bf16[320,128]{1,0:T(8,128)(2,1)S(1)}, u32[]{:S(2)}, u32[]{:S(2)}) collective-permute-start(bf16[320,128]{1,0:T(8,128)(2,1)S(1)} %get-tuple-element.49), channel_id=1, source_target_pairs={{0,32},{1,33},{2,34},{3,35},{4,36},{5,37},{6,38},{7,39},{8,40},{9,... | collective-permute-start | bytes 245768 | tf_op jit(solution)/shard_map/ppermute | solution.py:564
  113.9 9.8 %collective-permute-start.23 = (bf16[320,128]{1,0:T(8,128)(2,1)}, bf16[320,128]{1,0:T(8,128)(2,1)S(1)}, u32[]{:S(2)}, u32[]{:S(2)}) collective-permute-start(bf16[320,128]{1,0:T(8,128)(2,1)} %get-tuple-element.51), channel_id=1, source_target_pairs={{0,16},{1,17},{2,18},{3,19},{4,20},{5,21},{6,22},{7,23},{8,24},{9,... | collective-permute-start | bytes 245768 | tf_op jit(solution)/shard_map/ppermute | solution.py:564
  114.1 9.6 %collective-permute-start.24 = (bf16[320,128]{1,0:T(8,128)(2,1)S(1)}, bf16[320,128]{1,0:T(8,128)(2,1)}, u32[]{:S(2)}, u32[]{:S(2)}) collective-permute-start(bf16[320,128]{1,0:T(8,128)(2,1)S(1)} %get-tuple-element.50), channel_id=1, source_target_pairs={{0,48},{1,49},{2,50},{3,51},{4,52},{5,53},{6,54},{7,55},{8,56},{9,... | collective-permute-start | bytes 245768 | tf_op jit(solution)/shard_map/ppermute | solution.py:564
  118.7 7.9 %collective-permute-start.10 = (bf16[320,384]{1,0:T(8,128)(2,1)S(1)}, bf16[320,384]{1,0:T(8,128)(2,1)S(1)}, u32[]{:S(2)}, u32[]{:S(2)}) collective-permute-start(bf16[320,384]{1,0:T(8,128)(2,1)S(1)} %add_convert_fusion), channel_id=1, source_target_pairs={{0,2},{1,3},{2,0},{3,1},{4,6},{5,7},{6,4},{7,5},{8,10},{9,11},{10,... | collective-permute-start | bytes 737288 | tf_op jit(solution)/shard_map/ppermute | solution.py:564
  120.4 8.7 %collective-permute-start.11 = (bf16[320,384]{1,0:T(8,128)(2,1)S(1)}, bf16[320,384]{1,0:T(8,128)(2,1)S(1)}, u32[]{:S(2)}, u32[]{:S(2)}) collective-permute-start(bf16[320,384]{1,0:T(8,128)(2,1)S(1)} %add_convert_fusion), channel_id=1, source_target_pairs={{0,1},{1,2},{2,3},{3,0},{4,5},{5,6},{6,7},{7,4},{8,9},{9,10},{10,1... | collective-permute-start | bytes 737288 | tf_op jit(solution)/shard_map/ppermute | solution.py:564
  120.6 8.5 %collective-permute-start.12 = (bf16[320,384]{1,0:T(8,128)(2,1)S(1)}, bf16[320,384]{1,0:T(8,128)(2,1)S(1)}, u32[]{:S(2)}, u32[]{:S(2)}) collective-permute-start(bf16[320,384]{1,0:T(8,128)(2,1)S(1)} %add_convert_fusion), channel_id=1, source_target_pairs={{0,3},{1,0},{2,1},{3,2},{4,7},{5,4},{6,5},{7,6},{8,11},{9,8},{10,9... | collective-permute-start | bytes 737288 | tf_op jit(solution)/shard_map/ppermute | solution.py:564
  125.8 7.7 %collective-permute-start.26 = (bf16[320,128]{1,0:T(8,128)(2,1)S(1)}, bf16[320,128]{1,0:T(8,128)(2,1)S(1)}, u32[]{:S(2)}, u32[]{:S(2)}) collective-permute-start(bf16[320,128]{1,0:T(8,128)(2,1)S(1)} %add_convert_fusion.5), channel_id=1, source_target_pairs={{0,4},{1,5},{2,6},{3,7},{4,8},{5,9},{6,10},{7,11},{8,12},{9,13},{1... | collective-permute-start | bytes 245768 | tf_op jit(solution)/shard_map/ppermute | solution.py:564
  129.5 10.1 %collective-permute-start.13 = (bf16[320,384]{1,0:T(8,128)(2,1)S(1)}, bf16[320,384]{1,0:T(8,128)(2,1)S(1)}, u32[]{:S(2)}, u32[]{:S(2)}) collective-permute-start(bf16[320,384]{1,0:T(8,128)(2,1)S(1)} %fusion), channel_id=1, source_target_pairs={{0,4},{1,5},{2,6},{3,7},{4,8},{5,9},{6,10},{7,11},{8,12},{9,13},{1... | collective-permute-start | bytes 737288 | tf_op jit(solution)/shard_map/ppermute | solution.py:564
  129.6 10.8 %collective-permute-start.14 = (bf16[320,384]{1,0:T(8,128)(2,1)S(1)}, bf16[320,384]{1,0:T(8,128)(2,1)S(1)}, u32[]{:S(2)}, u32[]{:S(2)}) collective-permute-start(bf16[320,384]{1,0:T(8,128)(2,1)S(1)} %fusion), channel_id=1, source_target_pairs={{0,8},{1,9},{2,10},{3,11},{4,12},{5,13},{6,14},{7,15},{8,0},{9,1},... | collective-permute-start | bytes 737288 | tf_op jit(solution)/shard_map/ppermute | solution.py:564
  131.2 9.3 %collective-permute-start.15 = (bf16[320,384]{1,0:T(8,128)(2,1)S(1)}, bf16[320,384]{1,0:T(8,128)(2,1)S(1)}, u32[]{:S(2)}, u32[]{:S(2)}) collective-permute-start(bf16[320,384]{1,0:T(8,128)(2,1)S(1)} %fusion), channel_id=1, source_target_pairs={{0,12},{1,13},{2,14},{3,15},{4,0},{5,1},{6,2},{7,3},{8,4},{9,5},{1... | collective-permute-start | bytes 737288 | tf_op jit(solution)/shard_map/ppermute | solution.py:564
  133.5 10.4 %collective-permute-start.28 = (bf16[320,128]{1,0:T(8,128)(2,1)S(1)}, bf16[320,128]{1,0:T(8,128)(2,1)S(1)}, u32[]{:S(2)}, u32[]{:S(2)}) collective-permute-start(bf16[320,128]{1,0:T(8,128)(2,1)S(1)} %add_convert_fusion.4), channel_id=1, source_target_pairs={{0,16},{1,17},{2,18},{3,19},{4,20},{5,21},{6,22},{7,23},{8,24},{9,... | collective-permute-start | bytes 245768 | tf_op jit(solution)/shard_map/ppermute | solution.py:564
  133.7 10.8 %collective-permute-start.29 = (bf16[320,128]{1,0:T(8,128)(2,1)S(1)}, bf16[320,128]{1,0:T(8,128)(2,1)S(1)}, u32[]{:S(2)}, u32[]{:S(2)}) collective-permute-start(bf16[320,128]{1,0:T(8,128)(2,1)S(1)} %add_convert_fusion.4), channel_id=1, source_target_pairs={{0,32},{1,33},{2,34},{3,35},{4,36},{5,37},{6,38},{7,39},{8,40},{9,... | collective-permute-start | bytes 245768 | tf_op jit(solution)/shard_map/ppermute | solution.py:564
  140.6 25.9 %collective-permute-start.16 = (bf16[1280,384]{1,0:T(8,128)(2,1)S(1)}, bf16[1280,384]{1,0:T(8,128)(2,1)S(1)}, u32[]{:S(2)}, u32[]{:S(2)}) collective-permute-start(bf16[1280,384]{1,0:T(8,128)(2,1)S(1)} %pad_maximum_fusion.ref.refs_0_), channel_id=1, source_target_pairs={{0,16},{1,17},{2,18},{3,19},{4,20},{5,21},{6,22},{7,23},{8,24},{9,... | collective-permute-start | bytes 2949128 | tf_op jit(solution)/shard_map/ppermute | solution.py:564
  141.8 24.8 %collective-permute-start.18 = (bf16[1280,384]{1,0:T(8,128)(2,1)S(1)}, bf16[1280,384]{1,0:T(8,128)(2,1)S(1)}, u32[]{:S(2)}, u32[]{:S(2)}) collective-permute-start(bf16[1280,384]{1,0:T(8,128)(2,1)S(1)} %pad_maximum_fusion.ref.refs_0_), channel_id=1, source_target_pairs={{0,48},{1,49},{2,50},{3,51},{4,52},{5,53},{6,54},{7,55},{8,56},{9,... | collective-permute-start | bytes 2949128 | tf_op jit(solution)/shard_map/ppermute | solution.py:564
  144.0 22.9 %collective-permute-start.17 = (bf16[1280,384]{1,0:T(8,128)(2,1)S(1)}, bf16[1280,384]{1,0:T(8,128)(2,1)S(1)}, u32[]{:S(2)}, u32[]{:S(2)}) collective-permute-start(bf16[1280,384]{1,0:T(8,128)(2,1)S(1)} %pad_maximum_fusion.ref.refs_0_), channel_id=1, source_target_pairs={{0,32},{1,33},{2,34},{3,35},{4,36},{5,37},{6,38},{7,39},{8,40},{9,... | collective-permute-start | bytes 2949128 | tf_op jit(solution)/shard_map/ppermute | solution.py:564
  146.2 15.3 %collective-permute-start.31 = (bf16[1280,128]{1,0:T(8,128)(2,1)S(1)}, bf16[1280,128]{1,0:T(8,128)(2,1)S(1)}, u32[]{:S(2)}, u32[]{:S(2)}) collective-permute-start(bf16[1280,128]{1,0:T(8,128)(2,1)S(1)} %pad_maximum_fusion.1.ref.refs_4_), channel_id=1, source_target_pairs={{0,1},{1,2},{2,3},{3,0},{4,5},{5,6},{6,7},{7,4},{8,9},{9,10},{10,1... | collective-permute-start | bytes 983048 | tf_op jit(solution)/shard_map/ppermute | solution.py:564
  152.0 14.8 %collective-permute-start.32 = (bf16[1280,128]{1,0:T(8,128)(2,1)S(1)}, bf16[1280,128]{1,0:T(8,128)(2,1)S(1)}, u32[]{:S(2)}, u32[]{:S(2)}) collective-permute-start(bf16[1280,128]{1,0:T(8,128)(2,1)S(1)} %pad_maximum_fusion.1.ref.refs_4_), channel_id=1, source_target_pairs={{0,2},{1,3},{2,0},{3,1},{4,6},{5,7},{6,4},{7,5},{8,10},{9,11},{10,... | collective-permute-start | bytes 983048 | tf_op jit(solution)/shard_map/ppermute | solution.py:564
  (7 other events, 69.4 us)
